TPU v7x, 32 devices: a whole 2x2x4 slice. The times are simulated.
32 devices in a mesh: dp: 8 (over y, x, core), tensor: 4 (over z).
Axes of the slice: x: 2, y: 2, z: 4, core: 2. Of those that a mesh axis runs over, the one named last changes fastest.
Arguments:
- tokens: bfloat16 [8192, 2048], P(('dp', 'tensor')), may hold values from -6 to 6
- qkv_weight: bfloat16 [3, 2048, 2048], P(None, 'dp', 'tensor'), may hold values from -0.125 to 0.125
- qkv_bias: bfloat16 [3, 2048], P(None, ('tensor', 'dp')), may hold values from -4 to 4
- out_weight: bfloat16 [2048, 2048], P('tensor', 'dp'), may hold values from -1 to 1
- norm1_gain: bfloat16 [2048], P('dp'), may hold values from 0.5 to 1.5
- norm1_shift: bfloat16 [2048], P('dp'), may hold values from -4 to 4
- gate_weight: bfloat16 [2048, 5632], P('dp', 'tensor'), may hold values from -0.125 to 0.125
- up_weight: bfloat16 [2048, 5632], P('dp', 'tensor'), may hold values from -0.125 to 0.125
- down_weight: bfloat16 [5632, 2048], P('tensor', 'dp'), may hold values from -0.078125 to 0.078125
- norm2_gain: bfloat16 [2048], P('dp'), may hold values from 0.5 to 1.5
- norm2_shift: bfloat16 [2048], P('dp'), may hold values from -4 to 4
- cotangent: bfloat16 [8192, 2048], P(('dp', 'tensor')), may hold values from -6 to 6
Outputs:
- layer_output: bfloat16 [8192, 2048], P(('dp', 'tensor'))
- token_gradient: bfloat16 [8192, 2048], P(('dp', 'tensor'))
- qkvw_grad: float32 [3, 2048, 2048], P(None, 'dp', 'tensor')
- qkvb_grad: float32 [3, 2048], P(None, ('tensor', 'dp'))
- outw_grad: float32 [2048, 2048], P('tensor', 'dp')
- gain1_grad: float32 [2048], P('dp')
- shift1_grad: float32 [2048], P('dp')
- gatew_grad: float32 [2048, 5632], P('dp', 'tensor')
- upw_grad: float32 [2048, 5632], P('dp', 'tensor')
- downw_grad: float32 [5632, 2048], P('tensor', 'dp')
- gain2_grad: float32 [2048], P('dp')
- shift2_grad: float32 [2048], P('dp')
All inputs are finite; a program needn't handle non-finite values.
Results may differ from a plain program's by a relative error of at most 0.035.
Values may be sent and summed in bfloat16 or wider, within the bound.
A program may use at most 192 MiB of HBM per device.

v0:
```python
import jax
import jax.numpy as jnp
from jax import lax
from jax.sharding import PartitionSpec as P

HEAD_DIM = 64
ROT = 16


def apply_layer_norm(value, norm_scale, norm_bias):
    centered_input = value - jnp.mean(value, -1, keepdims=True)
    spread = jnp.mean(centered_input * centered_input, -1, keepdims=True)
    inverse_deviation = lax.rsqrt(spread + 1e-05)
    standardized_input = centered_input * inverse_deviation
    return (
        standardized_input * norm_scale.astype(jnp.float32) + norm_bias.astype(jnp.float32),
        standardized_input,
        inverse_deviation,
    )


def layer_norm_backward(output_gradient, standardized_input, inverse_deviation, norm_scale):
    scaled_gradient = output_gradient * norm_scale.astype(jnp.float32)
    return inverse_deviation * (
        scaled_gradient
        - jnp.mean(scaled_gradient, -1, keepdims=True)
        - standardized_input * jnp.mean(scaled_gradient * standardized_input, -1, keepdims=True)
    )


def tables(length):
    positions = jnp.arange(length, dtype=jnp.float32)
    freqs = 10000.0 ** (-jnp.arange(0, ROT, 2, dtype=jnp.float32) / ROT)
    angles = positions[:, None] * freqs[None, :]
    angles = jnp.concatenate([angles, angles], -1)
    return (jnp.cos(angles), jnp.sin(angles))


def rotate(heads, cosine, sine):
    half = ROT // 2
    part = heads[..., :ROT]
    turned = jnp.concatenate([-part[..., half:], part[..., :half]], -1)
    moved = part * cosine[:, None, :] + turned * sine[:, None, :]
    return jnp.concatenate([moved, heads[..., ROT:]], -1)


def unrotate(output_gradient, cosine, sine):
    half = ROT // 2
    part = output_gradient[..., :ROT]
    scaled_gradient = part * sine[:, None, :]
    back = jnp.concatenate([scaled_gradient[..., half:], -scaled_gradient[..., :half]], -1)
    moved = part * cosine[:, None, :] + back
    return jnp.concatenate([moved, output_gradient[..., ROT:]], -1)


def attn_params(qkv_weight, qkv_bias, out_weight, norm1_gain, norm1_shift):
    return (
        lax.all_gather(qkv_weight, "dp", axis=1, tiled=True),
        lax.all_gather(qkv_bias, "dp", axis=1, tiled=True),
        lax.all_gather(out_weight, "dp", axis=1, tiled=True),
        lax.all_gather(norm1_gain, "dp", axis=0, tiled=True),
        lax.all_gather(norm1_shift, "dp", axis=0, tiled=True),
    )


def mlp_params(gate_weight, up_weight, down_weight, norm2_gain, norm2_shift):
    return (
        lax.all_gather(gate_weight, "dp", axis=0, tiled=True),
        lax.all_gather(up_weight, "dp", axis=0, tiled=True),
        lax.all_gather(down_weight, "dp", axis=1, tiled=True),
        lax.all_gather(norm2_gain, "dp", axis=0, tiled=True),
        lax.all_gather(norm2_shift, "dp", axis=0, tiled=True),
    )


def gather_rows(rows):
    return lax.all_gather(rows, "tensor", axis=0, tiled=True)


def sum_rows(partial_value):
    return lax.psum_scatter(
        partial_value.astype(jnp.bfloat16), "tensor", scatter_dimension=0, tiled=True
    ).astype(jnp.float32)


def gather_grads(rows):
    return lax.all_gather(rows, "tensor", axis=0, tiled=True)


def sum_grads(partial_value):
    return lax.psum_scatter(
        partial_value.astype(jnp.bfloat16), "tensor", scatter_dimension=0, tiled=True
    ).astype(jnp.float32)


def local(
    tokens,
    qkv_weight,
    qkv_bias,
    out_weight,
    norm1_gain,
    norm1_shift,
    gate_weight,
    up_weight,
    down_weight,
    norm2_gain,
    norm2_shift,
    cotangent,
):
    scale = HEAD_DIM ** (-0.5)
    input_rows = tokens.astype(jnp.float32)
    wqkv, bqkv, wout, first_norm_scale, first_norm_bias = attn_params(
        qkv_weight, qkv_bias, out_weight, norm1_gain, norm1_shift
    )
    first_normed_rows, first_standardized, first_inverse_deviation = apply_layer_norm(
        input_rows, first_norm_scale, first_norm_bias
    )
    rows1 = gather_rows(first_normed_rows.astype(jnp.bfloat16))
    length = rows1.shape[0]
    width = wqkv.shape[2]
    local_heads = width // HEAD_DIM
    pre = (
        jnp.einsum("sd,jdc->jsc", rows1, wqkv, preferred_element_type=jnp.float32)
        + bqkv.astype(jnp.float32)[:, None, :]
    )
    cosine, sine = tables(length)
    query = rotate(pre[0].reshape(length, local_heads, HEAD_DIM), cosine, sine).astype(jnp.bfloat16)
    keys = rotate(pre[1].reshape(length, local_heads, HEAD_DIM), cosine, sine).astype(jnp.bfloat16)
    values = pre[2].reshape(length, local_heads, HEAD_DIM).astype(jnp.bfloat16)
    block = min(length, 512)
    count = length // block
    cols = jnp.arange(length, dtype=jnp.int32)

    def block_probs(qblock, start):
        scores = (
            jnp.einsum("qhd,khd->hqk", qblock, keys, preferred_element_type=jnp.float32) * scale
        )
        rows = start + jnp.arange(block, dtype=jnp.int32)
        keep = rows[:, None] >= cols[None, :]
        return jnp.where(keep[None], scores, -1e30)

    def forward_block(index):
        qblock = lax.dynamic_slice_in_dim(query, index * block, block, 0)
        scores = block_probs(qblock, index * block)
        most = jnp.max(scores, -1, keepdims=True)
        expo = jnp.exp(scores - most)
        total = jnp.sum(expo, -1, keepdims=True)
        probs = (expo / total).astype(jnp.bfloat16)
        out_block = jnp.einsum("hqk,khd->qhd", probs, values, preferred_element_type=jnp.float32)
        return (out_block.astype(jnp.bfloat16), most[..., 0] + jnp.log(total[..., 0]))

    indices = jnp.arange(count, dtype=jnp.int32)
    out_blocks, lse = lax.map(forward_block, indices)
    attended = out_blocks.reshape(length, width)
    branch = jnp.dot(attended, wout, preferred_element_type=jnp.float32)
    hidden_state = input_rows + sum_rows(branch)
    wgate, wup, wdown, second_norm_scale, second_norm_bias = mlp_params(
        gate_weight, up_weight, down_weight, norm2_gain, norm2_shift
    )
    second_normed_rows, second_standardized, second_inverse_deviation = apply_layer_norm(
        hidden_state, second_norm_scale, second_norm_bias
    )
    rows2 = gather_rows(second_normed_rows.astype(jnp.bfloat16))
    gate = jnp.dot(rows2, wgate, preferred_element_type=jnp.float32)
    up = jnp.dot(rows2, wup, preferred_element_type=jnp.float32)
    sigma = jax.nn.sigmoid(gate)
    silu = gate * sigma
    act = (silu * up).astype(jnp.bfloat16)
    mixed = sum_rows(jnp.dot(act, wdown, preferred_element_type=jnp.float32))
    layer_output = (hidden_state + mixed).astype(jnp.bfloat16)
    wgate, wup, wdown, second_norm_scale, second_norm_bias = mlp_params(
        gate_weight, up_weight, down_weight, norm2_gain, norm2_shift
    )
    incoming_gradient = cotangent.astype(jnp.float32)
    down_rows = gather_grads(cotangent)
    down_grad = jnp.einsum("sf,sd->fd", act, down_rows, preferred_element_type=jnp.float32)
    dact = jnp.einsum("sd,fd->sf", down_rows, wdown, preferred_element_type=jnp.float32)
    dgate = (dact * up * (sigma * (1.0 + gate * (1.0 - sigma)))).astype(jnp.bfloat16)
    dup = (dact * silu).astype(jnp.bfloat16)
    gate_grad = jnp.einsum("sd,sf->df", rows2, dgate, preferred_element_type=jnp.float32)
    up_grad = jnp.einsum("sd,sf->df", rows2, dup, preferred_element_type=jnp.float32)
    second_norm_gradient = jnp.einsum(
        "sf,df->sd", dgate, wgate, preferred_element_type=jnp.float32
    ) + jnp.einsum("sf,df->sd", dup, wup, preferred_element_type=jnp.float32)
    second_norm_gradient = sum_grads(second_norm_gradient)
    second_scale_partial = jnp.sum(second_norm_gradient * second_standardized, 0)
    shift2_part = jnp.sum(second_norm_gradient, 0)
    hidden_gradient = incoming_gradient + layer_norm_backward(
        second_norm_gradient, second_standardized, second_inverse_deviation, second_norm_scale
    )
    gatew_grad, upw_grad, downw_grad, gain2_total, shift2_total = (
        lax.psum_scatter(
            gate_grad.astype(jnp.bfloat16), "dp", scatter_dimension=0, tiled=True
        ).astype(jnp.float32),
        lax.psum_scatter(
            up_grad.astype(jnp.bfloat16), "dp", scatter_dimension=0, tiled=True
        ).astype(jnp.float32),
        lax.psum_scatter(
            down_grad.astype(jnp.bfloat16), "dp", scatter_dimension=1, tiled=True
        ).astype(jnp.float32),
        lax.psum_scatter(
            second_scale_partial.astype(jnp.bfloat16), "dp", scatter_dimension=0, tiled=True
        ).astype(jnp.float32),
        lax.psum_scatter(
            shift2_part.astype(jnp.bfloat16), "dp", scatter_dimension=0, tiled=True
        ).astype(jnp.float32),
    )
    wqkv, bqkv, wout, first_norm_scale, first_norm_bias = attn_params(
        qkv_weight, qkv_bias, out_weight, norm1_gain, norm1_shift
    )
    branch_rows = gather_grads(hidden_gradient.astype(jnp.bfloat16))
    out_grad = jnp.einsum("sc,sd->cd", attended, branch_rows, preferred_element_type=jnp.float32)
    dattended = jnp.einsum(
        "sd,cd->sc", branch_rows, wout, preferred_element_type=jnp.float32
    ).astype(jnp.bfloat16)
    dattended = dattended.reshape(length, local_heads, HEAD_DIM)

    def backward_block(carry, item):
        dkeys, dvalues = carry
        index, block_lse = item
        qblock = lax.dynamic_slice_in_dim(query, index * block, block, 0)
        dblock = lax.dynamic_slice_in_dim(dattended, index * block, block, 0)
        scores = block_probs(qblock, index * block)
        probs = jnp.exp(scores - block_lse[..., None])
        probs16 = probs.astype(jnp.bfloat16)
        dvalues = dvalues + jnp.einsum(
            "hqk,qhd->khd", probs16, dblock, preferred_element_type=jnp.float32
        )
        dprobs = jnp.einsum("qhd,khd->hqk", dblock, values, preferred_element_type=jnp.float32)
        inner = jnp.sum(dprobs * probs, -1, keepdims=True)
        dscores = (probs * (dprobs - inner)).astype(jnp.bfloat16)
        dquery = (
            jnp.einsum("hqk,khd->qhd", dscores, keys, preferred_element_type=jnp.float32) * scale
        )
        dkeys = (
            dkeys
            + jnp.einsum("hqk,qhd->khd", dscores, qblock, preferred_element_type=jnp.float32)
            * scale
        )
        return ((dkeys, dvalues), dquery)

    empty = jnp.zeros((length, local_heads, HEAD_DIM), jnp.float32)
    (dkeys, dvalues), dquery = lax.scan(backward_block, (empty, empty), (indices, lse))
    dquery = dquery.reshape(length, local_heads, HEAD_DIM)
    dpre = jnp.stack(
        [
            unrotate(dquery, cosine, sine).reshape(length, width),
            unrotate(dkeys, cosine, sine).reshape(length, width),
            dvalues.reshape(length, width),
        ],
        0,
    ).astype(jnp.bfloat16)
    qkv_grad = jnp.einsum("sd,jsc->jdc", rows1, dpre, preferred_element_type=jnp.float32)
    bias_grad = jnp.sum(dpre, axis=1, dtype=jnp.float32)
    first_norm_gradient = sum_grads(
        jnp.einsum("jsc,jdc->sd", dpre, wqkv, preferred_element_type=jnp.float32)
    )
    first_scale_partial = jnp.sum(first_norm_gradient * first_standardized, 0)
    shift1_part = jnp.sum(first_norm_gradient, 0)
    token_gradient = (
        hidden_gradient
        + layer_norm_backward(
            first_norm_gradient, first_standardized, first_inverse_deviation, first_norm_scale
        )
    ).astype(jnp.bfloat16)
    qkvw_grad, qkvb_grad, outw_grad, gain1_total, shift1_total = (
        lax.psum_scatter(
            qkv_grad.astype(jnp.bfloat16), "dp", scatter_dimension=1, tiled=True
        ).astype(jnp.float32),
        lax.psum_scatter(
            bias_grad.astype(jnp.bfloat16), "dp", scatter_dimension=1, tiled=True
        ).astype(jnp.float32),
        lax.psum_scatter(
            out_grad.astype(jnp.bfloat16), "dp", scatter_dimension=1, tiled=True
        ).astype(jnp.float32),
        lax.psum_scatter(
            first_scale_partial.astype(jnp.bfloat16), "dp", scatter_dimension=0, tiled=True
        ).astype(jnp.float32),
        lax.psum_scatter(
            shift1_part.astype(jnp.bfloat16), "dp", scatter_dimension=0, tiled=True
        ).astype(jnp.float32),
    )
    gain1_grad, shift1_grad, gain2_grad, shift2_grad = lax.psum(
        (gain1_total, shift1_total, gain2_total, shift2_total), "tensor"
    )
    return (
        layer_output,
        token_gradient,
        qkvw_grad,
        qkvb_grad,
        outw_grad,
        gain1_grad,
        shift1_grad,
        gatew_grad,
        upw_grad,
        downw_grad,
        gain2_grad,
        shift2_grad,
    )


def solution(mesh):
    placed = (
        P(("dp", "tensor"), None),
        P(None, "dp", "tensor"),
        P(None, ("tensor", "dp")),
        P("tensor", "dp"),
        P("dp"),
        P("dp"),
        P("dp", "tensor"),
        P("dp", "tensor"),
        P("tensor", "dp"),
        P("dp"),
        P("dp"),
        P(("dp", "tensor"), None),
    )
    return jax.shard_map(
        local,
        mesh=mesh,
        in_specs=placed,
        out_specs=(
            P(("dp", "tensor"), None),
            P(("dp", "tensor"), None),
            P(None, "dp", "tensor"),
            P(None, ("tensor", "dp")),
            P("tensor", "dp"),
            P("dp"),
            P("dp"),
            P("dp", "tensor"),
            P("dp", "tensor"),
            P("tensor", "dp"),
            P("dp"),
            P("dp"),
        ),
        check_vma=False,
    )
```

profile of v0, /device:TPU:0, one launch (start us, length us, event | category | flops | bytes accessed | tf_op | source)
XLA Modules:
  0.0 1303.1 jit_solution(2525364318627137801)
XLA Ops:
  11.8 10.4 all-gather.1
  22.2 8.9 all-gather
  35.2 7.9 all-gather.2
  43.4 70.9 %all-gather.15.cloned.1.call-done = bf16[1024,2048]{1,0:T(8,128)(2,1)} async-done(((bf16[256,2048]{1,0:T(8,128)(2,1)}), bf16[1024,2048]{1,0:T(8,128)(2,1)}) %all-gather.15.cloned.1.call-update) | async-done | bytes 4194320 | tf_op jit(solution)/shard_map/all_gather | solution.py:77
  114.3 47.7 %all-gather.17.cloned.1.call-done = bf16[3,2048,512]{1,2,0:T(8,128)(2,1)} async-done(((bf16[3,256,512]{1,2,0:T(8,128)(2,1)}), bf16[3,2048,512]{1,2,0:T(8,128)(2,1)}) %all-gather.17.cloned.1.call-update) | async-done | bytes 6291472 | tf_op jit(solution)/shard_map/all_gather | solution.py:58
  162.0 10.1 add_bitcast_fusion
  174.6 31.0 %while.28 = (s32[]{:T(128)}, bf16[2,512,8,64]{1,3,2,0:T(8,128)(2,1)S(1)}, f32[2,8,512]{2,1,0:T(8,128)S(1)}, s32[2]{0:T(128)S(1)}, bf16[1024,8,64]{0,2,1:T(8,128)...) while((s32[]{:T(128)}, ...), condition=%wide.region_5.6_spmd.clone, body=%wide.region_2.5_spmd.clone.sunk | while | flops 1124856320 | bytes 55709888 | solution.py:153
  207.0 6.3 convolution_convert_fusion.4
  214.0 8.8 all-gather.4
  222.8 8.0 all-gather.3
  230.8 59.4 %reduce-scatter.13.cloned.1.call-done = bf16[256,2048]{1,0:T(8,128)(2,1)} async-done(((bf16[1024,2048]{1,0:T(8,128)(2,1)}), bf16[256,2048]{1,0:T(8,128)(2,1)}) %reduce-scatter.13.cloned.1.call-update) | async-done | bytes 1048592 | tf_op jit(solution)/shard_map/reduce_scatter | solution.py:81
  297.4 38.5 %all-gather.25.cloned.1.call-done = bf16[2048,1408]{1,0:T(8,128)(2,1)} async-done(((bf16[256,1408]{1,0:T(8,128)(2,1)}), bf16[2048,1408]{1,0:T(8,128)(2,1)}) %all-gather.25.cloned.1.call-update) | async-done | bytes 5767184 | tf_op jit(solution)/shard_map/all_gather | solution.py:69
  335.9 82.9 %all-gather.21.cloned.1.call-done = bf16[1024,2048]{1,0:T(8,128)(2,1)} async-done(((bf16[256,2048]{1,0:T(8,128)(2,1)}), bf16[1024,2048]{1,0:T(8,128)(2,1)}) %all-gather.21.cloned.1.call-update) | async-done | bytes 4194320 | tf_op jit(solution)/shard_map/all_gather | solution.py:77
  418.8 11.7 fusion.74
  430.5 32.3 %all-gather.23.cloned.1.call-done = bf16[2048,1408]{1,0:T(8,128)(2,1)} async-done(((bf16[256,1408]{1,0:T(8,128)(2,1)}), bf16[2048,1408]{1,0:T(8,128)(2,1)}) %all-gather.23.cloned.1.call-update) | async-done | bytes 5767184 | tf_op jit(solution)/shard_map/all_gather | solution.py:68
  462.7 11.7 fusion.73
  474.4 70.8 %all-gather.29.cloned.1.call-done = bf16[1024,2048]{1,0:T(8,128)(2,1)} async-done(((bf16[256,2048]{1,0:T(8,128)(2,1)}), bf16[1024,2048]{1,0:T(8,128)(2,1)}) %all-gather.29.cloned.1.call-update) | async-done | bytes 4194320 | tf_op jit(solution)/shard_map/all_gather | solution.py:87
  545.2 45.0 %all-gather.27.cloned.1.call-done = bf16[1408,2048]{1,0:T(8,128)(2,1)} async-done(((bf16[1408,256]{1,0:T(8,128)(2,1)}), bf16[1408,2048]{1,0:T(8,128)(2,1)}) %all-gather.27.cloned.1.call-update) | async-done | bytes 5767184 | tf_op jit(solution)/shard_map/all_gather | solution.py:70
  590.1 16.5 %multiply_convert_fusion.1 = (bf16[1024,1408]{1,0:T(8,128)(2,1)}, bf16[1024,1408]{1,0:T(8,128)(2,1)}, bf16[1024,1408]{1,0:T(8,128)(2,1)}) fusion(f32[1024,1408]{1,0:T(8,128)} %fusion.73, f32[1024,1408]{1,0:T(8,128)} %fusion.74, bf16[1024,2048]{1,0:T(8,128)(2,1)} %all-gather.29.cloned.1.call-done, bf16[1408,2048]{1,0:T(8,128)(2,1)} %all-gather.27.cloned.1.call-done), kind=kOutput, calls=%fused_computation.47 | convolution fusion | flops 5927206912 | bytes 30146560 | tf_op jit(solution)/shard_map/sd,fd->sf/dot_general | solution.py:177
  606.7 8.7 fusion.75
  615.3 22.2 %add_convert_fusion = bf16[1024,2048]{1,0:T(8,128)(2,1)} fusion(f32[1024,2048]{1,0:T(8,128)S(1)} %fusion.75, bf16[1024,1408]{1,0:T(8,128)(2,1)S(1)} %copy-done.48, bf16[2048,1408]{1,0:T(8,128)(2,1)} %all-gather.25.cloned.1.call-done), kind=kOutput, calls=%fused_computation.41 | convolution fusion | flops 5909774336 | bytes 21233664 | tf_op jit(solution)/shard_map/sf,df->sd/dot_general | solution.py:184
  637.6 76.9 %reduce-scatter.17.cloned.1.call-done = bf16[256,2048]{1,0:T(8,128)(2,1)} async-done(((bf16[1024,2048]{1,0:T(8,128)(2,1)}), bf16[256,2048]{1,0:T(8,128)(2,1)}) %reduce-scatter.17.cloned.1.call-update) | async-done | bytes 1048592 | tf_op jit(solution)/shard_map/reduce_scatter | solution.py:91
  719.8 10.5 convolution_convert_fusion
  730.4 11.0 convolution_convert_fusion.1
  741.6 11.0 convolution_convert_fusion.2
  752.6 48.6 %all-gather.31.cloned.1.call-done = bf16[1024,2048]{1,0:T(8,128)(2,1)} async-done(((bf16[256,2048]{1,0:T(8,128)(2,1)}), bf16[1024,2048]{1,0:T(8,128)(2,1)}) %all-gather.31.cloned.1.call-update) | async-done | bytes 4194320 | tf_op jit(solution)/shard_map/all_gather | solution.py:87
  806.7 126.5 %while.29 = (s32[]{:T(128)}, f32[1024,8,64]{0,2,1:T(8,128)}, f32[1024,8,64]{0,2,1:T(8,128)}, f32[2,512,8,64]{1,0,3,2:T(2,128)}, s32[2]{0:T(128)S(1)}, /*index=5*...) while((s32[]{:T(128)}, f32[1024,8,64]{0,2,1:T(8,128)}, ...), condition=%wide.region_15.16_spmd.clone, body=%wide.region_13.15_spmd.clone.sunk | while | flops 2725507584 | bytes 200626592 | solution.py:243
  808.8 5.8 subtract_exponential_fusion.3
  817.6 11.1 multiply_reduce_fusion.3
  828.7 9.5 multiply_convert_fusion.5
  838.2 6.2 fusion.138
  849.7 19.6 %dynamic_update_slice.22 = f32[2,512,8,64]{1,0,3,2:T(2,128)} dynamic-update-slice(f32[2,512,8,64]{1,0,3,2:T(2,128)} %get-tuple-element.457, f32[1,512,8,64]{1,0,3,2:T(1,128)} %copy.80, s32[]{:T(128)S(6)} %copy.97, s32[]{:T(128)} %constant.70.clone.1..sunk.1, s32[]{:T(128)} %constant.70.clone.1..sunk.1, s32[]{:T(128)} %constant.70.clone.1..sunk.1) | dynamic-update-slice | bytes 2097156 | tf_op jit(solution)/shard_map/while/body/jit(dynamic_update_index_in_dim)/dynamic_update_slice | solution.py:243
  870.9 5.8 subtract_exponential_fusion.3
  881.6 11.0 multiply_reduce_fusion.3
  892.6 9.5 multiply_convert_fusion.5
  902.2 6.3 fusion.138
  913.6 19.6 %dynamic_update_slice.22 = f32[2,512,8,64]{1,0,3,2:T(2,128)} dynamic-update-slice(f32[2,512,8,64]{1,0,3,2:T(2,128)} %get-tuple-element.457, f32[1,512,8,64]{1,0,3,2:T(1,128)} %copy.80, s32[]{:T(128)S(6)} %copy.97, s32[]{:T(128)} %constant.70.clone.1..sunk.1, s32[]{:T(128)} %constant.70.clone.1..sunk.1, s32[]{:T(128)} %constant.70.clone.1..sunk.1) | dynamic-update-slice | bytes 2097156 | tf_op jit(solution)/shard_map/while/body/jit(dynamic_update_index_in_dim)/dynamic_update_slice | solution.py:243
  948.8 6.3 convolution_convert_fusion.5
  955.2 10.9 bitcast_convert_fusion
  966.2 11.0 convolution_convert_fusion.3
  977.3 11.2 convert_bitcast_fusion
  997.7 26.8 %reduce-scatter.31.cloned.1.call-done = bf16[64,3]{1,0:T(8,128)(2,1)} async-done(((bf16[512,3]{1,0:T(8,128)(2,1)}), bf16[64,3]{1,0:T(8,128)(2,1)}) %reduce-scatter.31.cloned.1.call-update) | async-done | bytes 400
  1025.9 43.0 %reduce-scatter.23.cloned.1.call-done = bf16[512,256]{1,0:T(8,128)(2,1)} async-done(((bf16[512,2048]{1,0:T(8,128)(2,1)}), bf16[512,256]{1,0:T(8,128)(2,1)}) %reduce-scatter.23.cloned.1.call-update) | async-done | bytes 262160 | tf_op jit(solution)/shard_map/reduce_scatter | solution.py:273
  1070.7 77.3 %reduce-scatter.19.cloned.1.call-done = bf16[256,2048]{1,0:T(8,128)(2,1)} async-done(((bf16[1024,2048]{1,0:T(8,128)(2,1)}), bf16[256,2048]{1,0:T(8,128)(2,1)}) %reduce-scatter.19.cloned.1.call-update) | async-done | bytes 1048592 | tf_op jit(solution)/shard_map/reduce_scatter | solution.py:91
  1151.7 25.2 %all-reduce.5 = (bf16[2048]{0:T(1024)(128)(2,1)S(1)}, bf16[2048]{0:T(1024)(128)(2,1)S(1)}, bf16[2048]{0:T(1024)(128)(2,1)S(1)}, bf16[2048]{0:T(1024)(128)(2,1)S(1)}) all-reduce(bf16[2048]{0:T(1024)(128)(2,1)S(1)} %get-tuple-element.220, bf16[2048]{0:T(1024)(128)(2,1)S(1)} %reduce_sum.154, ...), channel_id=9, replica_groups=mesh['dp'=8,'tensor'=4] {'dp'}, use_global_device_ids=true, to_apply=%region_24.25.clone | all-reduce | flops 8192 | bytes 32768
  1177.2 12.5 all-reduce.4
  1189.7 38.0 %reduce-scatter.15.cloned.1.call-done = bf16[256,2048]{1,0:T(8,128)(2,1)} async-done(((bf16[1024,2048]{1,0:T(8,128)(2,1)}), bf16[256,2048]{1,0:T(8,128)(2,1)}) %reduce-scatter.15.cloned.1.call-update) | async-done | bytes 1048592 | tf_op jit(solution)/shard_map/reduce_scatter | solution.py:81
  1232.5 61.2 %reduce-scatter.21.cloned.1.call-done = bf16[3,256,512]{1,2,0:T(8,128)(2,1)} async-done(((bf16[3,2048,512]{1,2,0:T(8,128)(2,1)}), bf16[3,256,512]{1,2,0:T(8,128)(2,1)}) %reduce-scatter.21.cloned.1.call-update) | async-done | bytes 786448 | tf_op jit(solution)/shard_map/reduce_scatter | solution.py:267
  (259 shorter events, 119.5 us)
Async XLA Ops:
  7.2 24.5 %copy-start.4 = (bf16[256,2048]{1,0:T(8,128)(2,1)S(1)}, bf16[256,2048]{1,0:T(8,128)(2,1)}, u32[]{:S(2)}) copy-start(bf16[256,2048]{1,0:T(8,128)(2,1)} %param.16) | copy-start | bytes 3145732
  7.2 26.0 %copy-start.18 = (bf16[3,256,512]{2,1,0:T(8,128)(2,1)S(1)}, bf16[3,256,512]{2,1,0:T(8,128)(2,1)}, u32[]{:S(2)}) copy-start(bf16[3,256,512]{2,1,0:T(8,128)(2,1)} %param.17) | copy-start | bytes 2359300
  7.2 107.1 %all-gather.15.cloned.1.call-start = ((), (), s32[]{:S(2)}) async-start(), calls=%async_computation.10 | async-start | bytes 5242880 | tf_op jit(solution)/shard_map/all_gather | solution.py:77
  10.1 20.9 %copy-start.31 = (f32[256]{0:T(256)}, f32[256]{0:T(256)S(1)}, u32[]{:S(2)}) copy-start(f32[256]{0:T(256)S(1)} %broadcast_multiply_fusion.5) | copy-start | bytes 3076
  11.8 19.3 %copy-start.35 = (f32[256]{0:T(256)}, f32[256]{0:T(256)S(1)}, u32[]{:S(2)}) copy-start(f32[256]{0:T(256)S(1)} %add_rsqrt_fusion.1) | copy-start | bytes 3076
  33.1 128.9 %all-gather.17.cloned.1.call-start = ((), (), s32[]{:S(2)}) async-start(), calls=%async_computation.11 | async-start | bytes 7077888 | tf_op jit(solution)/shard_map/all_gather | solution.py:58
  34.4 172.6 %all-gather.19.cloned.1.call-start = ((), (), s32[]{:S(2)}) async-start(), calls=%async_computation.12 | async-start | bytes 2359296 | tf_op jit(solution)/shard_map/all_gather | solution.py:60
  35.1 255.1 %reduce-scatter.13.cloned.1.call-start = ((), (), s32[]{:S(2)}) async-start(), calls=%async_computation.13 | async-start | bytes 5242880 | tf_op jit(solution)/shard_map/reduce_scatter | solution.py:81
  43.4 129.8 %copy-start.19 = (f32[1024,16]{0,1:T(8,128)}, f32[1024,16]{0,1:T(8,128)S(1)}, u32[]{:S(2)}) copy-start(f32[1024,16]{0,1:T(8,128)S(1)} %get-tuple-element.292) | copy-start | bytes 196612
  43.4 129.8 %copy-start.21 = (f32[1024,16]{0,1:T(8,128)}, f32[1024,16]{0,1:T(8,128)S(1)}, u32[]{:S(2)}) copy-start(f32[1024,16]{0,1:T(8,128)S(1)} %get-tuple-element.291) | copy-start | bytes 196612
  213.2 76.9 %copy-start.5 = (bf16[256,2048]{1,0:T(8,128)(2,1)S(1)}, bf16[256,2048]{1,0:T(8,128)(2,1)}, u32[]{:S(2)}) copy-start(bf16[256,2048]{1,0:T(8,128)(2,1)} %param.16) | copy-start | bytes 3145732
  213.3 122.7 %all-gather.25.cloned.1.call-start = ((), (), s32[]{:S(2)}) async-start(), calls=%async_computation.16 | async-start | bytes 6488064 | tf_op jit(solution)/shard_map/all_gather | solution.py:69
  213.9 204.9 %all-gather.21.cloned.1.call-start = ((), (), s32[]{:S(2)}) async-start(), calls=%async_computation.14 | async-start | bytes 5242880 | tf_op jit(solution)/shard_map/all_gather | solution.py:77
  230.8 486.8 %copy-start.23 = (f32[8,1,256]{2,1,0:T(1,128)}, f32[8,1,256]{2,1,0:T(1,128)S(1)}, u32[]{:S(2)}) copy-start(f32[8,1,256]{2,1,0:T(1,128)S(1)} %convert_element_type.200) | copy-start | bytes 24580
  291.9 425.7 %copy-start.29 = (f32[256]{0:T(256)}, f32[256]{0:T(256)S(1)}, u32[]{:S(2)}) copy-start(f32[256]{0:T(256)S(1)} %broadcast_multiply_fusion.4) | copy-start | bytes 3076
  293.6 424.0 %copy-start.33 = (f32[256]{0:T(256)}, f32[256]{0:T(256)S(1)}, u32[]{:S(2)}) copy-start(f32[256]{0:T(256)S(1)} %add_rsqrt_fusion) | copy-start | bytes 3076
  295.2 167.6 %all-gather.23.cloned.1.call-start = ((), (), s32[]{:S(2)}) async-start(), calls=%async_computation.15 | async-start | bytes 6488064 | tf_op jit(solution)/shard_map/all_gather | solution.py:68
  295.9 249.3 %all-gather.29.cloned.1.call-start = ((), (), s32[]{:S(2)}) async-start(), calls=%async_computation.19 | async-start | bytes 5242880 | tf_op jit(solution)/shard_map/all_gather | solution.py:87
  296.7 293.5 %all-gather.27.cloned.1.call-start = ((), (), s32[]{:S(2)}) async-start(), calls=%async_computation.17 | async-start | bytes 6488064 | tf_op jit(solution)/shard_map/all_gather | solution.py:70
  297.4 417.1 %reduce-scatter.17.cloned.1.call-start = ((), (), s32[]{:S(2)}) async-start(), calls=%async_computation.20 | async-start | bytes 5242880 | tf_op jit(solution)/shard_map/reduce_scatter | solution.py:91
  590.1 16.5 %copy-start.43 = (bf16[2048,1408]{1,0:T(8,128)(2,1)S(1)}, bf16[2048,1408]{1,0:T(8,128)(2,1)}, u32[]{:S(2)}) copy-start(bf16[2048,1408]{1,0:T(8,128)(2,1)} %all-gather.23.cloned.1.call-done) | copy-start | bytes 17301508
  606.7 8.7 copy-start.48
  637.6 163.6 %all-gather.31.cloned.1.call-start = ((), (), s32[]{:S(2)}) async-start(), calls=%async_computation.21 | async-start | bytes 5242880 | tf_op jit(solution)/shard_map/all_gather | solution.py:87
  719.8 270.8 %reduce-scatter.29.cloned.1.call-start = ((), (), s32[]{:S(2)}) async-start(), calls=%async_computation.27 | async-start | bytes 6488064 | tf_op jit(solution)/shard_map/reduce_scatter | solution.py:198
  730.4 262.5 %reduce-scatter.27.cloned.1.call-start = ((), (), s32[]{:S(2)}) async-start(), calls=%async_computation.26 | async-start | bytes 6488064 | tf_op jit(solution)/shard_map/reduce_scatter | solution.py:195
  741.5 253.9 %reduce-scatter.25.cloned.1.call-start = ((), (), s32[]{:S(2)}) async-start(), calls=%async_computation.25 | async-start | bytes 6488064 | tf_op jit(solution)/shard_map/reduce_scatter | solution.py:192
  752.5 48.6 %copy-start.44 = (bf16[512,2048]{1,0:T(8,128)(2,1)S(1)}, bf16[512,2048]{1,0:T(8,128)(2,1)}, u32[]{:S(2)}) copy-start(bf16[512,2048]{1,0:T(8,128)(2,1)} %all-gather.19.cloned.1.call-done) | copy-start | bytes 6291460
  752.6 272.0 %reduce-scatter.31.cloned.1.call-start = ((), (), s32[]{:S(2)}) async-start(), calls=%async_computation.28 | async-start | bytes 147456
  847.6 21.6 %copy-start.2 = (f32[1024,8,64]{0,2,1:T(8,128)}, f32[1024,8,64]{0,2,1:T(8,128)S(1)}, u32[]{:S(2)}) copy-start(f32[1024,8,64]{0,2,1:T(8,128)S(1)} %bitcast_add_fusion.4) | copy-start | bytes 6291460 | tf_op jit(solution)/shard_map/while
  847.6 21.6 %copy-start.26 = (f32[2,8,512]{2,1,0:T(8,128)S(1)}, f32[2,8,512]{2,1,0:T(8,128)}, u32[]{:S(2)}) copy-start(f32[2,8,512]{2,1,0:T(8,128)} %copy-done.25) | copy-start | bytes 98308 | tf_op jit(solution)/shard_map/while
  911.6 21.7 %copy-start.2 = (f32[1024,8,64]{0,2,1:T(8,128)}, f32[1024,8,64]{0,2,1:T(8,128)S(1)}, u32[]{:S(2)}) copy-start(f32[1024,8,64]{0,2,1:T(8,128)S(1)} %bitcast_add_fusion.4) | copy-start | bytes 6291460 | tf_op jit(solution)/shard_map/while
  911.6 21.7 %copy-start.26 = (f32[2,8,512]{2,1,0:T(8,128)S(1)}, f32[2,8,512]{2,1,0:T(8,128)}, u32[]{:S(2)}) copy-start(f32[2,8,512]{2,1,0:T(8,128)} %copy-done.25) | copy-start | bytes 98308 | tf_op jit(solution)/shard_map/while
  933.2 7.4 copy-start.20
  948.8 120.2 %reduce-scatter.23.cloned.1.call-start = ((), (), s32[]{:S(2)}) async-start(), calls=%async_computation.24 | async-start | bytes 2359296 | tf_op jit(solution)/shard_map/reduce_scatter | solution.py:273
  955.1 192.9 %reduce-scatter.19.cloned.1.call-start = ((), (), s32[]{:S(2)}) async-start(), calls=%async_computation.22 | async-start | bytes 5242880 | tf_op jit(solution)/shard_map/reduce_scatter | solution.py:91
  966.1 261.6 %reduce-scatter.15.cloned.1.call-start = ((), (), s32[]{:S(2)}) async-start(), calls=%async_computation.18 | async-start | bytes 5242880 | tf_op jit(solution)/shard_map/reduce_scatter | solution.py:81
  977.2 316.5 %reduce-scatter.21.cloned.1.call-start = ((), (), s32[]{:S(2)}) async-start(), calls=%async_computation.23 | async-start | bytes 7077888 | tf_op jit(solution)/shard_map/reduce_scatter | solution.py:267
  992.9 156.6 %copy-start.6 = (bf16[256,2048]{1,0:T(8,128)(2,1)S(1)}, bf16[256,2048]{1,0:T(8,128)(2,1)}, u32[]{:S(2)}) copy-start(bf16[256,2048]{1,0:T(8,128)(2,1)} %param.16) | copy-start | bytes 3145732
  992.9 156.6 %copy-start.28 = (f32[8,1,256]{2,1,0:T(1,128)S(1)}, f32[8,1,256]{2,1,0:T(1,128)}, u32[]{:S(2)}) copy-start(f32[8,1,256]{2,1,0:T(1,128)} %copy-done.27) | copy-start | bytes 24580
  992.9 156.6 %copy-start.32 = (f32[256]{0:T(256)S(1)}, f32[256]{0:T(256)}, u32[]{:S(2)}) copy-start(f32[256]{0:T(256)} %copy-done.31) | copy-start | bytes 3076
  992.9 156.6 %copy-start.36 = (f32[256]{0:T(256)S(1)}, f32[256]{0:T(256)}, u32[]{:S(2)}) copy-start(f32[256]{0:T(256)} %copy-done.35) | copy-start | bytes 3076
  995.3 156.4 %copy-start.37 = (bf16[2048]{0:T(1024)(128)(2,1)S(1)}, bf16[2048]{0:T(1024)(128)(2,1)}, u32[]{:S(2)}) copy-start(bf16[2048]{0:T(1024)(128)(2,1)} %get-tuple-element.218) | copy-start | bytes 12292
  995.3 232.4 %copy-start.9 = (bf16[256,2048]{1,0:T(8,128)(2,1)S(1)}, bf16[256,2048]{1,0:T(8,128)(2,1)}, u32[]{:S(2)}) copy-start(bf16[256,2048]{1,0:T(8,128)(2,1)} %reduce-scatter.13.cloned.1.call-done) | copy-start | bytes 3145732
  995.3 232.4 %copy-start.24 = (f32[8,1,256]{2,1,0:T(1,128)S(1)}, f32[8,1,256]{2,1,0:T(1,128)}, u32[]{:S(2)}) copy-start(f32[8,1,256]{2,1,0:T(1,128)} %copy-done.23) | copy-start | bytes 24580
  995.3 232.4 %copy-start.30 = (f32[256]{0:T(256)S(1)}, f32[256]{0:T(256)}, u32[]{:S(2)}) copy-start(f32[256]{0:T(256)} %copy-done.29) | copy-start | bytes 3076
  995.3 232.4 %copy-start.34 = (f32[256]{0:T(256)S(1)}, f32[256]{0:T(256)}, u32[]{:S(2)}) copy-start(f32[256]{0:T(256)} %copy-done.33) | copy-start | bytes 3076
  995.3 232.4 %copy-start.39 = (f32[256]{0:T(256)S(1)}, f32[256]{0:T(256)}, u32[]{:S(2)}) copy-start(f32[256]{0:T(256)} %copy-done.38) | copy-start | bytes 3076
  995.3 232.4 %copy-start.41 = (f32[256]{0:T(256)S(1)}, f32[256]{0:T(256)}, u32[]{:S(2)}) copy-start(f32[256]{0:T(256)} %copy-done.40) | copy-start | bytes 3076
  (26 other events, 87.6 us)
Sparse Core Ops, SparseCore 0:
  33.3 81.0 all-gather.14
  116.8 45.1 all-gather.16
  163.9 28.1 all-gather.18
  213.4 76.7 reduce-scatter.12
  292.1 43.8 all-gather.24
  338.0 80.7 all-gather.20
  420.8 41.8 all-gather.22
  464.4 80.7 all-gather.28
  547.2 42.8 all-gather.26
  637.7 76.7 reduce-scatter.16
  719.9 81.2 all-gather.30
  804.5 57.5 reduce-scatter.28
  866.0 59.1 reduce-scatter.26
  928.4 59.0 reduce-scatter.24
  991.2 33.3 reduce-scatter.30
  1027.7 41.2 reduce-scatter.22
  1071.2 76.7 reduce-scatter.18
  1150.2 77.5 reduce-scatter.14
  1231.5 62.2 reduce-scatter.20
where the time goes:
time: 1310 us; the launch traced here: 1300 us
  waiting for transfers between devices  823 us (63%)
  matrix products  243 us (19%)
  blocking collectives  81.7 us (6%)
  other arithmetic  67.9 us (5%)
  local copies, waits for them, and re-layouts  67.5 us (5%)
  between operations  15.6 us (1%)
    reduce_scatter x2, waiting for transfers between devices, sum_grads(): lax.psum_scatter(partial_value.astype(jnp.bfloat16), 'tensor', scatter_di...  154 us
    all_gather x2, waiting for transfers between devices, gather_rows(): return lax.all_gather(rows, 'tensor', axis=0, tiled=True)  154 us
    all_gather x2, waiting for transfers between devices, gather_grads(): return lax.all_gather(rows, 'tensor', axis=0, tiled=True)  119 us
    reduce_scatter x2, waiting for transfers between devices, sum_rows(): lax.psum_scatter(partial_value.astype(jnp.bfloat16), 'tensor', scatter_di...  97.4 us
    reduce_scatter x1, waiting for transfers between devices, local(): lax.psum_scatter(qkv_grad.astype(jnp.bfloat16), 'dp', scatter_dimension=1...  61.2 us
    all_gather x1, waiting for transfers between devices, attn_params(): lax.all_gather(qkv_weight, 'dp', axis=1, tiled=True)  47.7 us
    all_gather x1, waiting for transfers between devices, mlp_params(): lax.all_gather(down_weight, 'dp', axis=1, tiled=True)  45 us
    dynamic_update_slice x4, local copies, waits for them, and re-layouts, local(): lax.scan(backward_block, (empty, empty), (indices, lse))  43.3 us
  transfers between devices with their start and end apart: 19, of which 15 were waited for; matrix products, arithmetic and copies ran while one was open for 24% of the time, Pallas kernels for 0%

commit v1 on v0

--- a/solution.py
+++ b/solution.py
@@ -1,10 +1,325 @@
+import functools
+
 import jax
 import jax.numpy as jnp
 from jax import lax
+from jax.experimental import pallas as pl
+from jax.experimental.pallas import tpu as pltpu
 from jax.sharding import PartitionSpec as P
 
+MESH = pl.DeviceIdType.MESH
 HEAD_DIM = 64
 ROT = 16
+BF = jnp.bfloat16
+F32 = jnp.float32
+VMEM_LIMIT = 56 * 1024 * 1024
+ANY = pl.BlockSpec(memory_space=pl.ANY)
+INV = pl.BlockSpec(memory_space=pltpu.VMEM)
+
+
+def nt(a, b):
+    return lax.dot_general(a, b, (((1,), (1,)), ((), ())), preferred_element_type=F32)
+
+
+def tn(a, b):
+    return lax.dot_general(a, b, (((0,), (0,)), ((), ())), preferred_element_type=F32)
+
+
+def nn(a, b):
+    return jnp.dot(a, b, preferred_element_type=F32)
+
+
+def place():
+    d = lax.axis_index("dp")
+    z = lax.axis_index("tensor")
+    dy = 4 * (1 - 2 * lax.div(d, 4))
+    dx = 2 * (1 - 2 * lax.rem(lax.div(d, 2), 2))
+    dc = 1 - 2 * lax.rem(d, 2)
+    return d, z, (0, dc, dx, dx + dc, dy, dy + dc, dy + dx, dy + dx + dc)
+
+
+def send(src, dst, ssem, rsem, d, z):
+    return pltpu.make_async_remote_copy(
+        src_ref=src, dst_ref=dst, send_sem=ssem, recv_sem=rsem, device_id=(d, z), device_id_type=MESH
+    )
+
+
+def greet(d, z, flips, line, plane):
+    barrier = pltpu.get_barrier_semaphore()
+    for k in range(1, line):
+        pl.semaphore_signal(
+            barrier, inc=1, device_id=(d, lax.rem(z + k, line)), device_id_type=MESH
+        )
+    for r in plane:
+        pl.semaphore_signal(barrier, inc=1, device_id=(d + flips[r], z), device_id_type=MESH)
+    pl.semaphore_wait(barrier, line - 1 + len(plane))
+
+
+class LineGather:
+    def __init__(self, view, chunks, d, z, line, send_sems, recv_sems):
+        self.view, self.chunks, self.d, self.z, self.line = view, chunks, d, z, line
+        self.ss, self.rs = send_sems, recv_sems
+
+    def copy(self, s, h, way, src=None):
+        ref = self.view(s, h)
+        return send(
+            ref if src is None else src, ref, self.ss.at[way, s, h], self.rs.at[s, h],
+            self.d, self.z + (1 if way == 0 else -1),
+        )
+
+    def start(self, h, src=None):
+        pl.when(self.z < self.line - 1)(lambda: self.copy(self.z, h, 0, src).start())
+        pl.when(self.z > 0)(lambda: self.copy(self.z, h, 1, src).start())
+
+    def step(self, k, h):
+        z, line = self.z, self.line
+
+        @pl.when(z - k >= 0)
+        def _():
+            self.copy(z - k, h, 0).wait_recv()
+            pl.when(z < line - 1)(lambda: self.copy(z - k, h, 0).start())
+
+        @pl.when(z + k < line)
+        def _():
+            self.copy(z + k, h, 1).wait_recv()
+            pl.when(z > 0)(lambda: self.copy(z + k, h, 1).start())
+
+    def finish(self):
+        z, line = self.z, self.line
+        for k in range(line):
+            for h in range(self.chunks):
+                pl.when((z - k >= 0) & (z < line - 1))(lambda: self.copy(z - k, h, 0).wait_send())
+                pl.when((z + k < line) & (z > 0))(lambda: self.copy(z + k, h, 1).wait_send())
+
+
+def arrival(z, i):
+    orders = ((0, 1, 2, 3), (1, 0, 2, 3), (2, 3, 1, 0), (3, 2, 1, 0))
+    codes = [sum(s * 4**j for j, s in enumerate(o)) for o in orders]
+    code = jnp.where(
+        z == 0, codes[0], jnp.where(z == 1, codes[1], jnp.where(z == 2, codes[2], codes[3]))
+    )
+    power = jnp.where(i == 0, 1, jnp.where(i == 1, 4, jnp.where(i == 2, 16, 64)))
+    return lax.rem(lax.div(code, power), 4)
+
+
+def turn(u, cos, sin_up, sin_down, sign=1.0):
+    moved = pltpu.roll(u, 8, 1) * sin_up + pltpu.roll(u, 120, 1) * sin_down
+    return u * cos + moved if sign > 0 else u * cos - moved
+
+
+def attention_kernel(
+    tok, cot, wq, smalls, cos, sin_up, sin_down,
+    xall, cotall, n1, qkv, lse, attall, wqkv, small_sum,
+    xbuf, n1buf, wbuf, qbuf, abuf, smbuf,
+    tss, trs, css, crs, ass, ars, wss, wrs, mss, mrs, local,
+):
+    rows = tok.shape[0]
+    width = wq.shape[2]
+    pairs = width // 128
+    line = 4
+    d, z, flips = place()
+    greet(d, z, flips, line, range(1, 8))
+
+    tok_in = pltpu.make_async_copy(tok, xbuf.at[z], local.at[0])
+    tok_in.start()
+    cot_in = pltpu.make_async_copy(cot, cotall.at[pl.ds(z * rows, rows)], local.at[1])
+    cot_in.start()
+    depth = wq.shape[1]
+
+    def wblock(i):
+        return wbuf.at[:, pl.ds(pl.multiple_of(i * depth, 256), depth), :]
+
+    w_in = pltpu.make_async_copy(wq, wblock(d), local.at[2])
+    w_in.start()
+    small_copies = [
+        send(smalls, smbuf.at[r], mss.at[r], mrs.at[r], d + flips[r], z) for r in range(1, 8)
+    ]
+    for copy in small_copies:
+        copy.start()
+    w_sends = {
+        r: send(wq, wblock(d), wss.at[r], wrs.at[r], d + flips[r], z) for r in (4, 2, 1, 6)
+    }
+    half = rows // 2
+
+    def tview(s, h):
+        return xbuf.at[s, pl.ds(h * half, half)]
+
+    def cview(s, h):
+        return cotall.at[pl.ds(pl.multiple_of(s * rows + h * half, 128), half)]
+
+    def aview(s, h):
+        return attall.at[:, pl.ds(pl.multiple_of(s * width + h * 128, 128), 128)]
+
+    toks = LineGather(tview, 2, d, z, line, tss, trs)
+    cots = LineGather(cview, 2, d, z, line, css, crs)
+    atts = LineGather(aview, pairs, d, z, line, ass, ars)
+    tok_in.wait()
+    for h in range(2):
+        toks.start(h)
+    for copy in w_sends.values():
+        copy.start()
+    for copy in small_copies:
+        copy.wait()
+    total = smalls[...].astype(F32)
+    for r in range(1, 8):
+        total = total + smbuf[r].astype(F32)
+    small_sum[...] = total
+
+    def normalise(s):
+        piece = 32
+
+        @pl.loop(0, rows // piece)
+        def _(i):
+            at = pl.ds(pl.multiple_of(i * piece, piece), piece)
+            x = xbuf[s, at, :].astype(F32)
+            centred = x - jnp.mean(x, -1, keepdims=True)
+            spread = jnp.mean(centred * centred, -1, keepdims=True)
+            n = centred * lax.rsqrt(spread + 1e-05) * small_sum[0:1, :] + small_sum[1:2, :]
+            n1buf[pl.ds(pl.multiple_of(s * rows + i * piece, piece), piece), :] = n.astype(BF)
+
+    def project(s):
+        at = pl.ds(pl.multiple_of(s * rows, rows), rows)
+        for j in range(3):
+            pre = nn(n1buf[at, :], wbuf[j]) + small_sum[4 + j : 5 + j, :width]
+            for p in range(pairs):
+                part = pre[:, p * 128 : (p + 1) * 128]
+                if j < 2:
+                    part = turn(part, cos[at, :], sin_up[at, :], sin_down[at, :])
+                qbuf[j, p, at, :] = part.astype(BF)
+
+    for h in range(2):
+        toks.step(1, h)
+    for r in (2, 4, 6):
+        w_sends[r].wait_recv()
+        send(wblock(d + flips[r]), wblock(d + flips[r]), wss.at[r + 1], wrs.at[r + 1], d + flips[1], z).start()
+    w_in.wait()
+    w_sends[1].wait_recv()
+    for r in (3, 5, 7):
+        send(wblock(d), wblock(d), wss.at[r], wrs.at[r], d + flips[1], z).wait_recv()
+
+    @pl.loop(0, line)
+    def _(i):
+        @pl.when(i == line - 1)
+        def _():
+            cot_in.wait()
+            for h in range(2):
+                cots.start(h)
+
+        s = arrival(z, i)
+        normalise(s)
+        project(s)
+
+        @pl.when((i >= 1) & (i < line - 1))
+        def _():
+            for h in range(2):
+                toks.step(i + 1, h)
+
+    outs = [
+        pltpu.make_async_copy(n1buf, n1, local.at[3]),
+        pltpu.make_async_copy(wbuf, wqkv, local.at[4]),
+        pltpu.make_async_copy(qbuf, qkv, local.at[5]),
+    ] + [
+        pltpu.make_async_copy(xbuf.at[s], xall.at[pl.ds(s * rows, rows)], local.at[6 + s])
+        for s in range(line)
+    ]
+    for copy in outs:
+        copy.start()
+
+    lanes = lax.broadcasted_iota(jnp.int32, (1, 128), 1)
+    first = lanes < 64
+    lse[...] = jnp.zeros_like(lse)
+    length = rows * line
+
+    def attend(p, start):
+        for qi in range(line):
+            count = (qi + 1) * rows
+            at = pl.ds(qi * rows, rows)
+            q = qbuf[0, p, at, :] * BF(HEAD_DIM**-0.5)
+            k = qbuf[1, p, pl.ds(0, count), :]
+            v = qbuf[2, p, pl.ds(0, count), :]
+            row = lax.broadcasted_iota(jnp.int32, (rows, count), 0) + qi * rows
+            col = lax.broadcasted_iota(jnp.int32, (rows, count), 1)
+            keep = row >= col
+            results = []
+            stats = lse[at, :]
+            for a in range(2):
+                mine = first if a == 0 else ~first
+                s = nt(jnp.where(mine, q, BF(0)), k)
+                s = jnp.where(keep, s, -1e30)
+                most = jnp.max(s, -1, keepdims=True)
+                e = jnp.exp(s - most)
+                total = jnp.sum(e, -1, keepdims=True)
+                results.append(nn(e.astype(BF), v) / total)
+                stats = jnp.where(lanes == 2 * p + a, most + jnp.log(total), stats)
+            lse[at, :] = stats
+            abuf[p, at, :] = jnp.where(first, results[0], results[1]).astype(BF)
+
+    def own_columns(p):
+        return pltpu.make_async_copy(abuf.at[p], aview(z, p), local.at[10 + p])
+
+    @pl.loop(0, pairs)
+    def _(p):
+        attend(p, None)
+        own_columns(p).start()
+        atts.start(p, abuf.at[p])
+
+    for k in range(1, line):
+        for h in range(2):
+            cots.step(k, h)
+        for p in range(pairs):
+            atts.step(k, p)
+    for gather in (toks, cots, atts):
+        gather.finish()
+    for r in range(1, 8):
+        send(wblock(d), wblock(d), wss.at[r], wrs.at[r], d + flips[1], z).wait_send()
+    for copy in outs:
+        copy.wait()
+    for p in range(pairs):
+        own_columns(p).wait()
+
+
+def attention_forward(tok, cot, wq, smalls, tabs):
+    rows, model = tok.shape
+    line = 4
+    length = rows * line
+    _, depth, width = wq.shape
+    pairs = width // 128
+    dp = model // depth
+    sds = jax.ShapeDtypeStruct
+    return pl.pallas_call(
+        attention_kernel,
+        out_shape=(
+            sds((length, model), BF), sds((length, model), BF), sds((length, model), BF),
+            sds((3, pairs, length, 128), BF), sds((length, 128), F32), sds((length, model), BF),
+            sds((3, model, width), BF), sds((16, model), F32),
+        ),
+        in_specs=[ANY, ANY, ANY, INV, INV, INV, INV],
+        out_specs=(ANY, ANY, ANY, ANY, INV, ANY, ANY, INV),
+        scratch_shapes=[
+            pltpu.VMEM((line, rows, model), BF),
+            pltpu.VMEM((length, model), BF),
+            pltpu.VMEM((3, model, width), BF),
+            pltpu.VMEM((3, pairs, length, 128), BF),
+            pltpu.VMEM((pairs, length, 128), BF),
+            pltpu.VMEM((dp, 16, model), BF),
+            pltpu.SemaphoreType.DMA((2, line, 2)),
+            pltpu.SemaphoreType.DMA((line, 2)),
+            pltpu.SemaphoreType.DMA((2, line, 2)),
+            pltpu.SemaphoreType.DMA((line, 2)),
+            pltpu.SemaphoreType.DMA((2, line, pairs)),
+            pltpu.SemaphoreType.DMA((line, pairs)),
+            pltpu.SemaphoreType.DMA((8,)),
+            pltpu.SemaphoreType.DMA((8,)),
+            pltpu.SemaphoreType.DMA((8,)),
+            pltpu.SemaphoreType.DMA((8,)),
+            pltpu.SemaphoreType.DMA((16,)),
+        ],
+        compiler_params=pltpu.CompilerParams(
+            collective_id=1, has_side_effects=True, vmem_limit_bytes=VMEM_LIMIT
+        ),
+        cost_estimate=pl.CostEstimate(flops=2 * 10**11, bytes_accessed=10**8, transcendentals=0),
+        name="attention_forward",
+    )(tok, cot, wq, smalls, *tabs)
 
 
 def apply_layer_norm(value, norm_scale, norm_bias):
@@ -299,6 +614,152 @@
     )
 
 
+def turn_tables(length):
+    cosine, sine = tables(length)
+    rest = HEAD_DIM - ROT
+    half = ROT // 2
+    cos = jnp.concatenate([cosine, jnp.ones((length, rest), F32)], -1)
+    none = jnp.zeros((length, half), F32)
+    tail = jnp.zeros((length, rest), F32)
+    up = jnp.concatenate([none, sine[:, half:], tail], -1)
+    down = jnp.concatenate([-sine[:, :half], none, tail], -1)
+    return tuple(jnp.concatenate([t, t], -1) for t in (cos, up, down))
+
+
+def pack_smalls(d, model, qkv_bias, *vectors):
+    col = lax.broadcasted_iota(jnp.int32, (1, model), 1)
+    each = vectors[0].shape[0]
+    gains = jnp.stack([jnp.tile(v, model // each) for v in vectors], 0)
+    gains = jnp.where(col // each == d, gains, 0)
+    part = qkv_bias.shape[1]
+    bias = jnp.where(col // part == d, jnp.tile(qkv_bias, (1, model // part)), 0)
+    return jnp.concatenate([gains, bias, jnp.zeros((9, model), BF)], 0).astype(BF)
+
+
+def fast(
+    tokens, qkv_weight, qkv_bias, out_weight, norm1_gain, norm1_shift, gate_weight, up_weight,
+    down_weight, norm2_gain, norm2_shift, cotangent,
+):
+    scale = HEAD_DIM ** (-0.5)
+    d = lax.axis_index("dp")
+    z = lax.axis_index("tensor")
+    rows, model = tokens.shape
+    length = 4 * rows
+    tabs = turn_tables(length)
+    smalls = pack_smalls(d, model, qkv_bias, norm1_gain, norm1_shift, norm2_gain, norm2_shift)
+    xall, cotall, n1, qkv, lse, attall, wqkv, small_sum = attention_forward(
+        tokens, cotangent, qkv_weight, smalls, tabs
+    )
+    wout = lax.all_gather(out_weight, "tensor", axis=0, tiled=True)
+    wout = lax.all_gather(wout, "dp", axis=1, tiled=True)
+    wgate = lax.all_gather(gate_weight, "dp", axis=0, tiled=True)
+    wup = lax.all_gather(up_weight, "dp", axis=0, tiled=True)
+    wdown = lax.all_gather(down_weight, "dp", axis=1, tiled=True)
+    g1, b1, g2, b2 = small_sum[0], small_sum[1], small_sum[2], small_sum[3]
+
+    def own(a):
+        return lax.dynamic_slice_in_dim(a, z * rows, rows, 0)
+
+    hidden_all = xall.astype(F32) + nn(attall, wout)
+    n2_all, xhat_all, inv_all = apply_layer_norm(hidden_all, g2, b2)
+    rows2 = n2_all.astype(BF)
+    hidden_state, second_standardized, second_inverse_deviation = own(hidden_all), own(xhat_all), own(inv_all)
+    gate = nn(rows2, wgate)
+    up = nn(rows2, wup)
+    sigma = jax.nn.sigmoid(gate)
+    silu = gate * sigma
+    act = (silu * up).astype(BF)
+    mixed = sum_rows(nn(act, wdown))
+    layer_output = (hidden_state + mixed).astype(BF)
+    down_grad = tn(act, cotall)
+    dact = nt(cotall, wdown)
+    dgate = (dact * up * (sigma * (1.0 + gate * (1.0 - sigma)))).astype(BF)
+    dup = (dact * silu).astype(BF)
+    gate_grad = tn(rows2, dgate)
+    up_grad = tn(rows2, dup)
+    dn2 = sum_grads(nt(dgate, wgate) + nt(dup, wup))
+    second_scale_partial = jnp.sum(dn2 * second_standardized, 0)
+    shift2_part = jnp.sum(dn2, 0)
+    hidden_gradient = cotangent.astype(F32) + layer_norm_backward(
+        dn2, second_standardized, second_inverse_deviation, g2
+    )
+
+    def scatter(a, axis):
+        return lax.psum_scatter(a.astype(BF), "dp", scatter_dimension=axis, tiled=True)
+
+    gatew_grad = scatter(gate_grad, 0).astype(F32)
+    upw_grad = scatter(up_grad, 0).astype(F32)
+    downw_grad = scatter(down_grad, 1).astype(F32)
+    da = hidden_gradient.astype(BF)
+    out_grad = scatter(tn(own(attall), da), 1)
+    outw_grad = lax.psum_scatter(out_grad, "tensor", scatter_dimension=0, tiled=True).astype(F32)
+    dattended = nt(da, wout).astype(BF)
+    dattended = lax.all_to_all(dattended, "tensor", split_axis=1, concat_axis=0, tiled=True)
+    cosine, sine = tables(length)
+    width = wqkv.shape[2]
+    local_heads = width // HEAD_DIM
+    dattended = dattended.reshape(length, local_heads, HEAD_DIM)
+    query, keys, values = [
+        qkv[j].transpose(1, 0, 2).reshape(length, local_heads, HEAD_DIM) for j in range(3)
+    ]
+    stats = lse[:, :local_heads].T
+    cols = jnp.arange(length, dtype=jnp.int32)
+    block = 512
+
+    def backward_block(carry, index):
+        dkeys, dvalues = carry
+        qblock = lax.dynamic_slice_in_dim(query, index * block, block, 0)
+        dblock = lax.dynamic_slice_in_dim(dattended, index * block, block, 0)
+        block_lse = lax.dynamic_slice_in_dim(stats, index * block, block, 1)
+        scores = jnp.einsum("qhd,khd->hqk", qblock, keys, preferred_element_type=F32) * scale
+        keep = (index * block + jnp.arange(block, dtype=jnp.int32))[:, None] >= cols[None, :]
+        scores = jnp.where(keep[None], scores, -1e30)
+        probs = jnp.exp(scores - block_lse[..., None])
+        probs16 = probs.astype(BF)
+        dvalues = dvalues + jnp.einsum("hqk,qhd->khd", probs16, dblock, preferred_element_type=F32)
+        dprobs = jnp.einsum("qhd,khd->hqk", dblock, values, preferred_element_type=F32)
+        inner = jnp.sum(dprobs * probs, -1, keepdims=True)
+        dscores = (probs * (dprobs - inner)).astype(BF)
+        dquery = jnp.einsum("hqk,khd->qhd", dscores, keys, preferred_element_type=F32) * scale
+        dkeys = dkeys + jnp.einsum("hqk,qhd->khd", dscores, qblock, preferred_element_type=F32) * scale
+        return ((dkeys, dvalues), dquery)
+
+    empty = jnp.zeros((length, local_heads, HEAD_DIM), F32)
+    (dkeys, dvalues), dquery = lax.scan(backward_block, (empty, empty), jnp.arange(2, dtype=jnp.int32))
+    dquery = dquery.reshape(length, local_heads, HEAD_DIM)
+    dpre = jnp.stack(
+        [
+            unrotate(dquery, cosine, sine).reshape(length, width),
+            unrotate(dkeys, cosine, sine).reshape(length, width),
+            dvalues.reshape(length, width),
+        ],
+        0,
+    ).astype(BF)
+    qkv_grad = jnp.einsum("sd,jsc->jdc", n1, dpre, preferred_element_type=F32)
+    bias_grad = jnp.sum(dpre, axis=1, dtype=F32)
+    dn1 = sum_grads(jnp.einsum("jsc,jdc->sd", dpre, wqkv, preferred_element_type=F32))
+    _, first_standardized, first_inverse_deviation = apply_layer_norm(tokens.astype(F32), g1, b1)
+    token_gradient = (
+        hidden_gradient
+        + layer_norm_backward(dn1, first_standardized, first_inverse_deviation, g1)
+    ).astype(BF)
+    qkvw_grad = scatter(qkv_grad, 1).astype(F32)
+    small = jnp.concatenate(
+        [
+            jnp.stack(
+                [jnp.sum(dn1 * first_standardized, 0), jnp.sum(dn1, 0), second_scale_partial, shift2_part], 0
+            ),
+        ],
+        0,
+    )
+    small = lax.psum_scatter(lax.psum(small, "tensor"), "dp", scatter_dimension=1, tiled=True)
+    qkvb_grad = lax.psum_scatter(bias_grad, "dp", scatter_dimension=1, tiled=True)
+    return (
+        layer_output, token_gradient, qkvw_grad, qkvb_grad, outw_grad, small[0], small[1],
+        gatew_grad, upw_grad, downw_grad, small[2], small[3],
+    )
+
+
 def solution(mesh):
     placed = (
         P(("dp", "tensor"), None),
@@ -315,7 +776,7 @@
         P(("dp", "tensor"), None),
     )
     return jax.shard_map(
-        local,
+        fast if dict(mesh.shape) == {"dp": 8, "tensor": 4} else local,
         mesh=mesh,
         in_specs=placed,
         out_specs=(

time: 1310 us -> 1280 us (0.977)
  Pallas kernels: 0 us -> 243 us
  waiting for transfers between devices: 823 us -> 613 us
  blocking collectives: 81.7 us -> 11.7 us
  local copies, waits for them, and re-layouts: 67.5 us -> 96.9 us
  matrix products: 243 us -> 215 us
    all_gather x9 -> x5, waiting for transfers between devices: 436 us -> 32.3 us  [the longest x1 32.3 us: fast(): wout = lax.all_gather(out_weight, 'tensor', axis=0, tiled=True)]
    pallas_call x0 -> x1, Pallas kernels: none -> 243 us  [attention_forward(): pl.pallas_call(attention_kernel, out_shape=(sds((length, model), BF), sds...]
    reduce_scatter x5 -> x6, waiting for transfers between devices: 104 us -> 319 us  [the longest x5 292 us: scatter(): lax.psum_scatter(a.astype(BF), 'dp', scatter_dimension=axis, tiled=True)]
    reduce_scatter x2, waiting for transfers between devices: 154 us -> 94.1 us  [sum_grads(): lax.psum_scatter(partial_value.astype(jnp.bfloat16), 'tensor', scatter_di...]
    all_gather x5 -> x0, blocking collectives: 43.9 us -> none  [the longest x1 10.4 us: attn_params(): lax.all_gather(norm1_shift, 'dp', axis=0, tiled=True)]
    unnamed x20 -> x18, waiting for transfers between devices: 30.3 us -> 73 us
    dot_general x29 -> x24, matrix products: 243 us -> 215 us  [the longest x4 47.5 us: nn(): return jnp.dot(a, b, preferred_element_type=F32)]
    unnamed x1 -> x0, blocking collectives: 25.2 us -> none
  transfers between devices with their start and end apart: 19 -> 17, of which waited for: 15 -> 13; matrix products, arithmetic and copies ran while one was open for 24% -> 12% of each run, Pallas kernels for 0% -> 19%
where the time goes in v1:
time: 1280 us; the launch traced here: 1270 us
  waiting for transfers between devices  613 us (48%)
  Pallas kernels  243 us (19%)
  matrix products  215 us (17%)
  local copies, waits for them, and re-layouts  96.9 us (8%)
  other arithmetic  65.7 us (5%)
  between operations  14.7 us (1%)
    reduce_scatter x5, waiting for transfers between devices, scatter(): lax.psum_scatter(a.astype(BF), 'dp', scatter_dimension=axis, tiled=True)  292 us
    pallas_call x1, Pallas kernels, attention_forward(): pl.pallas_call(attention_kernel, out_shape=(sds((length, model), BF), sds...  243 us
    reduce_scatter x2, waiting for transfers between devices, sum_grads(): lax.psum_scatter(partial_value.astype(jnp.bfloat16), 'tensor', scatter_di...  94.1 us
    reduce_scatter x1, waiting for transfers between devices, sum_rows(): lax.psum_scatter(partial_value.astype(jnp.bfloat16), 'tensor', scatter_di...  79.1 us
    unnamed x18, waiting for transfers between devices  73 us
    dot_general x4, matrix products, nn(): return jnp.dot(a, b, preferred_element_type=F32)  47.5 us
    dot_general x4, matrix products, nt(): lax.dot_general(a, b, (((1,), (1,)), ((), ())), preferred_element_type=F32)  41.5 us
    dynamic_update_slice x4, local copies, waits for them, and re-layouts, fast(): lax.scan(backward_block, (empty, empty), jnp.arange(2, dtype=jnp.int32))  41.2 us
  transfers between devices with their start and end apart: 17, of which 13 were waited for; matrix products, arithmetic and copies ran while one was open for 12% of the time, Pallas kernels for 19%

profile of v1, /device:TPU:0, one launch (start us, length us, event | category | flops | bytes accessed | tf_op | source)
XLA Modules:
  0.0 1267.3 jit_solution(307105120361749586)
XLA Ops:
  8.0 32.3 %all-gather.6.cloned.1.call-done = bf16[2048,256]{1,0:T(8,128)(2,1)} async-done(((bf16[512,256]{1,0:T(8,128)(2,1)}), bf16[2048,256]{1,0:T(8,128)(2,1)}) %all-gather.6.cloned.1.call-update) | async-done | bytes 1048592 | tf_op jit(solution)/shard_map/all_gather | solution.py:653
  52.0 243.1 %attention_forward.1 = (bf16[1024,2048]{1,0:T(8,128)(2,1)}, bf16[1024,2048]{1,0:T(8,128)(2,1)}, bf16[1024,2048]{1,0:T(8,128)(2,1)}, bf16[3,4,1024,128]{3,2,1,0:T...) custom-call(bf16[256,2048]{1,0:T(8,128)(2,1)} %tok.1, ...), custom_call_target="tpu_custom_call" | custom-call | flops 199999995904 | bytes 100000000 | tf_op jit(solution)/shard_map/attention_forward/pallas_call | solution.py:289
  296.7 13.2 %fusion.59 = (f32[1024]{0:T(1024)S(1)}, f32[1024,2048]{1,0:T(8,128)S(1)}) fusion(bf16[1024,2048]{1,0:T(8,128)(2,1)} %get-tuple-element.80, bf16[2048,2048]{1,0:T(8,128)(2,1)} %all-gather.8.cloned.1.call-done, bf16[1024,2048]{1,0:T(8,128)(2,1)} %get-tuple-element.79), kind=kOutput, calls=%fused_computation.135 | convolution fusion | flops 8596225024 | bytes 25169920 | tf_op jit(solution)/shard_map/dot_general | solution.py:29
  313.2 5.5 add_convert_fusion.1
  318.7 11.6 fusion.60
  330.3 11.7 fusion.61
  342.0 15.8 %multiply_convert_fusion.1 = (bf16[1024,1408]{1,0:T(8,128)(2,1)S(1)}, bf16[1024,1408]{1,0:T(8,128)(2,1)S(1)}, bf16[1024,1408]{1,0:T(8,128)(2,1)}) fusion(f32[1024,1408]{1,0:T(8,128)} %fusion.60, f32[1024,1408]{1,0:T(8,128)} %fusion.61, bf16[1024,2048]{1,0:T(8,128)(2,1)} %get-tuple-element.82, bf16[1408,2048]{1,0:T(8,128)(2,1)} %all-gather.14.cloned.1.call-done), kind=kOutput, calls=%fused_computation.34 | convolution fusion | flops 5927206912 | bytes 30146560 | tf_op jit(solution)/shard_map/dot_general | solution.py:21
  357.8 10.9 fusion.62
  368.7 8.3 add_convert_fusion
  377.1 75.7 %reduce-scatter.18.cloned.1.call-done = bf16[256,2048]{1,0:T(8,128)(2,1)} async-done(((bf16[1024,2048]{1,0:T(8,128)(2,1)}), bf16[256,2048]{1,0:T(8,128)(2,1)}) %reduce-scatter.18.cloned.1.call-update) | async-done | bytes 1048592 | tf_op jit(solution)/shard_map/reduce_scatter | solution.py:406
  452.8 3.3 fusion.37
  458.7 6.5 convolution_convert_fusion.5
  466.3 4.2 all-to-all-start
  480.3 16.0 %all-to-all-done = bf16[256,4,512]{2,0,1:T(8,128)(2,1)S(1)} async-done(((bf16[256,4,512]{2,0,1:T(8,128)(2,1)}), bf16[256,4,512]{2,0,1:T(8,128)(2,1)S(1)}, u32[]{:S(2)}, u32[]{:S(2)}) %all-to-all-start) | async-done | bytes 1048608 | tf_op jit(solution)/shard_map/all_to_all | solution.py:697
  497.8 136.1 %while.15 = (s32[]{:T(128)}, f32[1024,8,64]{0,2,1:T(8,128)}, f32[1024,8,64]{0,2,1:T(8,128)}, f32[2,512,8,64]{1,0,3,2:T(2,128)}, s32[2]{0:T(128)S(1)}, /*index=5*...) while((s32[]{:T(128)}, f32[1024,8,64]{0,2,1:T(8,128)}, ...), condition=%wide.region_10.11_spmd.clone, body=%wide.region_8.10_spmd.clone.sunk | while | flops 2725507584 | bytes 317804992 | solution.py:728
  500.5 5.9 subtract_exponential_fusion.2
  506.4 10.7 multiply_reduce_fusion.3
  517.3 10.0 multiply_convert_fusion.5
  527.4 6.5 bitcast_add_fusion.4
  536.3 4.3 bitcast_add_fusion.5
  540.6 3.9 fusion.109
  545.6 19.5 %dynamic_update_slice.6 = f32[2,512,8,64]{1,0,3,2:T(2,128)} dynamic-update-slice(f32[2,512,8,64]{1,0,3,2:T(2,128)} %get-tuple-element.378, f32[1,512,8,64]{1,0,3,2:T(1,128)S(1)} %copy.123, s32[]{:T(128)S(6)} %copy.129, s32[]{:T(128)} %constant.80.clone.1..sunk, s32[]{:T(128)} %constant.80.clone.1..sunk, s32[]{:T(128)} %constant.80.clone.1..sunk) | dynamic-update-slice | bytes 2097156 | tf_op jit(solution)/shard_map/while/body/jit(dynamic_update_index_in_dim)/dynamic_update_slice | solution.py:728
  567.5 5.9 subtract_exponential_fusion.2
  573.5 10.7 multiply_reduce_fusion.3
  584.4 10.0 multiply_convert_fusion.5
  594.5 7.0 bitcast_add_fusion.4
  604.0 5.0 bitcast_add_fusion.5
  609.0 3.9 fusion.109
  614.0 19.5 %dynamic_update_slice.6 = f32[2,512,8,64]{1,0,3,2:T(2,128)} dynamic-update-slice(f32[2,512,8,64]{1,0,3,2:T(2,128)} %get-tuple-element.378, f32[1,512,8,64]{1,0,3,2:T(1,128)S(1)} %copy.123, s32[]{:T(128)S(6)} %copy.129, s32[]{:T(128)} %constant.80.clone.1..sunk, s32[]{:T(128)} %constant.80.clone.1..sunk, s32[]{:T(128)} %constant.80.clone.1..sunk) | dynamic-update-slice | bytes 2097156 | tf_op jit(solution)/shard_map/while/body/jit(dynamic_update_index_in_dim)/dynamic_update_slice | solution.py:728
  636.5 4.0 reshape.263
  657.5 11.0 bitcast_convert_fusion
  670.1 6.9 convolution_convert_fusion.3
  677.1 11.0 convolution_convert_fusion.4
  688.2 11.2 convolution_convert_fusion.2
  699.5 11.0 convolution_convert_fusion.1
  710.5 10.4 convolution_convert_fusion
  726.1 18.4 %reduce-scatter.20.cloned.1.call-done = bf16[256,2048]{1,0:T(8,128)(2,1)} async-done(((bf16[1024,2048]{1,0:T(8,128)(2,1)}), bf16[256,2048]{1,0:T(8,128)(2,1)}) %reduce-scatter.20.cloned.1.call-update) | async-done | bytes 1048592 | tf_op jit(solution)/shard_map/reduce_scatter | solution.py:406
  748.3 11.8 convert_bitcast_fusion
  760.1 59.7 %reduce-scatter.24.cloned.1.call-done = bf16[2048,256]{1,0:T(8,128)(2,1)} async-done(((bf16[2048,2048]{1,0:T(8,128)(2,1)}), bf16[2048,256]{1,0:T(8,128)(2,1)}) %reduce-scatter.24.cloned.1.call-update) | async-done | bytes 1048592 | tf_op jit(solution)/shard_map/reduce_scatter | solution.py:688
  819.8 79.1 %reduce-scatter.16.cloned.1.call-done = bf16[256,2048]{1,0:T(8,128)(2,1)} async-done(((bf16[1024,2048]{1,0:T(8,128)(2,1)}), bf16[256,2048]{1,0:T(8,128)(2,1)}) %reduce-scatter.16.cloned.1.call-update) | async-done | bytes 1048592 | tf_op jit(solution)/shard_map/reduce_scatter | solution.py:396
  902.1 59.7 %reduce-scatter.28.cloned.1.call-done = bf16[256,1408]{1,0:T(8,128)(2,1)} async-done(((bf16[2048,1408]{1,0:T(8,128)(2,1)}), bf16[256,1408]{1,0:T(8,128)(2,1)}) %reduce-scatter.28.cloned.1.call-update) | async-done | bytes 720912 | tf_op jit(solution)/shard_map/reduce_scatter | solution.py:688
  964.1 60.6 %reduce-scatter.30.cloned.1.call-done = bf16[256,1408]{1,0:T(8,128)(2,1)} async-done(((bf16[2048,1408]{1,0:T(8,128)(2,1)}), bf16[256,1408]{1,0:T(8,128)(2,1)}) %reduce-scatter.30.cloned.1.call-update) | async-done | bytes 720912 | tf_op jit(solution)/shard_map/reduce_scatter | solution.py:688
  1027.1 60.1 %reduce-scatter.32.cloned.1.call-done = bf16[1408,256]{1,0:T(8,128)(2,1)} async-done(((bf16[1408,2048]{1,0:T(8,128)(2,1)}), bf16[1408,256]{1,0:T(8,128)(2,1)}) %reduce-scatter.32.cloned.1.call-update) | async-done | bytes 720912 | tf_op jit(solution)/shard_map/reduce_scatter | solution.py:688
  1089.4 35.2 %reduce-scatter.34.cloned.1.call-done = f32[64,3]{1,0:T(8,128)} async-done(((f32[512,3]{1,0:T(8,128)}), f32[64,3]{1,0:T(8,128)}) %reduce-scatter.34.cloned.1.call-update) | async-done | bytes 784
  1129.1 35.2 %reduce-scatter.36.cloned.1.call-done = f32[256,4]{1,0:T(8,128)} async-done(((f32[2048,4]{1,0:T(8,128)}), f32[256,4]{1,0:T(8,128)}) %reduce-scatter.36.cloned.1.call-update) | async-done | bytes 4112
  1165.3 11.7 psum.8
  1177.6 51.7 %reduce-scatter.22.cloned.1.call-done = bf16[3,256,512]{1,2,0:T(8,128)(2,1)} async-done(((bf16[3,2048,512]{1,2,0:T(8,128)(2,1)}), bf16[3,256,512]{1,2,0:T(8,128)(2,1)}) %reduce-scatter.22.cloned.1.call-update) | async-done | bytes 786448 | tf_op jit(solution)/shard_map/reduce_scatter | solution.py:688
  1231.8 26.9 %reduce-scatter.26.cloned.1.call-done = bf16[512,256]{1,0:T(8,128)(2,1)} async-done(((bf16[2048,256]{1,0:T(8,128)(2,1)}), bf16[512,256]{1,0:T(8,128)(2,1)}) %reduce-scatter.26.cloned.1.call-update) | async-done | bytes 262160 | tf_op jit(solution)/shard_map/reduce_scatter | solution.py:695
  (206 shorter events, 93.9 us)
Async XLA Ops:
  7.2 35.9 %copy-start = (bf16[256]{0:T(256)(128)(2,1)S(1)}, bf16[256]{0:T(256)(128)(2,1)}, u32[]{:S(2)}) copy-start(bf16[256]{0:T(256)(128)(2,1)} %param.24) | copy-start | bytes 1540
  7.2 33.1 %all-gather.6.cloned.1.call-start = ((), (), s32[]{:S(2)}) async-start(), calls=%async_computation.12 | async-start | bytes 1310720 | tf_op jit(solution)/shard_map/all_gather | solution.py:653
  7.9 288.7 %all-gather.8.cloned.1.call-start = ((), (), s32[]{:S(2)}) async-start(), calls=%async_computation.13 | async-start | bytes 9437184 | tf_op jit(solution)/shard_map/all_gather | solution.py:654
  40.3 278.4 %all-gather.10.cloned.1.call-start = ((), (), s32[]{:S(2)}) async-start(), calls=%async_computation.14 | async-start | bytes 6488064 | tf_op jit(solution)/shard_map/all_gather | solution.py:655
  41.0 289.3 %all-gather.12.cloned.1.call-start = ((), (), s32[]{:S(2)}) async-start(), calls=%async_computation.15 | async-start | bytes 6488064 | tf_op jit(solution)/shard_map/all_gather | solution.py:656
  41.6 300.4 %all-gather.14.cloned.1.call-start = ((), (), s32[]{:S(2)}) async-start(), calls=%async_computation.16 | async-start | bytes 6488064 | tf_op jit(solution)/shard_map/all_gather | solution.py:657
  42.2 410.6 %reduce-scatter.18.cloned.1.call-start = ((), (), s32[]{:S(2)}) async-start(), calls=%async_computation.18 | async-start | bytes 5242880 | tf_op jit(solution)/shard_map/reduce_scatter | solution.py:406
  357.8 10.9 copy-start.26
  357.8 10.9 copy-start.27
  357.8 10.9 copy-start.25
  377.0 79.1 %copy-start.17 = (bf16[256,2048]{1,0:T(8,128)(2,1)S(1)}, bf16[256,2048]{1,0:T(8,128)(2,1)}, u32[]{:S(2)}) copy-start(bf16[256,2048]{1,0:T(8,128)(2,1)} %cot.1) | copy-start | bytes 3145732
  458.7 6.6 copy-start.9
  466.3 30.0 %all-to-all-start = ((bf16[256,4,512]{2,0,1:T(8,128)(2,1)}), bf16[256,4,512]{2,0,1:T(8,128)(2,1)S(1)}, u32[]{:S(2)}, u32[]{:S(2)}) async-start(bf16[256,4,512]{2,0,1:T(8,128)(2,1)} %bitcast.102), calls=%async_computation.2 | async-start | bytes 2097152 | tf_op jit(solution)/shard_map/all_to_all | solution.py:697
  470.5 274.0 %reduce-scatter.20.cloned.1.call-start = ((), (), s32[]{:S(2)}) async-start(), calls=%async_computation.19 | async-start | bytes 5242880 | tf_op jit(solution)/shard_map/reduce_scatter | solution.py:406
  498.0 8.3 copy-start.7
  506.4 11.0 copy-start.2
  517.3 10.0 copy-start.12
  527.4 8.9 copy-start.3
  527.4 13.2 %slice-start = ((s8[8388608]{0:T(1024)(128)(4,1)}), s8[4194304]{0:T(1024)(128)(4,1)S(1)}, s32[]{:S(2)}) async-start(s8[8388608]{0:T(1024)(128)(4,1)} %bitcast.121), calls=%async_computation.28 | async-start | bytes 8388608 | tf_op jit(solution)/shard_map/while
  536.3 4.3 slice-start.1
  544.5 20.6 %copy-start.8 = (bf16[1024,8,64]{0,2,1:T(8,128)(2,1)S(1)}, bf16[1024,8,64]{0,2,1:T(8,128)(2,1)}, u32[]{:S(2)}) copy-start(bf16[1024,8,64]{0,2,1:T(8,128)(2,1)} %copy-done.7) | copy-start | bytes 3145732 | tf_op jit(solution)/shard_map/while
  565.1 8.3 copy-start.7
  573.4 11.0 copy-start.2
  584.4 10.0 copy-start.12
  594.5 9.5 copy-start.3
  594.5 14.5 %slice-start = ((s8[8388608]{0:T(1024)(128)(4,1)}), s8[4194304]{0:T(1024)(128)(4,1)S(1)}, s32[]{:S(2)}) async-start(s8[8388608]{0:T(1024)(128)(4,1)} %bitcast.121), calls=%async_computation.28 | async-start | bytes 8388608 | tf_op jit(solution)/shard_map/while
  604.0 5.0 slice-start.1
  612.9 20.6 %copy-start.8 = (bf16[1024,8,64]{0,2,1:T(8,128)(2,1)S(1)}, bf16[1024,8,64]{0,2,1:T(8,128)(2,1)}, u32[]{:S(2)}) copy-start(bf16[1024,8,64]{0,2,1:T(8,128)(2,1)} %copy-done.7) | copy-start | bytes 3145732 | tf_op jit(solution)/shard_map/while
  633.9 6.6 copy-start.4
  633.9 6.6 copy-start.19
  640.5 4.8 copy-start.5
  642.8 7.6 copy-start.21
  647.9 8.6 copy-start.13
  647.9 3.8 copy-start.16
  652.4 4.2 copy-start.14
  668.6 151.2 %reduce-scatter.24.cloned.1.call-start = ((), (), s32[]{:S(2)}) async-start(), calls=%async_computation.21 | async-start | bytes 9437184 | tf_op jit(solution)/shard_map/reduce_scatter | solution.py:688
  677.1 221.9 %reduce-scatter.16.cloned.1.call-start = ((), (), s32[]{:S(2)}) async-start(), calls=%async_computation.17 | async-start | bytes 5242880 | tf_op jit(solution)/shard_map/reduce_scatter | solution.py:396
  688.1 273.7 %reduce-scatter.28.cloned.1.call-start = ((), (), s32[]{:S(2)}) async-start(), calls=%async_computation.23 | async-start | bytes 6488064 | tf_op jit(solution)/shard_map/reduce_scatter | solution.py:688
  699.4 325.4 %reduce-scatter.30.cloned.1.call-start = ((), (), s32[]{:S(2)}) async-start(), calls=%async_computation.24 | async-start | bytes 6488064 | tf_op jit(solution)/shard_map/reduce_scatter | solution.py:688
  710.5 376.7 %reduce-scatter.32.cloned.1.call-start = ((), (), s32[]{:S(2)}) async-start(), calls=%async_computation.25 | async-start | bytes 6488064 | tf_op jit(solution)/shard_map/reduce_scatter | solution.py:688
  721.0 23.5 %copy-start.22 = (f32[1,2048]{1,0:T(1,128)S(1)}, f32[1,2048]{1,0:T(1,128)}, u32[]{:S(2)}) copy-start(f32[1,2048]{1,0:T(1,128)} %get-tuple-element.277) | copy-start | bytes 24580
  721.0 25.8 %copy-start.23 = (f32[2048]{0:T(1024)S(1)}, f32[2048]{0:T(1024)}, u32[]{:S(2)}) copy-start(f32[2048]{0:T(1024)} %get-tuple-element.235) | copy-start | bytes 24580
  721.0 25.8 %copy-start.24 = (f32[2048]{0:T(1024)S(1)}, f32[2048]{0:T(1024)}, u32[]{:S(2)}) copy-start(f32[2048]{0:T(1024)} %get-tuple-element.242) | copy-start | bytes 24580
  721.0 403.6 %reduce-scatter.34.cloned.1.call-start = ((), (), s32[]{:S(2)}) async-start(), calls=%async_computation.26 | async-start | bytes 294912
  726.1 438.2 %reduce-scatter.36.cloned.1.call-start = ((), (), s32[]{:S(2)}) async-start(), calls=%async_computation.27 | async-start | bytes 1179648
  748.2 481.1 %reduce-scatter.22.cloned.1.call-start = ((), (), s32[]{:S(2)}) async-start(), calls=%async_computation.20 | async-start | bytes 7077888 | tf_op jit(solution)/shard_map/reduce_scatter | solution.py:688
  760.1 498.6 %reduce-scatter.26.cloned.1.call-start = ((), (), s32[]{:S(2)}) async-start(), calls=%async_computation.22 | async-start | bytes 1310720 | tf_op jit(solution)/shard_map/reduce_scatter | solution.py:695
  1126.0 134.5 %copy-start.1 = (bf16[256]{0:T(256)(128)(2,1)S(1)}, bf16[256]{0:T(256)(128)(2,1)}, u32[]{:S(2)}) copy-start(bf16[256]{0:T(256)(128)(2,1)} %param.24) | copy-start | bytes 1540
  (6 other events, 8.3 us)
Sparse Core Ops, SparseCore 0:
  9.6 30.6 all-gather.5
  42.1 87.2 all-gather.7
  131.3 43.3 all-gather.9
  176.5 43.3 all-gather.11
  221.5 44.3 all-gather.13
  377.1 75.6 reduce-scatter.17
  668.7 75.7 reduce-scatter.19
  748.0 71.7 reduce-scatter.23
  822.2 76.7 reduce-scatter.15
  902.3 59.5 reduce-scatter.27
  965.7 59.0 reduce-scatter.29
  1028.1 59.0 reduce-scatter.31
  1091.0 33.5 reduce-scatter.33
  1128.2 36.0 reduce-scatter.35
  1167.5 61.7 reduce-scatter.21
  1231.5 27.1 reduce-scatter.25

commit v2 on v1

--- a/solution.py
+++ b/solution.py
@@ -114,7 +114,7 @@
     tss, trs, css, crs, ass, ars, wss, wrs, mss, mrs, local,
 ):
     rows = tok.shape[0]
-    width = wq.shape[2]
+    width = wq.shape[1] // 3
     pairs = width // 128
     line = 4
     d, z, flips = place()
@@ -124,10 +124,10 @@
     tok_in.start()
     cot_in = pltpu.make_async_copy(cot, cotall.at[pl.ds(z * rows, rows)], local.at[1])
     cot_in.start()
-    depth = wq.shape[1]
+    depth = wq.shape[0]
 
     def wblock(i):
-        return wbuf.at[:, pl.ds(pl.multiple_of(i * depth, 256), depth), :]
+        return wbuf.at[pl.ds(pl.multiple_of(i * depth, 256), depth), :]
 
     w_in = pltpu.make_async_copy(wq, wblock(d), local.at[2])
     w_in.start()
@@ -180,7 +180,8 @@
     def project(s):
         at = pl.ds(pl.multiple_of(s * rows, rows), rows)
         for j in range(3):
-            pre = nn(n1buf[at, :], wbuf[j]) + small_sum[4 + j : 5 + j, :width]
+            cols = pl.ds(j * width, width)
+            pre = nn(n1buf[at, :], wbuf[:, cols]) + small_sum[4:5, cols]
             for p in range(pairs):
                 part = pre[:, p * 128 : (p + 1) * 128]
                 if j < 2:
@@ -282,7 +283,8 @@
     rows, model = tok.shape
     line = 4
     length = rows * line
-    _, depth, width = wq.shape
+    depth, width = wq.shape
+    width //= 3
     pairs = width // 128
     dp = model // depth
     sds = jax.ShapeDtypeStruct
@@ -291,14 +293,14 @@
         out_shape=(
             sds((length, model), BF), sds((length, model), BF), sds((length, model), BF),
             sds((3, pairs, length, 128), BF), sds((length, 128), F32), sds((length, model), BF),
-            sds((3, model, width), BF), sds((16, model), F32),
+            sds((model, 3 * width), BF), sds((16, model), F32),
         ),
         in_specs=[ANY, ANY, ANY, INV, INV, INV, INV],
         out_specs=(ANY, ANY, ANY, ANY, INV, ANY, ANY, INV),
         scratch_shapes=[
             pltpu.VMEM((line, rows, model), BF),
             pltpu.VMEM((length, model), BF),
-            pltpu.VMEM((3, model, width), BF),
+            pltpu.VMEM((model, 3 * width), BF),
             pltpu.VMEM((3, pairs, length, 128), BF),
             pltpu.VMEM((pairs, length, 128), BF),
             pltpu.VMEM((dp, 16, model), BF),
@@ -614,6 +616,770 @@
     )
 
 
+class LineScatter:
+    def __init__(self, part, slot, chunks, d, z, line, send_sems, recv_sems):
+        self.part, self.slot, self.chunks, self.d, self.z, self.line = part, slot, chunks, d, z, line
+        self.ss, self.rs = send_sems, recv_sems
+
+    def copy(self, s, h, way, target, place):
+        return send(
+            self.part(s, h), self.slot(place, h), self.ss.at[s, h], self.rs.at[place, h], self.d, target
+        )
+
+    def right(self, s, h):
+        return self.copy(s, h, 0, self.z + 1, s)
+
+    def left(self, s, h):
+        return self.copy(s, h, 1, self.z - 1, jnp.where(self.z - 1 == s, self.line, s))
+
+    def head(self, s):
+        z, line = self.z, self.line
+        for h in range(self.chunks):
+            pl.when((z == 0) & (s > 0))(lambda: self.right(s, h).start())
+            pl.when((z == line - 1) & (s < z))(lambda: self.left(s, h).start())
+
+    def add(self, s, h):
+        part = self.part(s, h)
+        part[...] = (part[...].astype(F32) + self.slot(s, h)[...].astype(F32)).astype(BF)
+
+    def relay(self, t):
+        z, line = self.z, self.line
+        up = line - 1 - t + z
+        down = t - (line - 1 - z)
+        for h in range(self.chunks):
+            @pl.when((z > 0) & (up > z) & (up < line))
+            def _():
+                self.copy(z, h, 0, z, up).wait_recv()
+                self.add(up, h)
+                self.right(up, h).start()
+
+            @pl.when((z < line - 1) & (down >= 0) & (down < z))
+            def _():
+                self.copy(z, h, 0, z, down).wait_recv()
+                self.add(down, h)
+                self.left(down, h).start()
+
+    def arrive(self, h):
+        z, line = self.z, self.line
+        pl.when(z > 0)(lambda: self.copy(z, h, 0, z, z).wait_recv())
+        pl.when(z < line - 1)(lambda: self.copy(z, h, 0, z, line).wait_recv())
+
+    def total(self, h, rows):
+        z = self.z
+        return (
+            self.part(z, h)[rows].astype(F32)
+            + self.slot(z, h)[rows].astype(F32)
+            + self.slot(self.line, h)[rows].astype(F32)
+        )
+
+    def finish(self):
+        z = self.z
+        for s in range(self.line):
+            for h in range(self.chunks):
+                pl.when(z != s)(lambda: self.copy(s, h, 0, z, s).wait_send())
+
+
+def far_first(z, i):
+    orders = ((3, 2, 1, 0), (3, 0, 2, 1), (0, 3, 1, 2), (0, 1, 2, 3))
+    codes = [sum(s * 4**j for j, s in enumerate(o)) for o in orders]
+    code = jnp.where(
+        z == 0, codes[0], jnp.where(z == 1, codes[1], jnp.where(z == 2, codes[2], codes[3]))
+    )
+    power = jnp.where(i == 0, 1, jnp.where(i == 1, 4, jnp.where(i == 2, 16, 64)))
+    return lax.rem(lax.div(code, power), 4)
+
+
+def spans(total, step):
+    return [(i, min(step, total - i)) for i in range(0, total, step)]
+
+
+def mlp_kernel(
+    n2, cot, wgate, wup, wdown,
+    dn2, mixed, gex, uex, dex, ghalf, uhalf, dhalf, grecv,
+    nbuf, cbuf, gw, uw, dw, act, act_t, dga, dup, part, slots, mixbuf, wide, tall, wide_in, tall_in,
+    ss, rs, local, mixsem, outsem, exs, exr, gss, grs,
+):
+    line = 4
+    rows = n2.shape[0] // line
+    model = n2.shape[1]
+    hidden = wgate.shape[1]
+    d, z, flips = place()
+    greet(d, z, flips, line, (1, 2, 4, 6))
+    core = lax.rem(d, 2)
+    chip = lax.div(d, 2)
+    loads = [
+        pltpu.make_async_copy(a, b, local.at[i])
+        for i, (a, b) in enumerate(((n2, nbuf), (wgate, gw), (wup, uw), (cot, cbuf), (wdown, dw)))
+    ]
+    for copy in loads:
+        copy.start()
+    half = rows // 2
+    scatter = LineScatter(
+        lambda s, h: part.at[s, pl.ds(h * half, half)],
+        lambda i, h: slots.at[i, pl.ds(h * half, half)],
+        2, d, z, line, ss, rs,
+    )
+    pl.when(z == 0)(lambda: slots.__setitem__((0,), jnp.zeros((rows, model), BF)))
+    pl.when(z == line - 1)(lambda: slots.__setitem__((line,), jnp.zeros((rows, model), BF)))
+    for copy in loads:
+        copy.wait()
+
+    @pl.loop(0, line)
+    def _(i):
+        s = far_first(z, i)
+        at = pl.ds(pl.multiple_of(s * rows, rows), rows)
+        for lo, size in spans(hidden, 512):
+            cols = pl.ds(lo, size)
+            gate = nn(nbuf[at, :], gw[:, cols])
+            up = nn(nbuf[at, :], uw[:, cols])
+            dact = nt(cbuf[at, :], dw[cols, :])
+            sigma = lax.logistic(gate)
+            silu = gate * sigma
+            act[at, cols] = (silu * up).astype(BF)
+            dga[at, cols] = (dact * up * (sigma * (1.0 + gate * (1.0 - sigma)))).astype(BF)
+            dup[at, cols] = (dact * silu).astype(BF)
+        for lo, size in spans(model, 512):
+            cols = pl.ds(lo, size)
+            part[s, :, cols] = (nt(dga[at, :], gw[cols, :]) + nt(dup[at, :], uw[cols, :])).astype(BF)
+        scatter.head(s)
+
+    scatter.relay(1)
+    blocks = model // rows // 2
+
+    def exchanged(m):
+        outs = (ghalf, uhalf, dhalf)
+        exes = (gex, uex, dex)
+        stage = tall if m == 2 else wide
+        stage_in = tall_in if m == 2 else wide_in
+
+        def block(t):
+            cols = pl.ds(pl.multiple_of(t * rows, rows), rows)
+            if m == 2:
+                return lambda lo, size: nn(act_t[pl.ds(lo, size), :], cbuf[:, cols])
+            right = dga if m == 0 else dup
+            return lambda lo, size: tn(nbuf[:, cols], right[:, pl.ds(lo, size)])
+
+        def piece(ref, lo, size):
+            return ref.at[pl.ds(lo, size), :] if m == 2 else ref.at[:, pl.ds(lo, size)]
+
+        def away(k):
+            slot = lax.rem(k, 2)
+            return send(stage.at[slot], exes[m].at[k], exs.at[m, k], exr.at[m, k], d + flips[1], z)
+
+        @pl.loop(0, blocks)
+        def _(k):
+            slot = lax.rem(k, 2)
+            pl.when(k >= 2)(lambda: away(k - 2).wait_send())
+            make = block(2 * k + 1 - core)
+            for lo, size in spans(hidden, 512):
+                piece(stage.at[slot], lo, size)[...] = make(lo, size).astype(BF)
+            away(k).start()
+
+        away(blocks - 2).wait_send()
+        away(blocks - 1).wait_send()
+
+        def chip_at(j):
+            return lax.rem(chip + 1 + j, blocks)
+
+        def store(j):
+            slot = lax.rem(j, 2)
+            return pltpu.make_async_copy(stage.at[slot], outs[m].at[chip_at(j)], outsem.at[slot])
+
+        def onward(j):
+            k = chip_at(j)
+            return send(ghalf.at[k], grecv.at[blocks - 2 - j], gss.at[j], grs.at[blocks - 2 - j], 2 * k + core, z)
+
+        @pl.loop(0, blocks)
+        def _(j):
+            slot = lax.rem(j, 2)
+            k = chip_at(j)
+
+            @pl.when(j >= 2)
+            def _():
+                store(j - 2).wait()
+                if m == 0:
+                    onward(j - 2).start()
+
+            away(k).wait_recv()
+            fetch = pltpu.make_async_copy(exes[m].at[k], stage_in, local.at[5])
+            fetch.start()
+            fetch.wait()
+            make = block(2 * k + core)
+            for lo, size in spans(hidden, 512):
+                piece(stage.at[slot], lo, size)[...] = (
+                    make(lo, size) + piece(stage_in, lo, size)[...].astype(F32)
+                ).astype(BF)
+            store(j).start()
+
+        for j in (blocks - 2, blocks - 1):
+            store(j).wait()
+            if m == 0 and j < blocks - 1:
+                onward(j).start()
+        return onward
+
+    onward = exchanged(0)
+
+    def mixed_out(i):
+        cols = pl.ds(pl.multiple_of(i * 512, 512), 512)
+        return pltpu.make_async_copy(mixbuf.at[lax.rem(i, 2)], mixed.at[:, cols], mixsem.at[lax.rem(i, 2)])
+
+    @pl.loop(0, line)
+    def _(s):
+        at = pl.ds(pl.multiple_of(s * rows, rows), rows)
+        for lo, size in spans(hidden, 512):
+            act_t[pl.ds(lo, size), at] = act[at, pl.ds(lo, size)].T
+
+    @pl.loop(0, model // 512)
+    def _(i):
+        pl.when(i >= 2)(lambda: mixed_out(i - 2).wait())
+        cols = pl.ds(pl.multiple_of(i * 512, 512), 512)
+        for s in range(line):
+            at = pl.ds(s * rows, rows)
+            mixbuf[lax.rem(i, 2), at, :] = nn(act[at, :], dw[:, cols]).astype(BF)
+        mixed_out(i).start()
+
+    scatter.relay(2)
+    exchanged(1)
+    exchanged(2)
+    for h in range(2):
+        scatter.arrive(h)
+
+        @pl.loop(0, half // 32)
+        def _(i):
+            rows_at = pl.ds(pl.multiple_of(i * 32, 32), 32)
+            dn2[pl.ds(pl.multiple_of(h * half + i * 32, 32), 32), :] = scatter.total(h, rows_at)
+
+    scatter.finish()
+    for i in (model // 512 - 2, model // 512 - 1):
+        mixed_out(i).wait()
+    for j in range(blocks - 1):
+        onward(j).wait()
+
+
+def mlp(n2, cot, wgate, wup, wdown):
+    length, model = n2.shape
+    hidden = wgate.shape[1]
+    line = 4
+    rows = length // line
+    blocks = model // rows // 2
+    sds = jax.ShapeDtypeStruct
+    wide = sds((blocks, rows, hidden), BF)
+    tall = sds((blocks, hidden, rows), BF)
+    return pl.pallas_call(
+        mlp_kernel,
+        out_shape=(
+            sds((rows, model), F32), sds((length, model), BF),
+            wide, wide, tall, wide, wide, tall, sds((blocks - 1, rows, hidden), BF),
+        ),
+        in_specs=[ANY] * 5,
+        out_specs=(INV,) + (ANY,) * 8,
+        scratch_shapes=[
+            pltpu.VMEM((length, model), BF),
+            pltpu.VMEM((length, model), BF),
+            pltpu.VMEM((model, hidden), BF),
+            pltpu.VMEM((model, hidden), BF),
+            pltpu.VMEM((hidden, model), BF),
+            pltpu.VMEM((length, hidden), BF),
+            pltpu.VMEM((hidden, length), BF),
+            pltpu.VMEM((length, hidden), BF),
+            pltpu.VMEM((length, hidden), BF),
+            pltpu.VMEM((line, rows, model), BF),
+            pltpu.VMEM((line + 1, rows, model), BF),
+            pltpu.VMEM((2, length, 512), BF),
+            pltpu.VMEM((2, rows, hidden), BF),
+            pltpu.VMEM((2, hidden, rows), BF),
+            pltpu.VMEM((rows, hidden), BF),
+            pltpu.VMEM((hidden, rows), BF),
+            pltpu.SemaphoreType.DMA((line, 2)),
+            pltpu.SemaphoreType.DMA((line + 1, 2)),
+            pltpu.SemaphoreType.DMA((6,)),
+            pltpu.SemaphoreType.DMA((2,)),
+            pltpu.SemaphoreType.DMA((2,)),
+            pltpu.SemaphoreType.DMA((3, blocks)),
+            pltpu.SemaphoreType.DMA((3, blocks)),
+            pltpu.SemaphoreType.DMA((blocks,)),
+            pltpu.SemaphoreType.DMA((blocks,)),
+        ],
+        compiler_params=pltpu.CompilerParams(
+            collective_id=2, has_side_effects=True, vmem_limit_bytes=62 * 1024 * 1024
+        ),
+        cost_estimate=pl.CostEstimate(flops=10**11, bytes_accessed=10**8, transcendentals=0),
+        name="mlp",
+    )(n2, cot, wgate, wup, wdown)
+
+
+def norm_parts(x):
+    centred = x - jnp.mean(x, -1, keepdims=True)
+    inverse = lax.rsqrt(jnp.mean(centred * centred, -1, keepdims=True) + 1e-05)
+    return centred * inverse, inverse
+
+
+def norm_back(grad, standard, inverse, gain):
+    scaled = grad * gain
+    return inverse * (
+        scaled
+        - jnp.mean(scaled, -1, keepdims=True)
+        - standard * jnp.mean(scaled * standard, -1, keepdims=True)
+    )
+
+
+def each_piece(rows, piece, body):
+    @pl.loop(0, rows // piece)
+    def _(i):
+        body(pl.ds(pl.multiple_of(i * piece, piece), piece))
+
+
+class PlaneSum:
+    def __init__(self, half, recv, d, z, blocks, send_sems, recv_sems):
+        self.half, self.recv, self.d, self.z, self.blocks = half, recv, d, z, blocks
+        self.ss, self.rs = send_sems, recv_sems
+        self.chip, self.core = lax.div(d, 2), lax.rem(d, 2)
+
+    def chip_at(self, j):
+        return lax.rem(self.chip + 1 + j, self.blocks)
+
+    def copy(self, j):
+        k, to = self.chip_at(j), self.blocks - 2 - j
+        return send(self.half.at[k], self.recv.at[to], self.ss.at[j], self.rs.at[to], 2 * k + self.core, self.z)
+
+    def wait(self):
+        for j in range(self.blocks - 1):
+            self.copy(j).wait()
+
+
+def sum_blocks(own, recv, out, buf, obuf, sems, pieces):
+    count = recv.shape[0]
+    rows = buf.shape[1]
+
+    @pl.loop(0, pieces)
+    def _(i):
+        at = pl.ds(pl.multiple_of(i * rows, rows), rows)
+        ins = [pltpu.make_async_copy(own.at[at], buf.at[0], sems.at[0])] + [
+            pltpu.make_async_copy(recv.at[j, at], buf.at[j + 1], sems.at[j + 1]) for j in range(count)
+        ]
+        for copy in ins:
+            copy.start()
+        for copy in ins:
+            copy.wait()
+        total = buf[0].astype(F32)
+        for j in range(count):
+            total = total + buf[j + 1].astype(F32)
+        obuf[...] = total
+        back = pltpu.make_async_copy(obuf, out.at[at], sems.at[count + 1])
+        back.start()
+        back.wait()
+
+
+def attention_back_kernel(
+    dn2, hid, cot, small, wout, attall, qkv, lse, mixed, ghalf, grecv, uhalf, cos, sin_up, sin_down,
+    lay, dhid, dpre, ograd, ggrad, ugrad, sums, urecv, oex,
+    wo, da, attr, att_t, attc, qbuf, dsend, datt, lse_t, part, slots, ostage, ofetch, osum, orecv, ofull, ozr,
+    sbuf, sobuf, dq,
+    mss, mrs, ass, ars, oss, ors, pss, prs, uss, urs, zss, zrs, local, ssem,
+):
+    line = 4
+    rows, model = hid.shape
+    length = rows * line
+    width = attc.shape[1]
+    pairs = width // 128
+    blocks = model // rows // 2
+    d, z, flips = place()
+    greet(d, z, flips, line, (1, 2, 4, 6))
+    core, chip = lax.rem(d, 2), lax.div(d, 2)
+    ups = PlaneSum(uhalf, urecv, d, z, blocks, uss, urs)
+    loads = [pltpu.make_async_copy(mixed.at[pl.ds(s * rows, rows)], part.at[s], local.at[s]) for s in range(line)]
+    loads += [
+        pltpu.make_async_copy(wout, wo, local.at[4]),
+        pltpu.make_async_copy(attall.at[pl.ds(pl.multiple_of(z * rows, rows), rows)], attr, local.at[5]),
+        pltpu.make_async_copy(attall.at[:, pl.ds(pl.multiple_of(z * width, width), width)], attc, local.at[6]),
+        pltpu.make_async_copy(qkv, qbuf, local.at[7]),
+    ]
+    for copy in loads:
+        copy.start()
+    for j in range(blocks - 1):
+        ups.copy(j).start()
+    half = rows // 2
+    scatter = LineScatter(
+        lambda s, h: part.at[s, pl.ds(h * half, half)],
+        lambda i, h: slots.at[i, pl.ds(h * half, half)],
+        2, d, z, line, mss, mrs,
+    )
+    pl.when(z == 0)(lambda: slots.__setitem__((0,), jnp.zeros((rows, model), BF)))
+    pl.when(z == line - 1)(lambda: slots.__setitem__((line,), jnp.zeros((rows, model), BF)))
+    for copy in loads[:4]:
+        copy.wait()
+    for i in range(line - 1):
+        pl.when(z == 0)(lambda: scatter.head(jnp.int32(line - 1 - i)))
+        pl.when(z == line - 1)(lambda: scatter.head(jnp.int32(i)))
+
+    sums[...] = jnp.zeros_like(sums)
+
+    def back(at):
+        grad = dn2[at, :]
+        standard, inverse = norm_parts(hid[at, :])
+        sums[2:3, :] += jnp.sum(grad * standard, 0, keepdims=True)
+        sums[3:4, :] += jnp.sum(grad, 0, keepdims=True)
+        total = cot[at, :].astype(F32) + norm_back(grad, standard, inverse, small[2:3, :])
+        dhid[at, :] = total
+        da[at, :] = total.astype(BF)
+
+    each_piece(rows, 32, back)
+    for copy in loads[4:]:
+        copy.wait()
+
+    def away(k):
+        to = lax.rem(z + k, line)
+        return send(
+            dsend.at[to], datt.at[pl.ds(pl.multiple_of(z * rows, rows), rows)], ass.at[k], ars.at[z], d, to
+        )
+
+    @pl.loop(1, line + 1)
+    def _(k):
+        to = lax.rem(z + k, line)
+        dsend[to] = nt(da[...], wo[pl.ds(pl.multiple_of(to * width, width), width), :]).astype(BF)
+        pl.when(k < line)(lambda: away(k).start())
+
+    datt[pl.ds(pl.multiple_of(z * rows, rows), rows), :] = dsend[z]
+    for lo, size in spans(model, 512):
+        att_t[pl.ds(lo, size), :] = attr[:, pl.ds(lo, size)].T
+    lse_t[...] = lse[...].T
+
+    def oblock(t):
+        return nn(att_t[...], da[:, pl.ds(pl.multiple_of(t * rows, rows), rows)])
+
+    def across(k):
+        return send(ostage.at[lax.rem(k, 2)], oex.at[k], oss.at[k], ors.at[k], d + flips[1], z)
+
+    @pl.loop(0, blocks)
+    def _(k):
+        pl.when(k >= 2)(lambda: across(k - 2).wait_send())
+        ostage[lax.rem(k, 2)] = oblock(2 * k + 1 - core).astype(BF)
+        across(k).start()
+
+    planes = PlaneSum(osum, orecv, d, z, blocks, pss, prs)
+
+    @pl.loop(0, blocks)
+    def _(j):
+        k = planes.chip_at(j)
+        across(k).wait_recv()
+        fetch = pltpu.make_async_copy(oex.at[k], ofetch, local.at[8])
+        fetch.start()
+        fetch.wait()
+        osum[k] = (oblock(2 * k + core) + ofetch[...].astype(F32)).astype(BF)
+        pl.when(j < blocks - 1)(lambda: planes.copy(j).start())
+
+    across(blocks - 2).wait_send()
+    across(blocks - 1).wait_send()
+    sum_blocks(ghalf.at[chip], grecv, ggrad, sbuf, sobuf, ssem, rows // sbuf.shape[1])
+    for k in range(1, line):
+        frm = lax.rem(z + k, line)
+        send(dsend.at[frm], datt.at[pl.ds(pl.multiple_of(frm * rows, rows), rows)], ass.at[k], ars.at[frm], d, frm).wait_recv()
+
+    scatter.relay(1)
+    lanes = lax.broadcasted_iota(jnp.int32, (1, 128), 1)
+    mine = (lanes < 64, lanes >= 64)
+    which = lax.broadcasted_iota(jnp.int32, (16, 128), 0)
+    lane16 = lax.broadcasted_iota(jnp.int32, (16, 128), 1)
+    pick = jnp.where(which == lax.div(lane16, 64), 1.0, 0.0).astype(BF)
+    scale = HEAD_DIM**-0.5
+
+    def zaway(k):
+        to = lax.rem(z + k, line)
+        return send(
+            ofull.at[pl.ds(pl.multiple_of(to * width, width), width)], ozr.at[k - 1], zss.at[k], zrs.at[k - 1], d, to
+        )
+
+    def plane_total():
+        planes.wait()
+
+        def add(at):
+            total = osum[chip, at, :].astype(F32)
+            for j in range(blocks - 1):
+                total = total + orecv[j, at, :].astype(F32)
+            ofull[at, :] = total.astype(BF)
+
+        each_piece(model, 256, add)
+        for k in range(1, line):
+            zaway(k).start()
+
+    def back_pair(p):
+        cols = pl.ds(pl.multiple_of(p * 128, 128), 128)
+        do = datt[:, cols]
+        prod = do.astype(F32) * attc[:, cols].astype(F32)
+        high = prod.astype(BF)
+        inner = nt(pick, high) + nt(pick, (prod - high.astype(F32)).astype(BF))
+        q = qbuf[0, p] * BF(scale)
+        dq[...] = jnp.zeros_like(dq)
+        for kj in range(line):
+            at = pl.ds(kj * rows, rows)
+            lo, count = kj * rows, length - kj * rows
+            k, v = qbuf[1, p, at, :], qbuf[2, p, at, :]
+            row = lax.broadcasted_iota(jnp.int32, (rows, count), 0)
+            col = lax.broadcasted_iota(jnp.int32, (rows, count), 1)
+            keep = col >= row
+            dk = jnp.zeros((rows, 128), F32)
+            dv = jnp.zeros((rows, 128), F32)
+            for a in range(2):
+                km, vm = jnp.where(mine[a], k, BF(0)), jnp.where(mine[a], v, BF(0))
+                qm, dm = jnp.where(mine[a], q[lo:], BF(0)), jnp.where(mine[a], do[lo:], BF(0))
+                s = jnp.where(keep, nt(km, q[lo:]), -1e30)
+                probs = jnp.exp(s - lse_t[pl.ds(2 * p + a, 1), pl.ds(lo, count)])
+                dv += nn(probs.astype(BF), dm)
+                dprobs = nt(vm, do[lo:])
+                ds = (probs * (dprobs - inner[a : a + 1, lo:])).astype(BF)
+                dk += nn(ds, qm)
+                dq[pl.ds(lo, count), :] += tn(ds, km)
+            dk = turn(dk, cos[at, :], sin_up[at, :], sin_down[at, :], -1.0)
+            dpre[at, pl.ds(pl.multiple_of(width + p * 128, 128), 128)] = dk.astype(BF)
+            dpre[at, pl.ds(pl.multiple_of(2 * width + p * 128, 128), 128)] = dv.astype(BF)
+        dpre[:, cols] = turn(dq[...] * scale, cos[...], sin_up[...], sin_down[...], -1.0).astype(BF)
+
+    @pl.loop(0, pairs)
+    def _(p):
+        back_pair(p)
+        pl.when(p == 1)(lambda: scatter.relay(2))
+
+    plane_total()
+    ups.wait()
+    sum_blocks(uhalf.at[chip], urecv, ugrad, sbuf, sobuf, ssem, rows // sbuf.shape[1])
+    for h in range(2):
+        scatter.arrive(h)
+
+        @pl.loop(0, half // 32)
+        def _(i):
+            at = pl.ds(pl.multiple_of(h * half + i * 32, 32), 32)
+            total = scatter.total(h, pl.ds(pl.multiple_of(i * 32, 32), 32))
+            lay[at, :] = (hid[at, :] + total).astype(BF)
+
+    total = ofull[pl.ds(pl.multiple_of(z * width, width), width), :].astype(F32)
+    for k in range(1, line):
+        zaway(k).wait()
+        total = total + ozr[k - 1].astype(F32)
+    ograd[...] = total
+    for k in range(1, line):
+        away(k).wait_send()
+    scatter.finish()
+
+
+def attention_backward(dn2, hid, cot, small, wout, attall, qkv, lse, mixed, ghalf, grecv, uhalf, tabs):
+    rows, model = hid.shape
+    line = 4
+    length = rows * line
+    width = model // line
+    pairs = width // 128
+    blocks = model // rows // 2
+    hidden = ghalf.shape[2]
+    sds = jax.ShapeDtypeStruct
+    dma = pltpu.SemaphoreType.DMA
+    return pl.pallas_call(
+        attention_back_kernel,
+        out_shape=(
+            sds((rows, model), BF), sds((rows, model), F32), sds((length, 3 * width), BF),
+            sds((width, rows), F32), sds((rows, hidden), F32), sds((rows, hidden), F32), sds((8, model), F32),
+            sds((blocks - 1, rows, hidden), BF), sds((blocks, model, rows), BF),
+        ),
+        in_specs=[INV, INV, INV, INV, ANY, ANY, ANY, INV, ANY, ANY, ANY, ANY, INV, INV, INV],
+        out_specs=(INV, INV, INV, INV, ANY, ANY, INV, ANY, ANY),
+        scratch_shapes=[
+            pltpu.VMEM((model, model), BF),
+            pltpu.VMEM((rows, model), BF),
+            pltpu.VMEM((rows, model), BF),
+            pltpu.VMEM((model, rows), BF),
+            pltpu.VMEM((length, width), BF),
+            pltpu.VMEM((3, pairs, length, 128), BF),
+            pltpu.VMEM((line, rows, width), BF),
+            pltpu.VMEM((length, width), BF),
+            pltpu.VMEM((128, length), F32),
+            pltpu.VMEM((line, rows, model), BF),
+            pltpu.VMEM((line + 1, rows, model), BF),
+            pltpu.VMEM((2, model, rows), BF),
+            pltpu.VMEM((model, rows), BF),
+            pltpu.VMEM((blocks, model, rows), BF),
+            pltpu.VMEM((blocks - 1, model, rows), BF),
+            pltpu.VMEM((model, rows), BF),
+            pltpu.VMEM((line - 1, width, rows), BF),
+            pltpu.VMEM((blocks, 64, hidden), BF),
+            pltpu.VMEM((64, hidden), F32),
+            pltpu.VMEM((length, 128), F32),
+            dma((line, 2)), dma((line + 1, 2)), dma((line,)), dma((line,)), dma((blocks,)), dma((blocks,)),
+            dma((blocks,)), dma((blocks,)), dma((blocks,)), dma((blocks,)), dma((line,)), dma((line,)),
+            dma((10,)), dma((blocks + 1,)),
+        ],
+        compiler_params=pltpu.CompilerParams(
+            collective_id=3, has_side_effects=True, vmem_limit_bytes=62 * 1024 * 1024
+        ),
+        cost_estimate=pl.CostEstimate(flops=10**11, bytes_accessed=10**8, transcendentals=0),
+        name="attention_backward",
+    )(dn2, hid, cot, small, wout, attall, qkv, lse, mixed, ghalf, grecv, uhalf, *tabs)
+
+
+def input_back_kernel(
+    dpre, wqkv, n1, dhalf, tok, dhid, small, sums_in,
+    tgrad, qgrad, dgrad, sums, drecv, qex,
+    pbuf, wbuf, nbuf, part, slots, qstage, qfetch, qsum, qrecv, zsums, dsums, sbuf, sobuf,
+    ss, rs, xss, xrs, pss, prs, dss, drs, zss, zrs, gss, grs, local, ssem,
+):
+    line = 4
+    rows, model = tok.shape
+    width = dpre.shape[1] // 3
+    blocks = model // rows // 2
+    d, z, flips = place()
+    greet(d, z, flips, line, range(1, 8))
+    core, chip = lax.rem(d, 2), lax.div(d, 2)
+    loads = [
+        pltpu.make_async_copy(a, b, local.at[i]) for i, (a, b) in enumerate(((dpre, pbuf), (wqkv, wbuf), (n1, nbuf)))
+    ]
+    for copy in loads:
+        copy.start()
+    downs = PlaneSum(dhalf, drecv, d, z, blocks, dss, drs)
+    half = rows // 2
+    scatter = LineScatter(
+        lambda s, h: part.at[s, pl.ds(h * half, half)],
+        lambda i, h: slots.at[i, pl.ds(h * half, half)],
+        2, d, z, line, ss, rs,
+    )
+    pl.when(z == 0)(lambda: slots.__setitem__((0,), jnp.zeros((rows, model), BF)))
+    pl.when(z == line - 1)(lambda: slots.__setitem__((line,), jnp.zeros((rows, model), BF)))
+    for copy in loads[:2]:
+        copy.wait()
+
+    @pl.loop(0, line)
+    def _(i):
+        s = far_first(z, i)
+        at = pl.ds(pl.multiple_of(s * rows, rows), rows)
+        for lo, size in spans(model, 512):
+            part[s, :, pl.ds(lo, size)] = nt(pbuf[at, :], wbuf[pl.ds(lo, size), :]).astype(BF)
+        scatter.head(s)
+
+    loads[2].wait()
+    sums[...] = sums_in[...]
+
+    def bias(at):
+        sums[4:5, : 3 * width] += jnp.sum(pbuf[at, :].astype(F32), 0, keepdims=True)
+
+    each_piece(rows * line, 64, bias)
+
+    def qblock(t):
+        return lambda lo, size: tn(nbuf[:, pl.ds(pl.multiple_of(t * rows, rows), rows)], pbuf[:, pl.ds(lo, size)])
+
+    def across(k):
+        return send(qstage.at[k], qex.at[k], xss.at[k], xrs.at[k], d + flips[1], z)
+
+    @pl.loop(0, blocks)
+    def _(k):
+        make = qblock(2 * k + 1 - core)
+        for lo, size in spans(3 * width, 512):
+            qstage[k, :, pl.ds(lo, size)] = make(lo, size).astype(BF)
+        across(k).start()
+
+    scatter.relay(1)
+    planes = PlaneSum(qsum, qrecv, d, z, blocks, pss, prs)
+
+    @pl.loop(0, blocks)
+    def _(j):
+        k = planes.chip_at(j)
+        across(k).wait_recv()
+        fetch = pltpu.make_async_copy(qex.at[k], qfetch, local.at[3])
+        fetch.start()
+        fetch.wait()
+        make = qblock(2 * k + core)
+        for lo, size in spans(3 * width, 512):
+            qsum[k, :, pl.ds(lo, size)] = (make(lo, size) + qfetch[:, pl.ds(lo, size)].astype(F32)).astype(BF)
+        pl.when(j < blocks - 1)(lambda: planes.copy(j).start())
+
+    for j in range(blocks - 1):
+        downs.copy(j).start()
+    scatter.relay(2)
+    planes.wait()
+    for j in range(3):
+        cols = pl.ds(j * width, width)
+        total = qsum[chip, :, cols].astype(F32)
+        for i in range(blocks - 1):
+            total = total + qrecv[i, :, cols].astype(F32)
+        qgrad[j] = total
+    downs.wait()
+    sum_blocks(dhalf.at[chip], drecv, dgrad, sbuf, sobuf, ssem, dhalf.shape[1] // sbuf.shape[1])
+    for h in range(2):
+        scatter.arrive(h)
+
+        @pl.loop(0, half // 32)
+        def _(i):
+            at = pl.ds(pl.multiple_of(h * half + i * 32, 32), 32)
+            grad = scatter.total(h, pl.ds(pl.multiple_of(i * 32, 32), 32))
+            standard, inverse = norm_parts(tok[at, :].astype(F32))
+            sums[0:1, :] += jnp.sum(grad * standard, 0, keepdims=True)
+            sums[1:2, :] += jnp.sum(grad, 0, keepdims=True)
+            tgrad[at, :] = (dhid[at, :] + norm_back(grad, standard, inverse, small[0:1, :])).astype(BF)
+
+    def zcopy(k):
+        to = lax.rem(z + k, line)
+        return send(sums, zsums.at[k - 1], zss.at[k], zrs.at[k - 1], d, to)
+
+    def dcopy(r):
+        return send(dsums.at[0], dsums.at[r], gss.at[r], grs.at[r], d + flips[r], z)
+
+    for k in range(1, line):
+        zcopy(k).start()
+    for k in range(1, line):
+        zcopy(k).wait()
+    dsums[0] = sums[...]
+    dsums[0, 0:4, :] = sums[0:4, :] + zsums[0, 0:4, :] + zsums[1, 0:4, :] + zsums[2, 0:4, :]
+    for r in range(1, 8):
+        dcopy(r).start()
+    for r in range(1, 8):
+        dcopy(r).wait()
+    total = dsums[0]
+    for r in range(1, 8):
+        total = total + dsums[r]
+    sums[...] = total
+    for k in range(blocks):
+        across(k).wait_send()
+    scatter.finish()
+
+
+def input_backward(dpre, wqkv, n1, dhalf, tok, dhid, small, sums):
+    rows, model = tok.shape
+    line = 4
+    length = rows * line
+    triple = dpre.shape[1]
+    blocks = model // rows // 2
+    hidden = dhalf.shape[1]
+    sds = jax.ShapeDtypeStruct
+    dma = pltpu.SemaphoreType.DMA
+    return pl.pallas_call(
+        input_back_kernel,
+        out_shape=(
+            sds((rows, model), BF), sds((3, rows, triple // 3), F32), sds((hidden, rows), F32), sds((8, model), F32),
+            sds((blocks - 1, hidden, rows), BF), sds((blocks, rows, triple), BF),
+        ),
+        in_specs=[ANY, ANY, ANY, ANY, INV, INV, INV, INV],
+        out_specs=(INV, INV, ANY, INV, ANY, ANY),
+        scratch_shapes=[
+            pltpu.VMEM((length, triple), BF),
+            pltpu.VMEM((model, triple), BF),
+            pltpu.VMEM((length, model), BF),
+            pltpu.VMEM((line, rows, model), BF),
+            pltpu.VMEM((line + 1, rows, model), BF),
+            pltpu.VMEM((blocks, rows, triple), BF),
+            pltpu.VMEM((rows, triple), BF),
+            pltpu.VMEM((blocks, rows, triple), BF),
+            pltpu.VMEM((blocks - 1, rows, triple), BF),
+            pltpu.VMEM((line - 1, 8, model), F32),
+            pltpu.VMEM((8, 8, model), F32),
+            pltpu.VMEM((blocks, 352, rows), BF),
+            pltpu.VMEM((352, rows), F32),
+            dma((line, 2)), dma((line + 1, 2)), dma((blocks,)), dma((blocks,)), dma((blocks,)), dma((blocks,)),
+            dma((blocks,)), dma((blocks,)), dma((line,)), dma((line,)), dma((8,)), dma((8,)),
+            dma((4,)), dma((blocks + 1,)),
+        ],
+        compiler_params=pltpu.CompilerParams(
+            collective_id=4, has_side_effects=True, vmem_limit_bytes=62 * 1024 * 1024
+        ),
+        cost_estimate=pl.CostEstimate(flops=10**11, bytes_accessed=10**8, transcendentals=0),
+        name="input_backward",
+    )(dpre, wqkv, n1, dhalf, tok, dhid, small, sums)
+
+
 def turn_tables(length):
     cosine, sine = tables(length)
     rest = HEAD_DIM - ROT
@@ -626,137 +1392,53 @@
     return tuple(jnp.concatenate([t, t], -1) for t in (cos, up, down))
 
 
-def pack_smalls(d, model, qkv_bias, *vectors):
+def pack_smalls(d, model, width, qkv_bias, *vectors):
     col = lax.broadcasted_iota(jnp.int32, (1, model), 1)
     each = vectors[0].shape[0]
     gains = jnp.stack([jnp.tile(v, model // each) for v in vectors], 0)
     gains = jnp.where(col // each == d, gains, 0)
     part = qkv_bias.shape[1]
-    bias = jnp.where(col // part == d, jnp.tile(qkv_bias, (1, model // part)), 0)
-    return jnp.concatenate([gains, bias, jnp.zeros((9, model), BF)], 0).astype(BF)
+    bias = jnp.tile(qkv_bias, (1, width // part)).reshape(1, 3 * width)
+    bias = jnp.pad(bias, ((0, 0), (0, model - 3 * width)))
+    bias = jnp.where(col % width // part == d, bias, 0)
+    return jnp.concatenate([gains, bias, jnp.zeros((11, model), BF)], 0).astype(BF)
 
 
 def fast(
     tokens, qkv_weight, qkv_bias, out_weight, norm1_gain, norm1_shift, gate_weight, up_weight,
     down_weight, norm2_gain, norm2_shift, cotangent,
 ):
-    scale = HEAD_DIM ** (-0.5)
     d = lax.axis_index("dp")
     z = lax.axis_index("tensor")
     rows, model = tokens.shape
     length = 4 * rows
     tabs = turn_tables(length)
-    smalls = pack_smalls(d, model, qkv_bias, norm1_gain, norm1_shift, norm2_gain, norm2_shift)
-    xall, cotall, n1, qkv, lse, attall, wqkv, small_sum = attention_forward(
-        tokens, cotangent, qkv_weight, smalls, tabs
-    )
+    depth, width = qkv_weight.shape[1:]
+    smalls = pack_smalls(d, model, width, qkv_bias, norm1_gain, norm1_shift, norm2_gain, norm2_shift)
+    wq = qkv_weight.transpose(1, 0, 2).reshape(depth, 3 * width)
+    xall, cotall, n1, qkv, lse, attall, wqkv, small = attention_forward(tokens, cotangent, wq, smalls, tabs)
     wout = lax.all_gather(out_weight, "tensor", axis=0, tiled=True)
     wout = lax.all_gather(wout, "dp", axis=1, tiled=True)
     wgate = lax.all_gather(gate_weight, "dp", axis=0, tiled=True)
     wup = lax.all_gather(up_weight, "dp", axis=0, tiled=True)
     wdown = lax.all_gather(down_weight, "dp", axis=1, tiled=True)
-    g1, b1, g2, b2 = small_sum[0], small_sum[1], small_sum[2], small_sum[3]
-
-    def own(a):
-        return lax.dynamic_slice_in_dim(a, z * rows, rows, 0)
-
     hidden_all = xall.astype(F32) + nn(attall, wout)
-    n2_all, xhat_all, inv_all = apply_layer_norm(hidden_all, g2, b2)
-    rows2 = n2_all.astype(BF)
-    hidden_state, second_standardized, second_inverse_deviation = own(hidden_all), own(xhat_all), own(inv_all)
-    gate = nn(rows2, wgate)
-    up = nn(rows2, wup)
-    sigma = jax.nn.sigmoid(gate)
-    silu = gate * sigma
-    act = (silu * up).astype(BF)
-    mixed = sum_rows(nn(act, wdown))
-    layer_output = (hidden_state + mixed).astype(BF)
-    down_grad = tn(act, cotall)
-    dact = nt(cotall, wdown)
-    dgate = (dact * up * (sigma * (1.0 + gate * (1.0 - sigma)))).astype(BF)
-    dup = (dact * silu).astype(BF)
-    gate_grad = tn(rows2, dgate)
-    up_grad = tn(rows2, dup)
-    dn2 = sum_grads(nt(dgate, wgate) + nt(dup, wup))
-    second_scale_partial = jnp.sum(dn2 * second_standardized, 0)
-    shift2_part = jnp.sum(dn2, 0)
-    hidden_gradient = cotangent.astype(F32) + layer_norm_backward(
-        dn2, second_standardized, second_inverse_deviation, g2
-    )
-
-    def scatter(a, axis):
-        return lax.psum_scatter(a.astype(BF), "dp", scatter_dimension=axis, tiled=True)
-
-    gatew_grad = scatter(gate_grad, 0).astype(F32)
-    upw_grad = scatter(up_grad, 0).astype(F32)
-    downw_grad = scatter(down_grad, 1).astype(F32)
-    da = hidden_gradient.astype(BF)
-    out_grad = scatter(tn(own(attall), da), 1)
-    outw_grad = lax.psum_scatter(out_grad, "tensor", scatter_dimension=0, tiled=True).astype(F32)
-    dattended = nt(da, wout).astype(BF)
-    dattended = lax.all_to_all(dattended, "tensor", split_axis=1, concat_axis=0, tiled=True)
-    cosine, sine = tables(length)
-    width = wqkv.shape[2]
-    local_heads = width // HEAD_DIM
-    dattended = dattended.reshape(length, local_heads, HEAD_DIM)
-    query, keys, values = [
-        qkv[j].transpose(1, 0, 2).reshape(length, local_heads, HEAD_DIM) for j in range(3)
-    ]
-    stats = lse[:, :local_heads].T
-    cols = jnp.arange(length, dtype=jnp.int32)
-    block = 512
-
-    def backward_block(carry, index):
-        dkeys, dvalues = carry
-        qblock = lax.dynamic_slice_in_dim(query, index * block, block, 0)
-        dblock = lax.dynamic_slice_in_dim(dattended, index * block, block, 0)
-        block_lse = lax.dynamic_slice_in_dim(stats, index * block, block, 1)
-        scores = jnp.einsum("qhd,khd->hqk", qblock, keys, preferred_element_type=F32) * scale
-        keep = (index * block + jnp.arange(block, dtype=jnp.int32))[:, None] >= cols[None, :]
-        scores = jnp.where(keep[None], scores, -1e30)
-        probs = jnp.exp(scores - block_lse[..., None])
-        probs16 = probs.astype(BF)
-        dvalues = dvalues + jnp.einsum("hqk,qhd->khd", probs16, dblock, preferred_element_type=F32)
-        dprobs = jnp.einsum("qhd,khd->hqk", dblock, values, preferred_element_type=F32)
-        inner = jnp.sum(dprobs * probs, -1, keepdims=True)
-        dscores = (probs * (dprobs - inner)).astype(BF)
-        dquery = jnp.einsum("hqk,khd->qhd", dscores, keys, preferred_element_type=F32) * scale
-        dkeys = dkeys + jnp.einsum("hqk,qhd->khd", dscores, qblock, preferred_element_type=F32) * scale
-        return ((dkeys, dvalues), dquery)
-
-    empty = jnp.zeros((length, local_heads, HEAD_DIM), F32)
-    (dkeys, dvalues), dquery = lax.scan(backward_block, (empty, empty), jnp.arange(2, dtype=jnp.int32))
-    dquery = dquery.reshape(length, local_heads, HEAD_DIM)
-    dpre = jnp.stack(
-        [
-            unrotate(dquery, cosine, sine).reshape(length, width),
-            unrotate(dkeys, cosine, sine).reshape(length, width),
-            dvalues.reshape(length, width),
-        ],
-        0,
-    ).astype(BF)
-    qkv_grad = jnp.einsum("sd,jsc->jdc", n1, dpre, preferred_element_type=F32)
-    bias_grad = jnp.sum(dpre, axis=1, dtype=F32)
-    dn1 = sum_grads(jnp.einsum("jsc,jdc->sd", dpre, wqkv, preferred_element_type=F32))
-    _, first_standardized, first_inverse_deviation = apply_layer_norm(tokens.astype(F32), g1, b1)
-    token_gradient = (
-        hidden_gradient
-        + layer_norm_backward(dn1, first_standardized, first_inverse_deviation, g1)
-    ).astype(BF)
-    qkvw_grad = scatter(qkv_grad, 1).astype(F32)
-    small = jnp.concatenate(
-        [
-            jnp.stack(
-                [jnp.sum(dn1 * first_standardized, 0), jnp.sum(dn1, 0), second_scale_partial, shift2_part], 0
-            ),
-        ],
-        0,
-    )
-    small = lax.psum_scatter(lax.psum(small, "tensor"), "dp", scatter_dimension=1, tiled=True)
-    qkvb_grad = lax.psum_scatter(bias_grad, "dp", scatter_dimension=1, tiled=True)
+    n2, _, _ = apply_layer_norm(hidden_all, small[2], small[3])
+    hidden = lax.dynamic_slice_in_dim(hidden_all, z * rows, rows, 0)
+    dn2, mixed, _, _, _, ghalf, uhalf, dhalf, grecv = mlp(n2.astype(BF), cotall, wgate, wup, wdown)
+    layer_output, dhid, dpre, outw_grad, gatew_grad, upw_grad, sums, _, _ = attention_backward(
+        dn2, hidden, cotangent, small, wout, attall, qkv, lse, mixed, ghalf, grecv, uhalf, tabs
+    )
+    token_gradient, qkvw_grad, downw_grad, sums, _, _ = input_backward(
+        dpre, wqkv, n1, dhalf, tokens, dhid, small, sums
+    )
+    gains = lax.dynamic_slice_in_dim(sums[:4], d * depth, depth, 1)
+    part = qkv_bias.shape[1]
+    bias = sums[4, : 3 * width].reshape(3, width)
+    qkvb_grad = lax.dynamic_slice_in_dim(bias, d * part, part, 1)
     return (
-        layer_output, token_gradient, qkvw_grad, qkvb_grad, outw_grad, small[0], small[1],
-        gatew_grad, upw_grad, downw_grad, small[2], small[3],
+        layer_output, token_gradient, qkvw_grad, qkvb_grad, outw_grad, gains[0], gains[1],
+        gatew_grad, upw_grad, downw_grad, gains[2], gains[3],
     )
 
 

time: 1280 us -> 751 us (0.59)
  waiting for transfers between devices: 613 us -> 34.7 us
  Pallas kernels: 243 us -> 643 us
  matrix products: 215 us -> 13.3 us
  local copies, waits for them, and re-layouts: 96.9 us -> 24.1 us
  other arithmetic: 65.7 us -> 6.45 us
    reduce_scatter x9 -> x0, waiting for transfers between devices: 492 us -> none  [the longest x5 292 us: scatter(): lax.psum_scatter(a.astype(BF), 'dp', scatter_dimension=axis, tiled=True)]
    pallas_call x0 -> x3, Pallas kernels: none -> 399 us  [the longest x1 161 us: attention_backward(): pl.pallas_call(attention_back_kernel, out_shape=(sds((rows, model), BF),...]
    dot_general x20 -> x0, matrix products: 168 us -> none  [the longest x4 41.5 us: nt(): lax.dot_general(a, b, (((1,), (1,)), ((), ())), preferred_element_type=F32)]
    unnamed x18 -> x5, waiting for transfers between devices: 73 us -> 2.43 us
    dynamic_update_slice x4 -> x0, local copies, waits for them, and re-layouts: 41.2 us -> none  [fast(): lax.scan(backward_block, (empty, empty), jnp.arange(2, dtype=jnp.int32))]
    convert_element_type x9 -> x1, other arithmetic: 40.5 us -> 2.98 us  [fast(): n2.astype(BF)]
    dot_general x4 -> x1, matrix products: 47.5 us -> 13.3 us  [nn(): return jnp.dot(a, b, preferred_element_type=F32)]
    all_to_all x1 -> x0, waiting for transfers between devices: 16 us -> none  [fast(): lax.all_to_all(dattended, 'tensor', split_axis=1, concat_axis=0, tiled=True)]
  transfers between devices with their start and end apart: 17 -> 5, of which waited for: 13 -> 1; matrix products, arithmetic and copies ran while one was open for 12% -> 4% of each run, Pallas kernels for 19% -> 33%
where the time goes in v2:
time: 751 us; the launch traced here: 736 us
  Pallas kernels  643 us (86%)
  waiting for transfers between devices  34.7 us (5%)
  local copies, waits for them, and re-layouts  24.1 us (3%)
  between operations  14.2 us (2%)
  matrix products  13.3 us (2%)
    pallas_call x1, Pallas kernels, attention_forward(): pl.pallas_call(attention_kernel, out_shape=(sds((length, model), BF), sds...  244 us
    pallas_call x1, Pallas kernels, attention_backward(): pl.pallas_call(attention_back_kernel, out_shape=(sds((rows, model), BF),...  161 us
    pallas_call x1, Pallas kernels, input_backward(): pl.pallas_call(input_back_kernel, out_shape=(sds((rows, model), BF), sds(...  129 us
    pallas_call x1, Pallas kernels, mlp(): pl.pallas_call(mlp_kernel, out_shape=(sds((rows, model), F32), sds((lengt...  108 us
    all_gather x1, waiting for transfers between devices, fast(): wout = lax.all_gather(out_weight, 'tensor', axis=0, tiled=True)  32.3 us
  transfers between devices with their start and end apart: 5, of which 1 were waited for; matrix products, arithmetic and copies ran while one was open for 4% of the time, Pallas kernels for 33%

profile of v2, /device:TPU:0, one launch (start us, length us, event | category | flops | bytes accessed | tf_op | source)
XLA Modules:
  0.0 736.2 jit_solution(15529840994464369409)
XLA Ops:
  7.2 0.7 all-gather.6.cloned.1.call-update
  7.9 0.0 all-gather.8.cloned.1.call-start
  8.0 32.3 %all-gather.6.cloned.1.call-done = bf16[2048,256]{1,0:T(8,128)(2,1)} async-done(((bf16[512,256]{1,0:T(8,128)(2,1)}), bf16[2048,256]{1,0:T(8,128)(2,1)}) %all-gather.6.cloned.1.call-update) | async-done | bytes 1048592 | tf_op jit(solution)/shard_map/all_gather | solution.py:1420
  40.3 0.0 all-gather.10.cloned.1.call-start
  40.3 0.7 all-gather.10.cloned.1.call-update
  41.0 0.0 all-gather.12.cloned.1.call-start
  41.1 0.5 all-gather.12.cloned.1.call-update
  41.6 0.0 all-gather.14.cloned.1.call-start
  41.6 0.5 all-gather.14.cloned.1.call-update
  42.3 0.7 broadcast_bitcast_fusion.2
  42.9 0.7 broadcast_bitcast_fusion.1
  43.6 0.7 broadcast_bitcast_fusion
  44.3 0.7 tile.16
  45.0 0.1 tile.17
  45.1 0.1 iota_multiply_fusion
  45.1 0.1 pad_maximum_fusion.1
  45.3 0.2 copy.34
  45.5 1.7 sin.3
  47.2 0.2 copy.32
  47.4 0.2 slice_negate_fusion
  47.7 1.7 concatenate.25.sin_down
  49.4 1.7 concatenate.24.sin_up
  51.1 0.3 copy.31
  51.4 1.2 copy.35.wq
  52.6 0.1 pad.13.clone
  52.7 1.3 pad_maximum_fusion.cos
  54.0 0.1 maximum_select_fusion
  54.0 0.7 maximum_maximum_fusion.smalls
  54.8 244.5 %attention_forward.1 = (bf16[1024,2048]{1,0:T(8,128)(2,1)}, bf16[1024,2048]{1,0:T(8,128)(2,1)}, bf16[1024,2048]{1,0:T(8,128)(2,1)}, bf16[3,4,1024,128]{3,2,1,0:T...) custom-call(bf16[256,2048]{1,0:T(8,128)(2,1)} %tok.3, ...), custom_call_target="tpu_custom_call" | custom-call | flops 199999995904 | bytes 100000000 | tf_op jit(solution)/shard_map/attention_forward/pallas_call | solution.py:291
  299.2 0.9 fusion.5
  300.2 13.3 %fusion.7 = (f32[1024]{0:T(1024)S(1)}, f32[1024,2048]{1,0:T(8,128)S(1)}) fusion(bf16[1024,2048]{1,0:T(8,128)(2,1)} %get-tuple-element.38.attall, bf16[2048,2048]{1,0:T(8,128)(2,1)} %all-gather.8.cloned.1.call-done.wout, bf16[1024,2048]{1,0:T(8,128)(2,1)} %get-tuple-element.37), kind=kOutput, calls=%fused_computation.37 | convolution fusion | flops 8596225024 | bytes 25169920 | tf_op jit(solution)/shard_map/dot_general | solution.py:29
  313.5 1.0 multiply_reduce_fusion
  314.5 1.5 constant_dynamic-slice_fusion.2.hid
  315.9 3.0 add_convert_fusion.n2
  318.9 107.9 %mlp.1 = (f32[256,2048]{1,0:T(8,128)}, bf16[1024,2048]{1,0:T(8,128)(2,1)}, bf16[4,256,1408]{2,1,0:T(8,128)(2,1)}, bf16[4,256,1408]{2,1,0:T(8,128)(2,1)}, bf16[4,...) custom-call(bf16[1024,2048]{1,0:T(8,128)(2,1)} %add_convert_fusion.n, ...), custom_call_target="tpu_custom_call" | custom-call | flops 99999997952 | bytes 100000000 | tf_op jit(solution)/shard_map/mlp/pallas_call | solution.py:868
  426.8 161.4 %attention_backward.1 = (bf16[256,2048]{1,0:T(8,128)(2,1)}, f32[256,2048]{1,0:T(8,128)}, bf16[1024,1536]{1,0:T(8,128)(2,1)}, f32[512,256]{1,0:T(8,128)}, f32[256...) custom-call(f32[256,2048]{1,0:T(8,128)} %get-tuple-element.41.dn2, ...), custom_call_target="tpu_custom_call" | custom-call | flops 99999997952 | bytes 100000000 | tf_op jit(solution)/shard_map/attention_backward/pallas_call | solution.py:1174
  588.3 129.4 %input_backward.1 = (bf16[256,2048]{1,0:T(8,128)(2,1)}, f32[3,256,512]{2,1,0:T(8,128)}, f32[1408,256]{1,0:T(8,128)}, f32[8,2048]{1,0:T(8,128)}, bf16[3,1408,256]...) custom-call(bf16[1024,1536]{1,0:T(8,128)(2,1)} %get-tuple-element.49.dpre, bf16[2048,1536]{1,0:T(8,128)(2,1)} %get-tuple-element.50.wqkv, ...), custom_call_target="tpu_custom_call" | custom-call | flops 99999997952 | bytes 100000000 | tf_op jit(solution)/shard_map/input_backward/pallas_call | solution.py:1349
  717.7 1.0 slice_reduce_fusion
  718.7 0.8 slice.35
  719.6 0.7 constant_dynamic-slice_fusion.1
  720.2 0.6 fusion.6
  720.9 1.0 copy.47
  721.8 2.4 copy.48
  724.3 1.1 copy.49
  725.4 0.8 copy.50
  726.2 1.1 copy.51
  727.3 1.1 copy.52
  728.4 1.1 copy.53
  (39 shorter events, 0.3 us)
Async XLA Ops:
  7.2 35.0 %copy-start = (bf16[256]{0:T(256)(128)(2,1)S(1)}, bf16[256]{0:T(256)(128)(2,1)}, u32[]{:S(2)}) copy-start(bf16[256]{0:T(256)(128)(2,1)} %param.16) | copy-start | bytes 1540
  7.2 33.1 %all-gather.6.cloned.1.call-start = ((), (), s32[]{:S(2)}) async-start(), calls=%async_computation | async-start | bytes 1310720 | tf_op jit(solution)/shard_map/all_gather | solution.py:1420
  7.9 292.3 %all-gather.8.cloned.1.call-start = ((), (), s32[]{:S(2)}) async-start(), calls=%async_computation.1 | async-start | bytes 9437184 | tf_op jit(solution)/shard_map/all_gather | solution.py:1421
  40.3 278.6 %all-gather.10.cloned.1.call-start = ((), (), s32[]{:S(2)}) async-start(), calls=%async_computation.2 | async-start | bytes 6488064 | tf_op jit(solution)/shard_map/all_gather | solution.py:1422
  41.0 277.9 %all-gather.12.cloned.1.call-start = ((), (), s32[]{:S(2)}) async-start(), calls=%async_computation.3 | async-start | bytes 6488064 | tf_op jit(solution)/shard_map/all_gather | solution.py:1423
  41.6 277.3 %all-gather.14.cloned.1.call-start = ((), (), s32[]{:S(2)}) async-start(), calls=%async_computation.4 | async-start | bytes 6488064 | tf_op jit(solution)/shard_map/all_gather | solution.py:1424
  47.6 3.6 copy-start.7
  588.3 132.6 %copy-start.6 = (bf16[256,2048]{1,0:T(8,128)(2,1)S(1)}, bf16[256,2048]{1,0:T(8,128)(2,1)}, u32[]{:S(2)}) copy-start(bf16[256,2048]{1,0:T(8,128)(2,1)} %get-tuple-element.86) | copy-start | bytes 3145732
  717.7 6.5 copy-start.2
  717.7 7.7 %copy-start.8 = (f32[512,256]{1,0:T(8,128)S(1)}, f32[512,256]{1,0:T(8,128)}, u32[]{:S(2)}) copy-start(f32[512,256]{1,0:T(8,128)} %get-tuple-element.90) | copy-start | bytes 1572868
  720.9 5.3 copy-start.4
  721.8 5.5 copy-start.3
  725.4 3.0 copy-start.5
  725.4 4.1 copy-start.1
Sparse Core Ops, SparseCore 0:
  9.6 30.6 all-gather.5
  42.1 87.5 all-gather.7
  131.6 43.2 all-gather.9
  176.6 43.3 all-gather.11
  221.7 44.3 all-gather.13

commit v3 on v2

--- a/solution.py
+++ b/solution.py
@@ -2,6 +2,7 @@
 
 import jax
 import jax.numpy as jnp
+import numpy as np
 from jax import lax
 from jax.experimental import pallas as pl
 from jax.experimental.pallas import tpu as pltpu
@@ -27,6 +28,10 @@
 
 def nn(a, b):
     return jnp.dot(a, b, preferred_element_type=F32)
+
+
+def spans(total, step):
+    return [(i, min(step, total - i)) for i in range(0, total, step)]
 
 
 def place():
@@ -71,25 +76,70 @@
         pl.when(self.z < self.line - 1)(lambda: self.copy(self.z, h, 0, src).start())
         pl.when(self.z > 0)(lambda: self.copy(self.z, h, 1, src).start())
 
-    def step(self, k, h):
+    def step(self, k, h, forward=True):
         z, line = self.z, self.line
 
         @pl.when(z - k >= 0)
         def _():
             self.copy(z - k, h, 0).wait_recv()
-            pl.when(z < line - 1)(lambda: self.copy(z - k, h, 0).start())
+            if forward:
+                pl.when(z < line - 1)(lambda: self.copy(z - k, h, 0).start())
 
         @pl.when(z + k < line)
         def _():
             self.copy(z + k, h, 1).wait_recv()
-            pl.when(z > 0)(lambda: self.copy(z + k, h, 1).start())
-
-    def finish(self):
+            if forward:
+                pl.when(z > 0)(lambda: self.copy(z + k, h, 1).start())
+
+    def finish(self, first=0, last=None):
         z, line = self.z, self.line
-        for k in range(line):
+        for k in range(first, line if last is None else last):
             for h in range(self.chunks):
                 pl.when((z - k >= 0) & (z < line - 1))(lambda: self.copy(z - k, h, 0).wait_send())
                 pl.when((z + k < line) & (z > 0))(lambda: self.copy(z + k, h, 1).wait_send())
+
+
+class PlaneGather:
+    def __init__(self, src, view, d, z, flips, send_sems, recv_sems):
+        self.src, self.view, self.d, self.z, self.flips = src, view, d, z, flips
+        self.ss, self.rs = send_sems, recv_sems
+        self.half = src.shape[0] // 2
+
+    def copy(self, key):
+        d, f = self.d, self.flips
+        block, to, part = {
+            1: (0, 1, None), 2: (0, 2, None), 4: (0, 4, None), 3: (2, 1, None), 5: (4, 1, None),
+            6: (2, 4, 0), 7: (4, 2, 1), 8: (6, 1, 0), 9: (6, 1, 1),
+        }[key]
+        dst = self.view(d + f[block])
+        src = self.src if block == 0 else dst
+        if part is not None:
+            at = pl.ds(part * self.half, self.half)
+            src, dst = src.at[at], dst.at[at]
+        return send(src, dst, self.ss.at[key], self.rs.at[key], d + f[to], self.z)
+
+    def start(self):
+        for key in (4, 2, 1):
+            self.copy(key).start()
+
+    def relay(self):
+        for key, onward in ((2, (6, 3)), (4, (7, 5))):
+            self.copy(key).wait_recv()
+            for to in onward:
+                self.copy(to).start()
+
+    def pass_on(self):
+        for key, onward in ((6, 8), (7, 9)):
+            self.copy(key).wait_recv()
+            self.copy(onward).start()
+
+    def arrive(self):
+        for key in (1, 3, 5, 8, 9):
+            self.copy(key).wait_recv()
+
+    def finish(self):
+        for key in range(1, 10):
+            self.copy(key).wait_send()
 
 
 def arrival(z, i):
@@ -108,12 +158,12 @@
 
 
 def attention_kernel(
-    tok, cot, wq, smalls, cos, sin_up, sin_down,
-    xall, cotall, n1, qkv, lse, attall, wqkv, small_sum,
-    xbuf, n1buf, wbuf, qbuf, abuf, smbuf,
-    tss, trs, css, crs, ass, ars, wss, wrs, mss, mrs, local,
+    tok, cot, wq, ow, gw, uw, dw, smalls, cos, sin_up, sin_down,
+    cotnear, n1, qkv, lse, attall, wqkv, small_sum, wout, n2, hidden, wgate, wup, wdown,
+    xbuf, n1buf, wbuf, qbuf, attv, wz, wo, acc, smbuf,
+    tss, trs, css, crs, ass, ars, mss, mrs, yss, yrs, pss, prs, local,
 ):
-    rows = tok.shape[0]
+    rows, model = tok.shape
     width = wq.shape[1] // 3
     pairs = width // 128
     line = 4
@@ -122,8 +172,6 @@
 
     tok_in = pltpu.make_async_copy(tok, xbuf.at[z], local.at[0])
     tok_in.start()
-    cot_in = pltpu.make_async_copy(cot, cotall.at[pl.ds(z * rows, rows)], local.at[1])
-    cot_in.start()
     depth = wq.shape[0]
 
     def wblock(i):
@@ -131,24 +179,58 @@
 
     w_in = pltpu.make_async_copy(wq, wblock(d), local.at[2])
     w_in.start()
+    tall = ow.shape[0]
+
+    def oview(s, h):
+        return wz.at[pl.ds(pl.multiple_of(s * tall, tall), tall)]
+
+    def oblock(i):
+        return wo.at[:, pl.ds(pl.multiple_of(i * depth, 256), depth)]
+
+    o_in = pltpu.make_async_copy(ow, oview(z, 0), local.at[14])
+    o_in.start()
+    outs_z = LineGather(oview, 1, d, z, line, yss, yrs)
     small_copies = [
         send(smalls, smbuf.at[r], mss.at[r], mrs.at[r], d + flips[r], z) for r in range(1, 8)
     ]
     for copy in small_copies:
         copy.start()
-    w_sends = {
-        r: send(wq, wblock(d), wss.at[r], wrs.at[r], d + flips[r], z) for r in (4, 2, 1, 6)
-    }
+    tall_block = dw.shape[1]
+
+    def rows_of(ref, i):
+        return ref.at[pl.ds(pl.multiple_of(i * depth, 256), depth)]
+
+    def columns_of(ref, i):
+        return ref.at[:, pl.ds(pl.multiple_of(i * tall_block, 256), tall_block)]
+
+    planes = [
+        PlaneGather(src, view, d, z, flips, pss.at[i], prs.at[i])
+        for i, (src, view) in enumerate((
+            (wq, wblock),
+            (wz, oblock),
+            (gw, lambda i: rows_of(wgate, i)),
+            (uw, lambda i: rows_of(wup, i)),
+            (dw, lambda i: columns_of(wdown, i)),
+        ))
+    ]
+    qkv_plane, out_plane, gate_plane, up_plane, down_plane = planes
+    keep_own = [
+        pltpu.make_async_copy(gw, rows_of(wgate, d), local.at[10]),
+        pltpu.make_async_copy(uw, rows_of(wup, d), local.at[11]),
+        pltpu.make_async_copy(dw, columns_of(wdown, d), local.at[12]),
+    ]
+    for copy in keep_own:
+        copy.start()
     half = rows // 2
 
     def tview(s, h):
         return xbuf.at[s, pl.ds(h * half, half)]
 
     def cview(s, h):
-        return cotall.at[pl.ds(pl.multiple_of(s * rows + h * half, 128), half)]
+        return cotnear.at[s, pl.ds(h * half, half)]
 
     def aview(s, h):
-        return attall.at[:, pl.ds(pl.multiple_of(s * width + h * 128, 128), 128)]
+        return attv.at[:, pl.ds(pl.multiple_of(s * width + h * 128, 128), 128)]
 
     toks = LineGather(tview, 2, d, z, line, tss, trs)
     cots = LineGather(cview, 2, d, z, line, css, crs)
@@ -156,8 +238,9 @@
     tok_in.wait()
     for h in range(2):
         toks.start(h)
-    for copy in w_sends.values():
-        copy.start()
+    qkv_plane.start()
+    o_in.wait()
+    outs_z.start(0)
     for copy in small_copies:
         copy.wait()
     total = smalls[...].astype(F32)
@@ -188,40 +271,46 @@
                     part = turn(part, cos[at, :], sin_up[at, :], sin_down[at, :])
                 qbuf[j, p, at, :] = part.astype(BF)
 
+    normalise(z)
     for h in range(2):
         toks.step(1, h)
-    for r in (2, 4, 6):
-        w_sends[r].wait_recv()
-        send(wblock(d + flips[r]), wblock(d + flips[r]), wss.at[r + 1], wrs.at[r + 1], d + flips[1], z).start()
+    outs_z.step(1, 0)
+    qkv_plane.relay()
+    gate_plane.start()
+    normalise(arrival(z, 1))
+    qkv_plane.pass_on()
+    for h in range(2):
+        toks.step(2, h)
+    outs_z.step(2, 0)
+    normalise(arrival(z, 2))
+    gate_plane.relay()
     w_in.wait()
-    w_sends[1].wait_recv()
-    for r in (3, 5, 7):
-        send(wblock(d), wblock(d), wss.at[r], wrs.at[r], d + flips[1], z).wait_recv()
+    qkv_plane.arrive()
 
     @pl.loop(0, line)
     def _(i):
+        s = arrival(z, i)
+
         @pl.when(i == line - 1)
         def _():
-            cot_in.wait()
+            gate_plane.pass_on()
             for h in range(2):
-                cots.start(h)
-
-        s = arrival(z, i)
-        normalise(s)
+                toks.step(3, h)
+            for h in range(2):
+                cots.start(h, cot.at[pl.ds(h * half, half)])
+            outs_z.step(3, 0)
+            out_plane.start()
+            normalise(s)
+
         project(s)
 
-        @pl.when((i >= 1) & (i < line - 1))
-        def _():
-            for h in range(2):
-                toks.step(i + 1, h)
+    o_own = pltpu.make_async_copy(wz, oblock(d), local.at[15])
+    o_own.start()
 
     outs = [
         pltpu.make_async_copy(n1buf, n1, local.at[3]),
         pltpu.make_async_copy(wbuf, wqkv, local.at[4]),
         pltpu.make_async_copy(qbuf, qkv, local.at[5]),
-    ] + [
-        pltpu.make_async_copy(xbuf.at[s], xall.at[pl.ds(s * rows, rows)], local.at[6 + s])
-        for s in range(line)
     ]
     for copy in outs:
         copy.start()
@@ -231,7 +320,7 @@
     lse[...] = jnp.zeros_like(lse)
     length = rows * line
 
-    def attend(p, start):
+    def attend(p):
         for qi in range(line):
             count = (qi + 1) * rows
             at = pl.ds(qi * rows, rows)
@@ -253,33 +342,93 @@
                 results.append(nn(e.astype(BF), v) / total)
                 stats = jnp.where(lanes == 2 * p + a, most + jnp.log(total), stats)
             lse[at, :] = stats
-            abuf[p, at, :] = jnp.where(first, results[0], results[1]).astype(BF)
-
-    def own_columns(p):
-        return pltpu.make_async_copy(abuf.at[p], aview(z, p), local.at[10 + p])
+            attv[at, pl.ds(pl.multiple_of(z * width + p * 128, 128), 128)] = jnp.where(
+                first, results[0], results[1]
+            ).astype(BF)
 
     @pl.loop(0, pairs)
     def _(p):
-        attend(p, None)
-        own_columns(p).start()
-        atts.start(p, abuf.at[p])
-
-    for k in range(1, line):
-        for h in range(2):
-            cots.step(k, h)
-        for p in range(pairs):
-            atts.step(k, p)
-    for gather in (toks, cots, atts):
-        gather.finish()
-    for r in range(1, 8):
-        send(wblock(d), wblock(d), wss.at[r], wrs.at[r], d + flips[1], z).wait_send()
+        attend(p)
+        atts.start(p)
+
+    up_plane.start()
+    for p in range(pairs):
+        atts.step(1, p)
+    for h in range(2):
+        cots.step(1, h, forward=False)
+    out_plane.relay()
+    down_plane.start()
+    out_plane.pass_on()
+    for p in range(pairs):
+        atts.step(2, p)
+    o_own.wait()
+    out_plane.arrive()
+    keep_wo = pltpu.make_async_copy(wo, wout, local.at[6])
+    keep_wo.start()
+
+    def project_out(s, at, lo, size):
+        heads = pl.ds(pl.multiple_of(s * width, width), width)
+        return nn(attv[at, heads], wo[heads, pl.ds(lo, size)])
+
+    for i in range(line - 1):
+        s = arrival(z, i)
+
+        @pl.loop(0, line)
+        def _(r):
+            at = pl.ds(pl.multiple_of(r * rows, rows), rows)
+            for lo, size in spans(model, 512):
+                base = xbuf[r, :, pl.ds(lo, size)].astype(F32) if i == 0 else acc[at, pl.ds(lo, size)]
+                acc[at, pl.ds(lo, size)] = base + project_out(s, at, lo, size)
+
+        if i == 1:
+            up_plane.relay()
     for copy in outs:
         copy.wait()
+    down_plane.relay()
+    up_plane.pass_on()
     for p in range(pairs):
-        own_columns(p).wait()
-
-
-def attention_forward(tok, cot, wq, smalls, tabs):
+        atts.step(3, p)
+    keep_att = pltpu.make_async_copy(attv, attall, local.at[7])
+    keep_att.start()
+    last = arrival(z, line - 1)
+
+    @pl.loop(0, line)
+    def _(r):
+        at = pl.ds(pl.multiple_of(r * rows, rows), rows)
+        for lo, size in spans(model, 512):
+            acc[at, pl.ds(lo, size)] += project_out(last, at, lo, size)
+
+        @pl.loop(0, rows // 32)
+        def _(i):
+            piece = pl.ds(pl.multiple_of(r * rows + i * 32, 32), 32)
+            x = acc[piece, :]
+            centred = x - jnp.mean(x, -1, keepdims=True)
+            spread = jnp.mean(centred * centred, -1, keepdims=True)
+            n = centred * lax.rsqrt(spread + 1e-05) * small_sum[2:3, :] + small_sum[3:4, :]
+            n1buf[piece, :] = n.astype(BF)
+
+    keep = [
+        pltpu.make_async_copy(n1buf, n2, local.at[8]),
+        pltpu.make_async_copy(acc.at[pl.ds(pl.multiple_of(z * rows, rows), rows)], hidden, local.at[9]),
+        keep_wo, keep_att,
+    ]
+    for copy in keep[:2]:
+        copy.start()
+    down_plane.pass_on()
+    for gather in (toks, atts, outs_z):
+        gather.finish()
+    cots.finish(0, 1)
+    for plane in (gate_plane, up_plane, down_plane):
+        plane.arrive()
+    for plane in planes:
+        plane.finish()
+    for copy in keep_own:
+        copy.wait()
+    for copy in keep:
+        copy.wait()
+
+
+def attention_forward(tok, cot, wq, ow, gw, uw, dw, smalls, tabs):
     rows, model = tok.shape
     line = 4
     length = rows * line
@@ -287,22 +436,28 @@
     width //= 3
     pairs = width // 128
     dp = model // depth
+    hidden = gw.shape[1]
     sds = jax.ShapeDtypeStruct
     return pl.pallas_call(
         attention_kernel,
         out_shape=(
-            sds((length, model), BF), sds((length, model), BF), sds((length, model), BF),
+            sds((line, rows, model), BF), sds((length, model), BF),
             sds((3, pairs, length, 128), BF), sds((length, 128), F32), sds((length, model), BF),
             sds((model, 3 * width), BF), sds((16, model), F32),
+            sds((model, model), BF), sds((length, model), BF), sds((rows, model), F32),
+            sds((model, hidden), BF), sds((model, hidden), BF), sds((hidden, model), BF),
         ),
-        in_specs=[ANY, ANY, ANY, INV, INV, INV, INV],
-        out_specs=(ANY, ANY, ANY, ANY, INV, ANY, ANY, INV),
+        in_specs=[ANY] * 7 + [INV] * 4,
+        out_specs=(ANY, ANY, ANY, INV, ANY, ANY, INV) + (ANY,) * 6,
         scratch_shapes=[
             pltpu.VMEM((line, rows, model), BF),
             pltpu.VMEM((length, model), BF),
             pltpu.VMEM((model, 3 * width), BF),
             pltpu.VMEM((3, pairs, length, 128), BF),
-            pltpu.VMEM((pairs, length, 128), BF),
+            pltpu.VMEM((length, model), BF),
+            pltpu.VMEM((model, depth), BF),
+            pltpu.VMEM((model, model), BF),
+            pltpu.VMEM((length, model), F32),
             pltpu.VMEM((dp, 16, model), BF),
             pltpu.SemaphoreType.DMA((2, line, 2)),
             pltpu.SemaphoreType.DMA((line, 2)),
@@ -312,8 +467,10 @@
             pltpu.SemaphoreType.DMA((line, pairs)),
             pltpu.SemaphoreType.DMA((8,)),
             pltpu.SemaphoreType.DMA((8,)),
-            pltpu.SemaphoreType.DMA((8,)),
-            pltpu.SemaphoreType.DMA((8,)),
+            pltpu.SemaphoreType.DMA((2, line, 1)),
+            pltpu.SemaphoreType.DMA((line, 1)),
+            pltpu.SemaphoreType.DMA((5, 10)),
+            pltpu.SemaphoreType.DMA((5, 10)),
             pltpu.SemaphoreType.DMA((16,)),
         ],
         compiler_params=pltpu.CompilerParams(
@@ -321,7 +478,7 @@
         ),
         cost_estimate=pl.CostEstimate(flops=2 * 10**11, bytes_accessed=10**8, transcendentals=0),
         name="attention_forward",
-    )(tok, cot, wq, smalls, *tabs)
+    )(tok, cot, wq, ow, gw, uw, dw, smalls, *tabs)
 
 
 def apply_layer_norm(value, norm_scale, norm_bias):
@@ -689,15 +846,11 @@
     return lax.rem(lax.div(code, power), 4)
 
 
-def spans(total, step):
-    return [(i, min(step, total - i)) for i in range(0, total, step)]
-
-
 def mlp_kernel(
-    n2, cot, wgate, wup, wdown,
-    dn2, mixed, gex, uex, dex, ghalf, uhalf, dhalf, grecv,
+    n2, cot, cotnear, wgate, wup, wdown,
+    dn2, mixed, mland, gex, uex, dex, ghalf, uhalf, dhalf, grecv,
     nbuf, cbuf, gw, uw, dw, act, act_t, dga, dup, part, slots, mixbuf, wide, tall, wide_in, tall_in,
-    ss, rs, local, mixsem, outsem, exs, exr, gss, grs,
+    ss, rs, css, crs, lss, lrs, local, mixsem, outsem, exs, exr, gss, grs,
 ):
     line = 4
     rows = n2.shape[0] // line
@@ -709,7 +862,7 @@
     chip = lax.div(d, 2)
     loads = [
         pltpu.make_async_copy(a, b, local.at[i])
-        for i, (a, b) in enumerate(((n2, nbuf), (wgate, gw), (wup, uw), (cot, cbuf), (wdown, dw)))
+        for i, (a, b) in enumerate(((n2, nbuf), (wgate, gw), (wup, uw), (wdown, dw)))
     ]
     for copy in loads:
         copy.start()
@@ -721,8 +874,37 @@
     )
     pl.when(z == 0)(lambda: slots.__setitem__((0,), jnp.zeros((rows, model), BF)))
     pl.when(z == line - 1)(lambda: slots.__setitem__((line,), jnp.zeros((rows, model), BF)))
+    cots = LineGather(
+        lambda s, h: cbuf.at[pl.ds(pl.multiple_of(s * rows + h * half, half), half)], 2, d, z, line, css, crs
+    )
+
+    def near(s, k):
+        return pltpu.make_async_copy(
+            cot if k == 0 else cotnear.at[s], cbuf.at[pl.ds(pl.multiple_of(s * rows, rows), rows)], local.at[5 + k]
+        )
+
+    for h in range(2):
+        @pl.when((z > 0) & (z < line - 1))
+        def _():
+            cots.copy(z - 1, h, 0, cotnear.at[z - 1, pl.ds(h * half, half)]).start()
+            cots.copy(z + 1, h, 1, cotnear.at[z + 1, pl.ds(h * half, half)]).start()
+    near(z, 0).start()
+    pl.when(z > 0)(lambda: near(z - 1, 1).start())
+    pl.when(z < line - 1)(lambda: near(z + 1, 2).start())
     for copy in loads:
         copy.wait()
+
+    def mixed_out(i):
+        s = far_first(z, i)
+        at = pl.ds(pl.multiple_of(s * rows, rows), rows)
+        return pltpu.make_async_copy(mixbuf.at[lax.rem(i, 2)], mixed.at[at], mixsem.at[lax.rem(i, 2)])
+
+    def mixed_ahead(i):
+        at = pl.ds(pl.multiple_of(far_first(z, i) * rows, rows), rows)
+        to = jnp.where(z == 0, 1, line - 2)
+        return send(mixed.at[at], mland.at[i], lss.at[i], lrs.at[i], d, to)
+
+    at_end = (z == 0) | (z == line - 1)
 
     @pl.loop(0, line)
     def _(i):
@@ -732,12 +914,43 @@
             cols = pl.ds(lo, size)
             gate = nn(nbuf[at, :], gw[:, cols])
             up = nn(nbuf[at, :], uw[:, cols])
-            dact = nt(cbuf[at, :], dw[cols, :])
             sigma = lax.logistic(gate)
             silu = gate * sigma
-            act[at, cols] = (silu * up).astype(BF)
-            dga[at, cols] = (dact * up * (sigma * (1.0 + gate * (1.0 - sigma)))).astype(BF)
-            dup[at, cols] = (dact * silu).astype(BF)
+            value = (silu * up).astype(BF)
+            act[:, cols] = value
+            act_t[cols, at] = value.T
+            dga[at, cols] = (up * (sigma * (1.0 + gate * (1.0 - sigma)))).astype(BF)
+            dup[at, cols] = silu.astype(BF)
+        for lo, size in spans(model, 512):
+            mixbuf[lax.rem(i, 2), :, pl.ds(lo, size)] = nn(act[...], dw[:, pl.ds(lo, size)]).astype(BF)
+        mixed_out(i).start()
+
+        @pl.when(i >= 1)
+        def _():
+            mixed_out(i - 1).wait()
+            pl.when(at_end & (i <= 2))(lambda: mixed_ahead(i - 1).start())
+
+        @pl.when(i == line - 2)
+        def _():
+            for h in range(2):
+                cots.step(2, h)
+
+    mixed_out(line - 1).wait()
+    near(z, 0).wait()
+    pl.when(z > 0)(lambda: near(z - 1, 1).wait())
+    pl.when(z < line - 1)(lambda: near(z + 1, 2).wait())
+    for h in range(2):
+        cots.step(3, h)
+
+    @pl.loop(0, line)
+    def _(i):
+        s = far_first(z, i)
+        at = pl.ds(pl.multiple_of(s * rows, rows), rows)
+        for lo, size in spans(hidden, 512):
+            cols = pl.ds(lo, size)
+            dact = nt(cbuf[at, :], dw[cols, :])
+            dga[at, cols] = (dact * dga[at, cols].astype(F32)).astype(BF)
+            dup[at, cols] = (dact * dup[at, cols].astype(F32)).astype(BF)
         for lo, size in spans(model, 512):
             cols = pl.ds(lo, size)
             part[s, :, cols] = (nt(dga[at, :], gw[cols, :]) + nt(dup[at, :], uw[cols, :])).astype(BF)
@@ -801,7 +1014,7 @@
                     onward(j - 2).start()
 
             away(k).wait_recv()
-            fetch = pltpu.make_async_copy(exes[m].at[k], stage_in, local.at[5])
+            fetch = pltpu.make_async_copy(exes[m].at[k], stage_in, local.at[4])
             fetch.start()
             fetch.wait()
             make = block(2 * k + core)
@@ -819,25 +1032,6 @@
 
     onward = exchanged(0)
 
-    def mixed_out(i):
-        cols = pl.ds(pl.multiple_of(i * 512, 512), 512)
-        return pltpu.make_async_copy(mixbuf.at[lax.rem(i, 2)], mixed.at[:, cols], mixsem.at[lax.rem(i, 2)])
-
-    @pl.loop(0, line)
-    def _(s):
-        at = pl.ds(pl.multiple_of(s * rows, rows), rows)
-        for lo, size in spans(hidden, 512):
-            act_t[pl.ds(lo, size), at] = act[at, pl.ds(lo, size)].T
-
-    @pl.loop(0, model // 512)
-    def _(i):
-        pl.when(i >= 2)(lambda: mixed_out(i - 2).wait())
-        cols = pl.ds(pl.multiple_of(i * 512, 512), 512)
-        for s in range(line):
-            at = pl.ds(s * rows, rows)
-            mixbuf[lax.rem(i, 2), at, :] = nn(act[at, :], dw[:, cols]).astype(BF)
-        mixed_out(i).start()
-
     scatter.relay(2)
     exchanged(1)
     exchanged(2)
@@ -850,13 +1044,15 @@
             dn2[pl.ds(pl.multiple_of(h * half + i * 32, 32), 32), :] = scatter.total(h, rows_at)
 
     scatter.finish()
-    for i in (model // 512 - 2, model // 512 - 1):
-        mixed_out(i).wait()
+    for i in range(2):
+        pl.when(at_end)(lambda: mixed_ahead(i).wait_send())
+        pl.when(~at_end)(lambda: mixed_ahead(i).wait_recv())
+    cots.finish(1, line - 1)
     for j in range(blocks - 1):
         onward(j).wait()
 
 
-def mlp(n2, cot, wgate, wup, wdown):
+def mlp(n2, cot, cotnear, wgate, wup, wdown):
     length, model = n2.shape
     hidden = wgate.shape[1]
     line = 4
@@ -868,31 +1064,35 @@
     return pl.pallas_call(
         mlp_kernel,
         out_shape=(
-            sds((rows, model), F32), sds((length, model), BF),
+            sds((rows, model), F32), sds((length, model), BF), sds((2, rows, model), BF),
             wide, wide, tall, wide, wide, tall, sds((blocks - 1, rows, hidden), BF),
         ),
-        in_specs=[ANY] * 5,
-        out_specs=(INV,) + (ANY,) * 8,
+        in_specs=[ANY] * 6,
+        out_specs=(INV,) + (ANY,) * 9,
         scratch_shapes=[
             pltpu.VMEM((length, model), BF),
             pltpu.VMEM((length, model), BF),
             pltpu.VMEM((model, hidden), BF),
             pltpu.VMEM((model, hidden), BF),
             pltpu.VMEM((hidden, model), BF),
-            pltpu.VMEM((length, hidden), BF),
+            pltpu.VMEM((rows, hidden), BF),
             pltpu.VMEM((hidden, length), BF),
             pltpu.VMEM((length, hidden), BF),
             pltpu.VMEM((length, hidden), BF),
             pltpu.VMEM((line, rows, model), BF),
             pltpu.VMEM((line + 1, rows, model), BF),
-            pltpu.VMEM((2, length, 512), BF),
+            pltpu.VMEM((2, rows, model), BF),
             pltpu.VMEM((2, rows, hidden), BF),
             pltpu.VMEM((2, hidden, rows), BF),
             pltpu.VMEM((rows, hidden), BF),
             pltpu.VMEM((hidden, rows), BF),
             pltpu.SemaphoreType.DMA((line, 2)),
             pltpu.SemaphoreType.DMA((line + 1, 2)),
-            pltpu.SemaphoreType.DMA((6,)),
+            pltpu.SemaphoreType.DMA((2, line, 2)),
+            pltpu.SemaphoreType.DMA((line, 2)),
+            pltpu.SemaphoreType.DMA((2,)),
+            pltpu.SemaphoreType.DMA((2,)),
+            pltpu.SemaphoreType.DMA((8,)),
             pltpu.SemaphoreType.DMA((2,)),
             pltpu.SemaphoreType.DMA((2,)),
             pltpu.SemaphoreType.DMA((3, blocks)),
@@ -905,7 +1105,7 @@
         ),
         cost_estimate=pl.CostEstimate(flops=10**11, bytes_accessed=10**8, transcendentals=0),
         name="mlp",
-    )(n2, cot, wgate, wup, wdown)
+    )(n2, cot, cotnear, wgate, wup, wdown)
 
 
 def norm_parts(x):
@@ -945,6 +1145,57 @@
     def wait(self):
         for j in range(self.blocks - 1):
             self.copy(j).wait()
+
+
+class PlaneChain:
+    def __init__(self, half, recv, mid, d, z, flips, send_sems, recv_sems):
+        self.half, self.recv, self.mid, self.d, self.z, self.flips = half, recv, mid, d, z, flips
+        self.ss, self.rs = send_sems, recv_sems
+        self.rows = half.shape[1] // 2
+
+    def block(self, r):
+        return lax.div(self.d + self.flips[r], 2)
+
+    def copy(self, key):
+        block, over, part = ((6, 2, 0), (6, 4, 1), (4, 4, 1), (2, 2, 0), (4, 4, 0), (2, 2, 1))[key]
+        at = pl.ds(part * self.rows, self.rows)
+        dst = self.mid.at[key] if key < 2 else self.recv.at[0 if over == 2 else 1, at]
+        return send(
+            self.half.at[self.block(block), at], dst, self.ss.at[key], self.rs.at[key], self.d + self.flips[over], self.z
+        )
+
+    def start(self):
+        for key in range(4):
+            self.copy(key).start()
+
+    def relay(self):
+        for key, block, part in ((0, 4, 0), (1, 2, 1)):
+            self.copy(key).wait_recv()
+            k = self.block(block)
+            piece = min(self.rows, 128)
+
+            @pl.loop(0, self.rows // piece)
+            def _(i):
+                at = pl.ds(pl.multiple_of(part * self.rows + i * piece, piece), piece)
+                mid = self.mid[key, pl.ds(pl.multiple_of(i * piece, piece), piece), :]
+                self.half[k, at, :] = (self.half[k, at, :].astype(F32) + mid.astype(F32)).astype(BF)
+
+            self.copy(key + 4).start()
+
+    def arrive(self):
+        for key in range(2, 6):
+            self.copy(key).wait_recv()
+
+    def total(self, at):
+        return (
+            self.half[(self.block(0),) + at].astype(F32)
+            + self.recv[(0,) + at].astype(F32)
+            + self.recv[(1,) + at].astype(F32)
+        )
+
+    def finish(self):
+        for key in range(6):
+            self.copy(key).wait_send()
 
 
 def sum_blocks(own, recv, out, buf, obuf, sems, pieces):
@@ -971,9 +1222,9 @@
 
 
 def attention_back_kernel(
-    dn2, hid, cot, small, wout, attall, qkv, lse, mixed, ghalf, grecv, uhalf, cos, sin_up, sin_down,
+    dn2, hid, cot, small, wout, attall, qkv, lse, mixed, mland, ghalf, grecv, uhalf, cos, sin_up, sin_down,
     lay, dhid, dpre, ograd, ggrad, ugrad, sums, urecv, oex,
-    wo, da, attr, att_t, attc, qbuf, dsend, datt, lse_t, part, slots, ostage, ofetch, osum, orecv, ofull, ozr,
+    wo, da, attr, att_t, attc, qbuf, dsend, datt, lse_t, part, slots, ostage, ofetch, osum, orecv, omid, ofull, ozr,
     sbuf, sobuf, dq,
     mss, mrs, ass, ars, oss, ors, pss, prs, uss, urs, zss, zrs, local, ssem,
 ):
@@ -994,6 +1245,13 @@
         pltpu.make_async_copy(attall.at[:, pl.ds(pl.multiple_of(z * width, width), width)], attc, local.at[6]),
         pltpu.make_async_copy(qkv, qbuf, local.at[7]),
     ]
+
+    def landed(i):
+        return pltpu.make_async_copy(mland.at[i], slots.at[jnp.where(z == 1, line - 1 - i, i)], local.at[9 + i])
+
+    between = (z > 0) & (z < line - 1)
+    for i in range(2):
+        pl.when(between)(lambda: landed(i).start())
     for copy in loads:
         copy.start()
     for j in range(blocks - 1):
@@ -1006,12 +1264,22 @@
     )
     pl.when(z == 0)(lambda: slots.__setitem__((0,), jnp.zeros((rows, model), BF)))
     pl.when(z == line - 1)(lambda: slots.__setitem__((line,), jnp.zeros((rows, model), BF)))
+    def onward(i, h):
+        @pl.when(z == 1)
+        def _():
+            scatter.add(line - 1 - i, h)
+            scatter.right(line - 1 - i, h).start()
+
+        @pl.when(z == line - 2)
+        def _():
+            scatter.add(i, h)
+            scatter.left(i, h).start()
+
     for copy in loads[:4]:
         copy.wait()
-    for i in range(line - 1):
-        pl.when(z == 0)(lambda: scatter.head(jnp.int32(line - 1 - i)))
-        pl.when(z == line - 1)(lambda: scatter.head(jnp.int32(i)))
-
+    for i in range(2):
+        pl.when(between)(lambda: landed(i).wait())
+    onward(0, 0)
     sums[...] = jnp.zeros_like(sums)
 
     def back(at):
@@ -1039,6 +1307,25 @@
         dsend[to] = nt(da[...], wo[pl.ds(pl.multiple_of(to * width, width), width), :]).astype(BF)
         pl.when(k < line)(lambda: away(k).start())
 
+    onward(0, 1)
+    for h in range(2):
+        onward(1, h)
+        pl.when(z == 0)(lambda: scatter.right(jnp.int32(1), h).start())
+        pl.when(z == line - 1)(lambda: scatter.left(jnp.int32(line - 2), h).start())
+
+    def relay(h):
+        @pl.when(z == 1)
+        def _():
+            scatter.copy(z, h, 0, z, 0).wait_recv()
+            scatter.add(0, h)
+            scatter.left(0, h).start()
+
+        @pl.when(z == line - 2)
+        def _():
+            scatter.copy(z, h, 0, z, line - 1).wait_recv()
+            scatter.add(line - 1, h)
+            scatter.right(line - 1, h).start()
+
     datt[pl.ds(pl.multiple_of(z * rows, rows), rows), :] = dsend[z]
     for lo, size in spans(model, 512):
         att_t[pl.ds(lo, size), :] = attr[:, pl.ds(lo, size)].T
@@ -1056,18 +1343,17 @@
         ostage[lax.rem(k, 2)] = oblock(2 * k + 1 - core).astype(BF)
         across(k).start()
 
-    planes = PlaneSum(osum, orecv, d, z, blocks, pss, prs)
+    planes = PlaneChain(osum, orecv, omid, d, z, flips, pss, prs)
 
     @pl.loop(0, blocks)
-    def _(j):
-        k = planes.chip_at(j)
+    def _(k):
         across(k).wait_recv()
         fetch = pltpu.make_async_copy(oex.at[k], ofetch, local.at[8])
         fetch.start()
         fetch.wait()
         osum[k] = (oblock(2 * k + core) + ofetch[...].astype(F32)).astype(BF)
-        pl.when(j < blocks - 1)(lambda: planes.copy(j).start())
-
+
+    planes.start()
     across(blocks - 2).wait_send()
     across(blocks - 1).wait_send()
     sum_blocks(ghalf.at[chip], grecv, ggrad, sbuf, sobuf, ssem, rows // sbuf.shape[1])
@@ -1075,7 +1361,7 @@
         frm = lax.rem(z + k, line)
         send(dsend.at[frm], datt.at[pl.ds(pl.multiple_of(frm * rows, rows), rows)], ass.at[k], ars.at[frm], d, frm).wait_recv()
 
-    scatter.relay(1)
+    relay(0)
     lanes = lax.broadcasted_iota(jnp.int32, (1, 128), 1)
     mine = (lanes < 64, lanes >= 64)
     which = lax.broadcasted_iota(jnp.int32, (16, 128), 0)
@@ -1090,13 +1376,10 @@
         )
 
     def plane_total():
-        planes.wait()
+        planes.arrive()
 
         def add(at):
-            total = osum[chip, at, :].astype(F32)
-            for j in range(blocks - 1):
-                total = total + orecv[j, at, :].astype(F32)
-            ofull[at, :] = total.astype(BF)
+            ofull[at, :] = planes.total((at, slice(None))).astype(BF)
 
         each_piece(model, 256, add)
         for k in range(1, line):
@@ -1137,9 +1420,10 @@
     @pl.loop(0, pairs)
     def _(p):
         back_pair(p)
-        pl.when(p == 1)(lambda: scatter.relay(2))
-
-    plane_total()
+        pl.when(p == 0)(lambda: planes.relay())
+        pl.when(p == 1)(lambda: relay(1))
+        pl.when(p == 2)(lambda: plane_total())
+
     ups.wait()
     sum_blocks(uhalf.at[chip], urecv, ugrad, sbuf, sobuf, ssem, rows // sbuf.shape[1])
     for h in range(2):
@@ -1158,10 +1442,14 @@
     ograd[...] = total
     for k in range(1, line):
         away(k).wait_send()
-    scatter.finish()
-
-
-def attention_backward(dn2, hid, cot, small, wout, attall, qkv, lse, mixed, ghalf, grecv, uhalf, tabs):
+    planes.finish()
+    for s in range(line):
+        for h in range(2):
+            sent = (z != s) & ((z > 0) | (s == 1)) & ((z < line - 1) | (s == line - 2))
+            pl.when(sent)(lambda: scatter.copy(s, h, 0, z, s).wait_send())
+
+
+def attention_backward(dn2, hid, cot, small, wout, attall, qkv, lse, mixed, mland, ghalf, grecv, uhalf, tabs):
     rows, model = hid.shape
     line = 4
     length = rows * line
@@ -1178,7 +1466,7 @@
             sds((width, rows), F32), sds((rows, hidden), F32), sds((rows, hidden), F32), sds((8, model), F32),
             sds((blocks - 1, rows, hidden), BF), sds((blocks, model, rows), BF),
         ),
-        in_specs=[INV, INV, INV, INV, ANY, ANY, ANY, INV, ANY, ANY, ANY, ANY, INV, INV, INV],
+        in_specs=[INV] * 4 + [ANY] * 3 + [INV] + [ANY] * 5 + [INV] * 3,
         out_specs=(INV, INV, INV, INV, ANY, ANY, INV, ANY, ANY),
         scratch_shapes=[
             pltpu.VMEM((model, model), BF),
@@ -1195,29 +1483,30 @@
             pltpu.VMEM((2, model, rows), BF),
             pltpu.VMEM((model, rows), BF),
             pltpu.VMEM((blocks, model, rows), BF),
-            pltpu.VMEM((blocks - 1, model, rows), BF),
+            pltpu.VMEM((2, model, rows), BF),
+            pltpu.VMEM((2, model // 2, rows), BF),
             pltpu.VMEM((model, rows), BF),
             pltpu.VMEM((line - 1, width, rows), BF),
             pltpu.VMEM((blocks, 64, hidden), BF),
             pltpu.VMEM((64, hidden), F32),
             pltpu.VMEM((length, 128), F32),
             dma((line, 2)), dma((line + 1, 2)), dma((line,)), dma((line,)), dma((blocks,)), dma((blocks,)),
-            dma((blocks,)), dma((blocks,)), dma((blocks,)), dma((blocks,)), dma((line,)), dma((line,)),
-            dma((10,)), dma((blocks + 1,)),
+            dma((6,)), dma((6,)), dma((blocks,)), dma((blocks,)), dma((line,)), dma((line,)),
+            dma((12,)), dma((blocks + 1,)),
         ],
         compiler_params=pltpu.CompilerParams(
             collective_id=3, has_side_effects=True, vmem_limit_bytes=62 * 1024 * 1024
         ),
         cost_estimate=pl.CostEstimate(flops=10**11, bytes_accessed=10**8, transcendentals=0),
         name="attention_backward",
-    )(dn2, hid, cot, small, wout, attall, qkv, lse, mixed, ghalf, grecv, uhalf, *tabs)
+    )(dn2, hid, cot, small, wout, attall, qkv, lse, mixed, mland, ghalf, grecv, uhalf, *tabs)
 
 
 def input_back_kernel(
     dpre, wqkv, n1, dhalf, tok, dhid, small, sums_in,
-    tgrad, qgrad, dgrad, sums, drecv, qex,
-    pbuf, wbuf, nbuf, part, slots, qstage, qfetch, qsum, qrecv, zsums, dsums, sbuf, sobuf,
-    ss, rs, xss, xrs, pss, prs, dss, drs, zss, zrs, gss, grs, local, ssem,
+    tgrad, qgrad, dgrad, gains, bout, drecv, qex,
+    pbuf, wbuf, nbuf, part, slots, qstage, qfetch, qsum, qrecv, qmid, sums, zsums, dsums, bsums, sbuf, sobuf,
+    ss, rs, xss, xrs, pss, prs, dss, drs, zss, zrs, gss, grs, bss, brs, local, ssem,
 ):
     line = 4
     rows, model = tok.shape
@@ -1232,6 +1521,8 @@
     for copy in loads:
         copy.start()
     downs = PlaneSum(dhalf, drecv, d, z, blocks, dss, drs)
+    for j in range(blocks - 1):
+        downs.copy(j).start()
     half = rows // 2
     scatter = LineScatter(
         lambda s, h: part.at[s, pl.ds(h * half, half)],
@@ -1252,12 +1543,6 @@
         scatter.head(s)
 
     loads[2].wait()
-    sums[...] = sums_in[...]
-
-    def bias(at):
-        sums[4:5, : 3 * width] += jnp.sum(pbuf[at, :].astype(F32), 0, keepdims=True)
-
-    each_piece(rows * line, 64, bias)
 
     def qblock(t):
         return lambda lo, size: tn(nbuf[:, pl.ds(pl.multiple_of(t * rows, rows), rows)], pbuf[:, pl.ds(lo, size)])
@@ -1272,12 +1557,10 @@
             qstage[k, :, pl.ds(lo, size)] = make(lo, size).astype(BF)
         across(k).start()
 
-    scatter.relay(1)
-    planes = PlaneSum(qsum, qrecv, d, z, blocks, pss, prs)
+    planes = PlaneChain(qsum, qrecv, qmid, d, z, flips, pss, prs)
 
     @pl.loop(0, blocks)
-    def _(j):
-        k = planes.chip_at(j)
+    def _(k):
         across(k).wait_recv()
         fetch = pltpu.make_async_copy(qex.at[k], qfetch, local.at[3])
         fetch.start()
@@ -1285,20 +1568,36 @@
         make = qblock(2 * k + core)
         for lo, size in spans(3 * width, 512):
             qsum[k, :, pl.ds(lo, size)] = (make(lo, size) + qfetch[:, pl.ds(lo, size)].astype(F32)).astype(BF)
-        pl.when(j < blocks - 1)(lambda: planes.copy(j).start())
-
-    for j in range(blocks - 1):
-        downs.copy(j).start()
+
+    planes.start()
+    scatter.relay(1)
+    bsums[0] = jnp.zeros(bsums.shape[1:], F32)
+
+    def bias(at):
+        bsums[0, 0:1, :] += jnp.sum(pbuf[at, :].astype(F32), 0, keepdims=True)
+
+    each_piece(rows * line, 64, bias)
+
+    def bcopy(r):
+        return send(bsums.at[0], bsums.at[r], bss.at[r], brs.at[r], d + flips[r], z)
+
+    for r in range(1, 8):
+        bcopy(r).start()
+    planes.relay()
     scatter.relay(2)
-    planes.wait()
+    planes.arrive()
     for j in range(3):
         cols = pl.ds(j * width, width)
-        total = qsum[chip, :, cols].astype(F32)
-        for i in range(blocks - 1):
-            total = total + qrecv[i, :, cols].astype(F32)
-        qgrad[j] = total
+        qgrad[j] = planes.total((slice(None), cols))
     downs.wait()
     sum_blocks(dhalf.at[chip], drecv, dgrad, sbuf, sobuf, ssem, dhalf.shape[1] // sbuf.shape[1])
+    total = jnp.zeros(bout.shape, F32)
+    for r in range(8):
+        if r:
+            bcopy(r).wait()
+        total = total + bsums[r]
+    bout[...] = total
+    sums[...] = sums_in[...]
     for h in range(2):
         scatter.arrive(h)
 
@@ -1311,27 +1610,31 @@
             sums[1:2, :] += jnp.sum(grad, 0, keepdims=True)
             tgrad[at, :] = (dhid[at, :] + norm_back(grad, standard, inverse, small[0:1, :])).astype(BF)
 
+    depth = gains.shape[1]
+
+    def columns(i):
+        return sums.at[:, pl.ds(pl.multiple_of(i * depth, 256), depth)]
+
+    def dcopy(r):
+        return send(columns(d + flips[r]), dsums.at[r], gss.at[r], grs.at[r], d + flips[r], z)
+
     def zcopy(k):
-        to = lax.rem(z + k, line)
-        return send(sums, zsums.at[k - 1], zss.at[k], zrs.at[k - 1], d, to)
-
-    def dcopy(r):
-        return send(dsums.at[0], dsums.at[r], gss.at[r], grs.at[r], d + flips[r], z)
-
+        return send(zsums.at[0], zsums.at[k], zss.at[k], zrs.at[k], d, lax.rem(z + k, line))
+
+    for r in range(1, 8):
+        dcopy(r).start()
+    total = columns(d)[...]
+    for r in range(1, 8):
+        dcopy(r).wait()
+        total = total + dsums[r]
+    zsums[0] = total
     for k in range(1, line):
         zcopy(k).start()
     for k in range(1, line):
         zcopy(k).wait()
-    dsums[0] = sums[...]
-    dsums[0, 0:4, :] = sums[0:4, :] + zsums[0, 0:4, :] + zsums[1, 0:4, :] + zsums[2, 0:4, :]
-    for r in range(1, 8):
-        dcopy(r).start()
-    for r in range(1, 8):
-        dcopy(r).wait()
-    total = dsums[0]
-    for r in range(1, 8):
-        total = total + dsums[r]
-    sums[...] = total
+        total = total + zsums[k]
+    gains[...] = total
+    planes.finish()
     for k in range(blocks):
         across(k).wait_send()
     scatter.finish()
@@ -1349,11 +1652,11 @@
     return pl.pallas_call(
         input_back_kernel,
         out_shape=(
-            sds((rows, model), BF), sds((3, rows, triple // 3), F32), sds((hidden, rows), F32), sds((8, model), F32),
-            sds((blocks - 1, hidden, rows), BF), sds((blocks, rows, triple), BF),
+            sds((rows, model), BF), sds((3, rows, triple // 3), F32), sds((hidden, rows), F32), sds((8, rows), F32),
+            sds((8, triple), F32), sds((blocks - 1, hidden, rows), BF), sds((blocks, rows, triple), BF),
         ),
         in_specs=[ANY, ANY, ANY, ANY, INV, INV, INV, INV],
-        out_specs=(INV, INV, ANY, INV, ANY, ANY),
+        out_specs=(INV, INV, ANY, INV, INV, ANY, ANY),
         scratch_shapes=[
             pltpu.VMEM((length, triple), BF),
             pltpu.VMEM((model, triple), BF),
@@ -1363,14 +1666,17 @@
             pltpu.VMEM((blocks, rows, triple), BF),
             pltpu.VMEM((rows, triple), BF),
             pltpu.VMEM((blocks, rows, triple), BF),
-            pltpu.VMEM((blocks - 1, rows, triple), BF),
-            pltpu.VMEM((line - 1, 8, model), F32),
-            pltpu.VMEM((8, 8, model), F32),
+            pltpu.VMEM((2, rows, triple), BF),
+            pltpu.VMEM((2, rows // 2, triple), BF),
+            pltpu.VMEM((8, model), F32),
+            pltpu.VMEM((line, 8, rows), F32),
+            pltpu.VMEM((8, 8, rows), F32),
+            pltpu.VMEM((8, 8, triple), F32),
             pltpu.VMEM((blocks, 352, rows), BF),
             pltpu.VMEM((352, rows), F32),
-            dma((line, 2)), dma((line + 1, 2)), dma((blocks,)), dma((blocks,)), dma((blocks,)), dma((blocks,)),
+            dma((line, 2)), dma((line + 1, 2)), dma((blocks,)), dma((blocks,)), dma((6,)), dma((6,)),
             dma((blocks,)), dma((blocks,)), dma((line,)), dma((line,)), dma((8,)), dma((8,)),
-            dma((4,)), dma((blocks + 1,)),
+            dma((8,)), dma((8,)), dma((4,)), dma((blocks + 1,)),
         ],
         compiler_params=pltpu.CompilerParams(
             collective_id=4, has_side_effects=True, vmem_limit_bytes=62 * 1024 * 1024
@@ -1381,15 +1687,16 @@
 
 
 def turn_tables(length):
-    cosine, sine = tables(length)
-    rest = HEAD_DIM - ROT
     half = ROT // 2
-    cos = jnp.concatenate([cosine, jnp.ones((length, rest), F32)], -1)
-    none = jnp.zeros((length, half), F32)
-    tail = jnp.zeros((length, rest), F32)
-    up = jnp.concatenate([none, sine[:, half:], tail], -1)
-    down = jnp.concatenate([-sine[:, :half], none, tail], -1)
-    return tuple(jnp.concatenate([t, t], -1) for t in (cos, up, down))
+    freqs = np.float32(10000.0) ** (-np.arange(0, ROT, 2, dtype=np.float32) / np.float32(ROT))
+    angles = np.arange(length, dtype=np.float32)[:, None] * freqs[None, :]
+    cos = np.ones((length, HEAD_DIM), np.float32)
+    up = np.zeros((length, HEAD_DIM), np.float32)
+    down = np.zeros((length, HEAD_DIM), np.float32)
+    cos[:, :half] = cos[:, half:ROT] = np.cos(angles)
+    up[:, half:ROT] = np.sin(angles)
+    down[:, :half] = -np.sin(angles)
+    return tuple(jnp.asarray(np.tile(t, (1, 2))) for t in (cos, up, down))
 
 
 def pack_smalls(d, model, width, qkv_bias, *vectors):
@@ -1409,32 +1716,24 @@
     down_weight, norm2_gain, norm2_shift, cotangent,
 ):
     d = lax.axis_index("dp")
-    z = lax.axis_index("tensor")
     rows, model = tokens.shape
     length = 4 * rows
     tabs = turn_tables(length)
     depth, width = qkv_weight.shape[1:]
     smalls = pack_smalls(d, model, width, qkv_bias, norm1_gain, norm1_shift, norm2_gain, norm2_shift)
     wq = qkv_weight.transpose(1, 0, 2).reshape(depth, 3 * width)
-    xall, cotall, n1, qkv, lse, attall, wqkv, small = attention_forward(tokens, cotangent, wq, smalls, tabs)
-    wout = lax.all_gather(out_weight, "tensor", axis=0, tiled=True)
-    wout = lax.all_gather(wout, "dp", axis=1, tiled=True)
-    wgate = lax.all_gather(gate_weight, "dp", axis=0, tiled=True)
-    wup = lax.all_gather(up_weight, "dp", axis=0, tiled=True)
-    wdown = lax.all_gather(down_weight, "dp", axis=1, tiled=True)
-    hidden_all = xall.astype(F32) + nn(attall, wout)
-    n2, _, _ = apply_layer_norm(hidden_all, small[2], small[3])
-    hidden = lax.dynamic_slice_in_dim(hidden_all, z * rows, rows, 0)
-    dn2, mixed, _, _, _, ghalf, uhalf, dhalf, grecv = mlp(n2.astype(BF), cotall, wgate, wup, wdown)
+    cotnear, n1, qkv, lse, attall, wqkv, small, wout, n2, hidden, wgate, wup, wdown = attention_forward(
+        tokens, cotangent, wq, out_weight, gate_weight, up_weight, down_weight, smalls, tabs
+    )
+    dn2, mixed, mland, _, _, _, ghalf, uhalf, dhalf, grecv = mlp(n2, cotangent, cotnear, wgate, wup, wdown)
     layer_output, dhid, dpre, outw_grad, gatew_grad, upw_grad, sums, _, _ = attention_backward(
-        dn2, hidden, cotangent, small, wout, attall, qkv, lse, mixed, ghalf, grecv, uhalf, tabs
-    )
-    token_gradient, qkvw_grad, downw_grad, sums, _, _ = input_backward(
+        dn2, hidden, cotangent, small, wout, attall, qkv, lse, mixed, mland, ghalf, grecv, uhalf, tabs
+    )
+    token_gradient, qkvw_grad, downw_grad, gains, bias, _, _ = input_backward(
         dpre, wqkv, n1, dhalf, tokens, dhid, small, sums
     )
-    gains = lax.dynamic_slice_in_dim(sums[:4], d * depth, depth, 1)
     part = qkv_bias.shape[1]
-    bias = sums[4, : 3 * width].reshape(3, width)
+    bias = bias[0].reshape(3, width)
     qkvb_grad = lax.dynamic_slice_in_dim(bias, d * part, part, 1)
     return (
         layer_output, token_gradient, qkvw_grad, qkvb_grad, outw_grad, gains[0], gains[1],

time: 751 us -> 569 us (0.76)
  Pallas kernels: 643 us -> 541 us
  waiting for transfers between devices: 34.7 us -> 0 us
  matrix products: 13.3 us -> 0 us
  between operations: 14.2 us -> 1.19 us
    pallas_call x1, Pallas kernels: 161 us -> 114 us  [attention_backward(): pl.pallas_call(attention_back_kernel, out_shape=(sds((rows, model), BF),...]
    pallas_call x1, Pallas kernels: 244 us -> 199 us  [attention_forward(): pl.pallas_call(attention_kernel, out_shape=(sds((line, rows, model), BF),...]
    pallas_call x1, Pallas kernels: 129 us -> 92.8 us  [input_backward(): pl.pallas_call(input_back_kernel, out_shape=(sds((rows, model), BF), sds(...]
    all_gather x5 -> x0, waiting for transfers between devices: 32.3 us -> none  [the longest x1 32.3 us: fast(): wout = lax.all_gather(out_weight, 'tensor', axis=0, tiled=True)]
    pallas_call x1, Pallas kernels: 108 us -> 135 us  [mlp(): pl.pallas_call(mlp_kernel, out_shape=(sds((rows, model), F32), sds((lengt...]
    dot_general x1 -> x0, matrix products: 13.3 us -> none  [nn(): return jnp.dot(a, b, preferred_element_type=F32)]
  transfers between devices with their start and end apart: 5 -> 0, of which waited for: 1 -> 0; matrix products, arithmetic and copies ran while one was open for 4% -> 0% of each run, Pallas kernels for 33% -> 0%
where the time goes in v3:
time: 569 us; the launch traced here: 560 us
  Pallas kernels  541 us (95%)
  local copies, waits for them, and re-layouts  17.6 us (3%)
    pallas_call x1, Pallas kernels, attention_forward(): pl.pallas_call(attention_kernel, out_shape=(sds((line, rows, model), BF),...  199 us
    pallas_call x1, Pallas kernels, mlp(): pl.pallas_call(mlp_kernel, out_shape=(sds((rows, model), F32), sds((lengt...  135 us
    pallas_call x1, Pallas kernels, attention_backward(): pl.pallas_call(attention_back_kernel, out_shape=(sds((rows, model), BF),...  114 us
    pallas_call x1, Pallas kernels, input_backward(): pl.pallas_call(input_back_kernel, out_shape=(sds((rows, model), BF), sds(...  92.8 us
    unnamed x32, local copies, waits for them, and re-layouts  12.7 us

profile of v3, /device:TPU:0, one launch (start us, length us, event | category | flops | bytes accessed | tf_op | source)
XLA Modules:
  0.0 560.3 jit_solution(8926083684887916398)
XLA Ops:
  0.6 0.0 copy-start
  0.7 0.1 pad.7.clone
  0.8 0.5 copy-done
  1.3 0.7 broadcast_bitcast_fusion.2
  2.0 0.7 broadcast_bitcast_fusion.1
  2.7 0.7 broadcast_bitcast_fusion
  3.3 0.1 maximum_select_fusion
  3.4 0.7 tile.16
  4.1 0.1 tile.17
  4.2 0.7 maximum_maximum_fusion.smalls
  4.9 1.4 copy.28
  6.3 1.2 copy.29.wq
  7.5 199.2 %attention_forward.1 = (bf16[4,256,2048]{2,1,0:T(8,128)(2,1)}, bf16[1024,2048]{1,0:T(8,128)(2,1)}, bf16[3,4,1024,128]{3,2,1,0:T(8,128)(2,1)}, f32[1024,128]{1,0:...) custom-call(bf16[256,2048]{1,0:T(8,128)(2,1)} %tok.3, ...), custom_call_target="tpu_custom_call" | custom-call | flops 199999995904 | bytes 100000000 | tf_op jit(solution)/shard_map/attention_forward/pallas_call | solution.py:441
  206.7 135.2 %mlp.1 = (f32[256,2048]{1,0:T(8,128)}, bf16[1024,2048]{1,0:T(8,128)(2,1)}, bf16[2,256,2048]{2,1,0:T(8,128)(2,1)}, bf16[4,256,1408]{2,1,0:T(8,128)(2,1)}, bf16[4,...) custom-call(bf16[1024,2048]{1,0:T(8,128)(2,1)} %get-tuple-element.44, ...), custom_call_target="tpu_custom_call" | custom-call | flops 99999997952 | bytes 100000000 | tf_op jit(solution)/shard_map/mlp/pallas_call | solution.py:1064
  341.9 113.5 %attention_backward.1 = (bf16[256,2048]{1,0:T(8,128)(2,1)}, f32[256,2048]{1,0:T(8,128)}, bf16[1024,1536]{1,0:T(8,128)(2,1)}, f32[512,256]{1,0:T(8,128)}, f32[256...) custom-call(f32[256,2048]{1,0:T(8,128)} %get-tuple-element.49.dn2, ...), custom_call_target="tpu_custom_call" | custom-call | flops 99999997952 | bytes 100000000 | tf_op jit(solution)/shard_map/attention_backward/pallas_call | solution.py:1462
  455.4 0.0 copy-start.6
  455.4 92.8 %input_backward.1 = (bf16[256,2048]{1,0:T(8,128)(2,1)}, f32[3,256,512]{2,1,0:T(8,128)}, f32[1408,256]{1,0:T(8,128)}, f32[8,256]{1,0:T(8,128)}, f32[8,1536]{1,0:T...) custom-call(bf16[1024,1536]{1,0:T(8,128)(2,1)} %get-tuple-element.62.dpre, ...), custom_call_target="tpu_custom_call" | custom-call | flops 99999997952 | bytes 100000000 | tf_op jit(solution)/shard_map/input_backward/pallas_call | solution.py:1652
  548.2 0.0 copy-start.2
  548.2 1.4 fusion.4
  549.7 0.8 slice_reduce_fusion
  550.5 0.7 constant_dynamic-slice_fusion
  551.2 0.0 copy-done.6
  551.2 1.0 copy.41
  552.1 0.0 copy-start.7
  552.1 0.0 copy-start.4
  552.1 2.4 copy.42
  554.6 0.0 copy-done.2
  554.6 0.0 copy-start.3
  554.6 1.1 copy.43
  555.7 0.0 copy-done.7
  555.7 0.8 copy.44
  556.5 0.0 copy-done.4
  556.5 0.0 copy-start.5
  556.5 0.0 copy-start.1
  556.5 1.1 copy.45
  557.6 0.0 copy-done.3
  557.6 1.1 copy.46
  558.7 0.0 copy-done.5
  558.7 1.1 copy.47
  559.8 0.0 copy-done.1
  (9 shorter events, 0.1 us)
Async XLA Ops:
  0.6 0.7 copy-start
  455.4 95.8 %copy-start.6 = (bf16[256,2048]{1,0:T(8,128)(2,1)S(1)}, bf16[256,2048]{1,0:T(8,128)(2,1)}, u32[]{:S(2)}) copy-start(bf16[256,2048]{1,0:T(8,128)(2,1)} %get-tuple-element.92) | copy-start | bytes 3145732
  548.2 6.4 %copy-start.2 = (f32[3,256,512]{2,1,0:T(8,128)S(1)}, f32[3,256,512]{2,1,0:T(8,128)}, u32[]{:S(2)}) copy-start(f32[3,256,512]{2,1,0:T(8,128)} %get-tuple-element.94) | copy-start | bytes 4718596
  552.1 3.6 copy-start.7
  552.1 4.4 copy-start.4
  554.6 3.1 copy-start.3
  556.5 2.2 copy-start.5
  556.5 3.3 copy-start.1

commit v4 on v3

--- a/solution.py
+++ b/solution.py
@@ -152,19 +152,20 @@
     return lax.rem(lax.div(code, power), 4)
 
 
-def turn(u, cos, sin_up, sin_down, sign=1.0):
-    moved = pltpu.roll(u, 8, 1) * sin_up + pltpu.roll(u, 120, 1) * sin_down
+def turn(u, cos, sin, sign=1.0):
+    low = lax.rem(lax.broadcasted_iota(jnp.int32, (1, 128), 1), HEAD_DIM) < ROT // 2
+    moved = jnp.where(low, pltpu.roll(u, 128 - ROT // 2, 1), pltpu.roll(u, ROT // 2, 1)) * sin
     return u * cos + moved if sign > 0 else u * cos - moved
 
 
 def attention_kernel(
-    tok, cot, wq, ow, gw, uw, dw, smalls, cos, sin_up, sin_down,
-    cotnear, n1, qkv, lse, attall, wqkv, small_sum, wout, n2, hidden, wgate, wup, wdown,
-    xbuf, n1buf, wbuf, qbuf, attv, wz, wo, acc, smbuf,
+    tok, cot, wq, ow, gw, uw, dw, smalls, cos, sin,
+    cotnear, n1, qkv, lse_t, attall, wqkv, small_sum, wout, n2, hidden, wgate, wup, wdown,
+    xbuf, n1buf, wbuf, qbuf, attv, wz, wo, acc, smbuf, lse,
     tss, trs, css, crs, ass, ars, mss, mrs, yss, yrs, pss, prs, local,
 ):
     rows, model = tok.shape
-    width = wq.shape[1] // 3
+    width = wq.shape[2]
     pairs = width // 128
     line = 4
     d, z, flips = place()
@@ -172,13 +173,17 @@
 
     tok_in = pltpu.make_async_copy(tok, xbuf.at[z], local.at[0])
     tok_in.start()
-    depth = wq.shape[0]
+    depth = wq.shape[1]
 
     def wblock(i):
         return wbuf.at[pl.ds(pl.multiple_of(i * depth, 256), depth), :]
 
-    w_in = pltpu.make_async_copy(wq, wblock(d), local.at[2])
-    w_in.start()
+    w_in = [
+        pltpu.make_async_copy(wq.at[j], wblock(d).at[:, pl.ds(j * width, width)], local.at[(2, 1, 13)[j]])
+        for j in range(3)
+    ]
+    for copy in w_in:
+        copy.start()
     tall = ow.shape[0]
 
     def oview(s, h):
@@ -206,7 +211,7 @@
     planes = [
         PlaneGather(src, view, d, z, flips, pss.at[i], prs.at[i])
         for i, (src, view) in enumerate((
-            (wq, wblock),
+            (wblock(d), wblock),
             (wz, oblock),
             (gw, lambda i: rows_of(wgate, i)),
             (uw, lambda i: rows_of(wup, i)),
@@ -238,6 +243,8 @@
     tok_in.wait()
     for h in range(2):
         toks.start(h)
+    for copy in w_in:
+        copy.wait()
     qkv_plane.start()
     o_in.wait()
     outs_z.start(0)
@@ -268,7 +275,7 @@
             for p in range(pairs):
                 part = pre[:, p * 128 : (p + 1) * 128]
                 if j < 2:
-                    part = turn(part, cos[at, :], sin_up[at, :], sin_down[at, :])
+                    part = turn(part, cos[at, :], sin[at, :])
                 qbuf[j, p, at, :] = part.astype(BF)
 
     normalise(z)
@@ -284,7 +291,6 @@
     outs_z.step(2, 0)
     normalise(arrival(z, 2))
     gate_plane.relay()
-    w_in.wait()
     qkv_plane.arrive()
 
     @pl.loop(0, line)
@@ -351,6 +357,7 @@
         attend(p)
         atts.start(p)
 
+    lse_t[...] = lse[...].T
     up_plane.start()
     for p in range(pairs):
         atts.step(1, p)
@@ -388,6 +395,13 @@
     up_plane.pass_on()
     for p in range(pairs):
         atts.step(3, p)
+    inner = (z > 0) & (z < line - 1)
+
+    @pl.when(inner)
+    def _():
+        cots.copy(z - 1, 0, 0).start()
+        cots.copy(z + 1, 0, 1).start()
+
     keep_att = pltpu.make_async_copy(attv, attall, local.at[7])
     keep_att.start()
     last = arrival(z, line - 1)
@@ -418,6 +432,14 @@
     for gather in (toks, atts, outs_z):
         gather.finish()
     cots.finish(0, 1)
+
+    @pl.when(inner)
+    def _():
+        cots.copy(z - 1, 0, 0).wait_send()
+        cots.copy(z + 1, 0, 1).wait_send()
+
+    pl.when(z >= 2)(lambda: cots.copy(z - 2, 0, 0).wait_recv())
+    pl.when(z + 2 < line)(lambda: cots.copy(z + 2, 0, 1).wait_recv())
     for plane in (gate_plane, up_plane, down_plane):
         plane.arrive()
     for plane in planes:
@@ -432,8 +454,7 @@
     rows, model = tok.shape
     line = 4
     length = rows * line
-    depth, width = wq.shape
-    width //= 3
+    _, depth, width = wq.shape
     pairs = width // 128
     dp = model // depth
     hidden = gw.shape[1]
@@ -442,12 +463,12 @@
         attention_kernel,
         out_shape=(
             sds((line, rows, model), BF), sds((length, model), BF),
-            sds((3, pairs, length, 128), BF), sds((length, 128), F32), sds((length, model), BF),
+            sds((3, pairs, length, 128), BF), sds((128, length), F32), sds((length, model), BF),
             sds((model, 3 * width), BF), sds((16, model), F32),
             sds((model, model), BF), sds((length, model), BF), sds((rows, model), F32),
             sds((model, hidden), BF), sds((model, hidden), BF), sds((hidden, model), BF),
         ),
-        in_specs=[ANY] * 7 + [INV] * 4,
+        in_specs=[ANY] * 7 + [INV] * 3,
         out_specs=(ANY, ANY, ANY, INV, ANY, ANY, INV) + (ANY,) * 6,
         scratch_shapes=[
             pltpu.VMEM((line, rows, model), BF),
@@ -459,6 +480,7 @@
             pltpu.VMEM((model, model), BF),
             pltpu.VMEM((length, model), F32),
             pltpu.VMEM((dp, 16, model), BF),
+            pltpu.VMEM((length, 128), F32),
             pltpu.SemaphoreType.DMA((2, line, 2)),
             pltpu.SemaphoreType.DMA((line, 2)),
             pltpu.SemaphoreType.DMA((2, line, 2)),
@@ -883,11 +905,22 @@
             cot if k == 0 else cotnear.at[s], cbuf.at[pl.ds(pl.multiple_of(s * rows, rows), rows)], local.at[5 + k]
         )
 
-    for h in range(2):
+    for h in (1, 0):
         @pl.when((z > 0) & (z < line - 1))
         def _():
-            cots.copy(z - 1, h, 0, cotnear.at[z - 1, pl.ds(h * half, half)]).start()
-            cots.copy(z + 1, h, 1, cotnear.at[z + 1, pl.ds(h * half, half)]).start()
+            if h == 1:
+                cots.copy(z - 1, h, 0, cotnear.at[z - 1, pl.ds(h * half, half)]).start()
+                cots.copy(z + 1, h, 1, cotnear.at[z + 1, pl.ds(h * half, half)]).start()
+            else:
+                pl.when(z == 2)(lambda: cots.copy(z - 2, h, 0, cotnear.at[z - 2, pl.ds(0, half)]).start())
+                pl.when(z == 1)(lambda: cots.copy(z + 2, h, 1, cotnear.at[z + 2, pl.ds(0, half)]).start())
+    def first_half(s, k):
+        return pltpu.make_async_copy(
+            cotnear.at[s, pl.ds(0, half)], cbuf.at[pl.ds(pl.multiple_of(s * rows, rows), half)], local.at[8 + k]
+        )
+
+    pl.when(z >= 2)(lambda: first_half(z - 2, 0).start())
+    pl.when(z + 2 < line)(lambda: first_half(z + 2, 1).start())
     near(z, 0).start()
     pl.when(z > 0)(lambda: near(z - 1, 1).start())
     pl.when(z < line - 1)(lambda: near(z + 1, 2).start())
@@ -924,19 +957,53 @@
         for lo, size in spans(model, 512):
             mixbuf[lax.rem(i, 2), :, pl.ds(lo, size)] = nn(act[...], dw[:, pl.ds(lo, size)]).astype(BF)
         mixed_out(i).start()
-
-        @pl.when(i >= 1)
+        mixed_out(i).wait()
+        pl.when(at_end & (i < 2))(lambda: mixed_ahead(i).start())
+        pl.when(i == 1)(lambda: cots.step(2, 1))
+
+    def add_mixed(s, slot, send_slot, to, lands):
+        at = pl.ds(pl.multiple_of(s * rows, rows), rows)
+        ins = [
+            pltpu.make_async_copy(mixed.at[at], mixbuf.at[0], mixsem.at[0]),
+            pltpu.make_async_copy(mland.at[slot], mixbuf.at[1], mixsem.at[1]),
+        ]
+        for copy in ins:
+            copy.start()
+        for copy in ins:
+            copy.wait()
+
+        @pl.loop(0, rows // 32)
+        def _(i):
+            piece = pl.ds(pl.multiple_of(i * 32, 32), 32)
+            mixbuf[0, piece, :] = (mixbuf[0, piece, :].astype(F32) + mixbuf[1, piece, :].astype(F32)).astype(BF)
+
+        back = pltpu.make_async_copy(mixbuf.at[0], mixed.at[at], mixsem.at[0])
+        back.start()
+        back.wait()
+        send(mixed.at[at], mland.at[lands], lss.at[send_slot], lrs.at[lands], d, to).start()
+
+    def landing(slot, send_slot):
+        return send(mland.at[slot], mland.at[slot], lss.at[send_slot], lrs.at[slot], d, z)
+
+    other = line - 1 - z
+    edge = jnp.where(z == 1, 0, line - 1)
+
+    def mixed_on(i):
+        @pl.when(~at_end)
         def _():
-            mixed_out(i - 1).wait()
-            pl.when(at_end & (i <= 2))(lambda: mixed_ahead(i - 1).start())
-
-        @pl.when(i == line - 2)
+            landing(i, i).wait_recv()
+            add_mixed(line - 1 - edge if i == 0 else other, i, 2 + i, other, 2 + i)
+
+    def mixed_relay():
+        @pl.when(~at_end)
         def _():
-            for h in range(2):
-                cots.step(2, h)
-
-    mixed_out(line - 1).wait()
+            landing(2, 2).wait_recv()
+            add_mixed(edge, 2, 0, edge, 3)
+
+    mixed_on(0)
     near(z, 0).wait()
+    pl.when(z >= 2)(lambda: first_half(z - 2, 0).wait())
+    pl.when(z + 2 < line)(lambda: first_half(z + 2, 1).wait())
     pl.when(z > 0)(lambda: near(z - 1, 1).wait())
     pl.when(z < line - 1)(lambda: near(z + 1, 2).wait())
     for h in range(2):
@@ -956,7 +1023,6 @@
             part[s, :, cols] = (nt(dga[at, :], gw[cols, :]) + nt(dup[at, :], uw[cols, :])).astype(BF)
         scatter.head(s)
 
-    scatter.relay(1)
     blocks = model // rows // 2
 
     def exchanged(m):
@@ -1030,10 +1096,13 @@
                 onward(j).start()
         return onward
 
+    mixed_on(1)
     onward = exchanged(0)
-
+    scatter.relay(1)
+    mixed_relay()
+
+    exchanged(1)
     scatter.relay(2)
-    exchanged(1)
     exchanged(2)
     for h in range(2):
         scatter.arrive(h)
@@ -1046,8 +1115,12 @@
     scatter.finish()
     for i in range(2):
         pl.when(at_end)(lambda: mixed_ahead(i).wait_send())
-        pl.when(~at_end)(lambda: mixed_ahead(i).wait_recv())
-    cots.finish(1, line - 1)
+    for i in (0, 2, 3):
+        pl.when(~at_end)(lambda: landing(3, i).wait_send())
+    landing(3, 3).wait_recv()
+    for k, h in ((1, 1), (2, 0), (2, 1)):
+        pl.when((z - k >= 0) & (z < line - 1))(lambda: cots.copy(z - k, h, 0).wait_send())
+        pl.when((z + k < line) & (z > 0))(lambda: cots.copy(z + k, h, 1).wait_send())
     for j in range(blocks - 1):
         onward(j).wait()
 
@@ -1064,7 +1137,7 @@
     return pl.pallas_call(
         mlp_kernel,
         out_shape=(
-            sds((rows, model), F32), sds((length, model), BF), sds((2, rows, model), BF),
+            sds((rows, model), F32), sds((length, model), BF), sds((4, rows, model), BF),
             wide, wide, tall, wide, wide, tall, sds((blocks - 1, rows, hidden), BF),
         ),
         in_specs=[ANY] * 6,
@@ -1090,9 +1163,9 @@
             pltpu.SemaphoreType.DMA((line + 1, 2)),
             pltpu.SemaphoreType.DMA((2, line, 2)),
             pltpu.SemaphoreType.DMA((line, 2)),
-            pltpu.SemaphoreType.DMA((2,)),
-            pltpu.SemaphoreType.DMA((2,)),
-            pltpu.SemaphoreType.DMA((8,)),
+            pltpu.SemaphoreType.DMA((4,)),
+            pltpu.SemaphoreType.DMA((4,)),
+            pltpu.SemaphoreType.DMA((10,)),
             pltpu.SemaphoreType.DMA((2,)),
             pltpu.SemaphoreType.DMA((2,)),
             pltpu.SemaphoreType.DMA((3, blocks)),
@@ -1130,21 +1203,21 @@
 
 
 class PlaneSum:
-    def __init__(self, half, recv, d, z, blocks, send_sems, recv_sems):
-        self.half, self.recv, self.d, self.z, self.blocks = half, recv, d, z, blocks
+    def __init__(self, half, recv, d, z, flips, send_sems, recv_sems):
+        self.half, self.recv, self.d, self.z, self.flips = half, recv, d, z, flips
         self.ss, self.rs = send_sems, recv_sems
-        self.chip, self.core = lax.div(d, 2), lax.rem(d, 2)
-
-    def chip_at(self, j):
-        return lax.rem(self.chip + 1 + j, self.blocks)
-
-    def copy(self, j):
-        k, to = self.chip_at(j), self.blocks - 2 - j
-        return send(self.half.at[k], self.recv.at[to], self.ss.at[j], self.rs.at[to], 2 * k + self.core, self.z)
+
+    def copy(self, r):
+        to, slot = self.d + self.flips[r], r // 2 - 1
+        return send(self.half.at[lax.div(to, 2)], self.recv.at[slot], self.ss.at[slot], self.rs.at[slot], to, self.z)
+
+    def start(self, *which):
+        for r in which:
+            self.copy(r).start()
 
     def wait(self):
-        for j in range(self.blocks - 1):
-            self.copy(j).wait()
+        for r in (2, 4, 6):
+            self.copy(r).wait()
 
 
 class PlaneChain:
@@ -1198,35 +1271,55 @@
             self.copy(key).wait_send()
 
 
-def sum_blocks(own, recv, out, buf, obuf, sems, pieces):
-    count = recv.shape[0]
-    rows = buf.shape[1]
-
-    @pl.loop(0, pieces)
-    def _(i):
+class BlockSum:
+    def __init__(self, own, recv, bufs, stage, out, in_sems, out_sems):
+        self.ins = [own] + [recv.at[j] for j in range(recv.shape[0])]
+        self.bufs, self.stage, self.out, self.in_sems, self.out_sems = bufs, stage, out, in_sems, out_sems
+
+    def copies(self):
+        return [pltpu.make_async_copy(a, b, self.in_sems.at[i]) for i, (a, b) in enumerate(zip(self.ins, self.bufs))]
+
+    def fetch(self):
+        for copy in self.copies():
+            copy.start()
+
+    def store(self, i):
+        rows = self.stage.shape[1]
         at = pl.ds(pl.multiple_of(i * rows, rows), rows)
-        ins = [pltpu.make_async_copy(own.at[at], buf.at[0], sems.at[0])] + [
-            pltpu.make_async_copy(recv.at[j, at], buf.at[j + 1], sems.at[j + 1]) for j in range(count)
-        ]
-        for copy in ins:
-            copy.start()
-        for copy in ins:
+        return pltpu.make_async_copy(self.stage.at[lax.rem(i, 2)], self.out.at[at], self.out_sems.at[lax.rem(i, 2)])
+
+    def add(self):
+        for copy in self.copies():
             copy.wait()
-        total = buf[0].astype(F32)
-        for j in range(count):
-            total = total + buf[j + 1].astype(F32)
-        obuf[...] = total
-        back = pltpu.make_async_copy(obuf, out.at[at], sems.at[count + 1])
-        back.start()
-        back.wait()
+        rows = self.stage.shape[1]
+        pieces = self.out.shape[0] // rows
+        small = 32
+
+        @pl.loop(0, pieces)
+        def _(i):
+            pl.when(i >= 2)(lambda: self.store(i - 2).wait())
+
+            @pl.loop(0, rows // small)
+            def _(j):
+                at = pl.ds(pl.multiple_of(i * rows + j * small, small), small)
+                total = self.bufs[0][at, :].astype(F32)
+                for buf in self.bufs[1:]:
+                    total = total + buf[at, :].astype(F32)
+                self.stage[lax.rem(i, 2), pl.ds(pl.multiple_of(j * small, small), small), :] = total
+
+            self.store(i).start()
+
+        self.store(jnp.int32(pieces - 2)).wait()
+        self.store(jnp.int32(pieces - 1)).wait()
 
 
 def attention_back_kernel(
-    dn2, hid, cot, small, wout, attall, qkv, lse, mixed, mland, ghalf, grecv, uhalf, cos, sin_up, sin_down,
-    lay, dhid, dpre, ograd, ggrad, ugrad, sums, urecv, oex,
-    wo, da, attr, att_t, attc, qbuf, dsend, datt, lse_t, part, slots, ostage, ofetch, osum, orecv, omid, ofull, ozr,
-    sbuf, sobuf, dq,
-    mss, mrs, ass, ars, oss, ors, pss, prs, uss, urs, zss, zrs, local, ssem,
+    hid, small, lse_t, cos, sin, dn2, cot, tok, wout, attall, qkv, mixed, mland, ghalf, grecv, uhalf, dhalf, wqkv, n1,
+    tgrad, ograd, gains, bout, lay, ggrad, ugrad, dgrad, qgrad, urecv, drecv, oex, qex,
+    wo, da, dhid, attr, att_t, attc, qbuf, dsend, datt, part, slots, marr, ofull, osum, orecv, omid, ozr,
+    dq, dpre, nbuf, qstage, qfetch, qsum, qrecv, qmid, wide_sum, tall_sum, qtotal, sums, zsums, dsums, bsums,
+    mss, mrs, ass, ars, oss, ors, pss, prs, uss, urs, zss, zrs,
+    ss, rs, xss, xrs, qss, qrs, dss, drs, yss, yrs, gss, grs, bss, brs, local, tsem, fsem, gsem,
 ):
     line = 4
     rows, model = hid.shape
@@ -1234,134 +1327,122 @@
     width = attc.shape[1]
     pairs = width // 128
     blocks = model // rows // 2
+    half = rows // 2
     d, z, flips = place()
-    greet(d, z, flips, line, (1, 2, 4, 6))
-    core, chip = lax.rem(d, 2), lax.div(d, 2)
-    ups = PlaneSum(uhalf, urecv, d, z, blocks, uss, urs)
-    loads = [pltpu.make_async_copy(mixed.at[pl.ds(s * rows, rows)], part.at[s], local.at[s]) for s in range(line)]
-    loads += [
+    greet(d, z, flips, line, range(1, 8))
+    core = lax.rem(d, 2)
+    ups = PlaneSum(uhalf, urecv, d, z, flips, uss, urs)
+    downs = PlaneSum(dhalf, drecv, d, z, flips, dss, drs)
+    loads = [
         pltpu.make_async_copy(wout, wo, local.at[4]),
         pltpu.make_async_copy(attall.at[pl.ds(pl.multiple_of(z * rows, rows), rows)], attr, local.at[5]),
         pltpu.make_async_copy(attall.at[:, pl.ds(pl.multiple_of(z * width, width), width)], attc, local.at[6]),
         pltpu.make_async_copy(qkv, qbuf, local.at[7]),
     ]
-
-    def landed(i):
-        return pltpu.make_async_copy(mland.at[i], slots.at[jnp.where(z == 1, line - 1 - i, i)], local.at[9 + i])
-
-    between = (z > 0) & (z < line - 1)
-    for i in range(2):
-        pl.when(between)(lambda: landed(i).start())
+    rows_in = [pltpu.make_async_copy(dn2, dhid, local.at[11]), pltpu.make_async_copy(cot, da, local.at[12])]
+    for copy in rows_in:
+        copy.start()
+
+    at_end = (z == 0) | (z == line - 1)
+    inner = jnp.where(z == 0, 1, line - 2)
+
+    def mixed_last(h):
+        at = pl.ds(pl.multiple_of(inner * rows + h * half, half), half)
+        return send(mixed.at[at], marr.at[pl.ds(h * half, half)], mss.at[h], mrs.at[h], d, inner)
+
+    pl.when(at_end)(lambda: mixed_last(0).start())
+    pl.when(at_end)(lambda: marr.__setitem__(Ellipsis, jnp.zeros((rows, model), BF)))
     for copy in loads:
         copy.start()
-    for j in range(blocks - 1):
-        ups.copy(j).start()
-    half = rows // 2
-    scatter = LineScatter(
-        lambda s, h: part.at[s, pl.ds(h * half, half)],
-        lambda i, h: slots.at[i, pl.ds(h * half, half)],
-        2, d, z, line, mss, mrs,
-    )
-    pl.when(z == 0)(lambda: slots.__setitem__((0,), jnp.zeros((rows, model), BF)))
-    pl.when(z == line - 1)(lambda: slots.__setitem__((line,), jnp.zeros((rows, model), BF)))
-    def onward(i, h):
-        @pl.when(z == 1)
-        def _():
-            scatter.add(line - 1 - i, h)
-            scatter.right(line - 1 - i, h).start()
-
-        @pl.when(z == line - 2)
-        def _():
-            scatter.add(i, h)
-            scatter.left(i, h).start()
-
-    for copy in loads[:4]:
+    ups.start(2, 4)
+
+    def chain(part, slots, send_sems, recv_sems):
+        pl.when(z == 0)(lambda: slots.__setitem__((0,), jnp.zeros((rows, model), BF)))
+        pl.when(z == line - 1)(lambda: slots.__setitem__((line,), jnp.zeros((rows, model), BF)))
+        return LineScatter(
+            lambda s, h: part.at[s, pl.ds(h * half, half)],
+            lambda i, h: slots.at[i, pl.ds(h * half, half)],
+            2, d, z, line, send_sems, recv_sems,
+        )
+
+    for copy in rows_in:
         copy.wait()
-    for i in range(2):
-        pl.when(between)(lambda: landed(i).wait())
-    onward(0, 0)
     sums[...] = jnp.zeros_like(sums)
 
     def back(at):
-        grad = dn2[at, :]
+        grad = dhid[at, :]
         standard, inverse = norm_parts(hid[at, :])
         sums[2:3, :] += jnp.sum(grad * standard, 0, keepdims=True)
         sums[3:4, :] += jnp.sum(grad, 0, keepdims=True)
-        total = cot[at, :].astype(F32) + norm_back(grad, standard, inverse, small[2:3, :])
+        total = da[at, :].astype(F32) + norm_back(grad, standard, inverse, small[2:3, :])
         dhid[at, :] = total
         da[at, :] = total.astype(BF)
 
     each_piece(rows, 32, back)
-    for copy in loads[4:]:
+    for copy in loads:
         copy.wait()
 
-    def away(k):
+    def away(k, p):
         to = lax.rem(z + k, line)
+        cols = pl.ds(p * 128, 128)
         return send(
-            dsend.at[to], datt.at[pl.ds(pl.multiple_of(z * rows, rows), rows)], ass.at[k], ars.at[z], d, to
+            dsend.at[to, :, cols], datt.at[pl.ds(pl.multiple_of(z * rows, rows), rows), cols],
+            ass.at[k, p], ars.at[z, p], d, to,
+        )
+
+    def taken(k, p):
+        frm = lax.rem(z + k, line)
+        cols = pl.ds(pl.multiple_of(p * 128, 128), 128)
+        return send(
+            dsend.at[frm, :, cols], datt.at[pl.ds(pl.multiple_of(frm * rows, rows), rows), cols],
+            ass.at[k, p], ars.at[frm, p], d, frm,
         )
 
     @pl.loop(1, line + 1)
     def _(k):
         to = lax.rem(z + k, line)
         dsend[to] = nt(da[...], wo[pl.ds(pl.multiple_of(to * width, width), width), :]).astype(BF)
-        pl.when(k < line)(lambda: away(k).start())
-
-    onward(0, 1)
-    for h in range(2):
-        onward(1, h)
-        pl.when(z == 0)(lambda: scatter.right(jnp.int32(1), h).start())
-        pl.when(z == line - 1)(lambda: scatter.left(jnp.int32(line - 2), h).start())
-
-    def relay(h):
-        @pl.when(z == 1)
-        def _():
-            scatter.copy(z, h, 0, z, 0).wait_recv()
-            scatter.add(0, h)
-            scatter.left(0, h).start()
-
-        @pl.when(z == line - 2)
-        def _():
-            scatter.copy(z, h, 0, z, line - 1).wait_recv()
-            scatter.add(line - 1, h)
-            scatter.right(line - 1, h).start()
-
+
+    for p in range(pairs):
+        for k in range(1, line):
+            away(k, p).start()
+    pl.when(at_end)(lambda: mixed_last(1).start())
+    weights_in = pltpu.make_async_copy(wqkv, wo.at[:, pl.ds(0, 3 * width)], local.at[4])
+    weights_in.start()
     datt[pl.ds(pl.multiple_of(z * rows, rows), rows), :] = dsend[z]
     for lo, size in spans(model, 512):
         att_t[pl.ds(lo, size), :] = attr[:, pl.ds(lo, size)].T
-    lse_t[...] = lse[...].T
+    tok_in = pltpu.make_async_copy(tok, attr, local.at[6])
+    tok_in.start()
 
     def oblock(t):
         return nn(att_t[...], da[:, pl.ds(pl.multiple_of(t * rows, rows), rows)])
 
-    def across(k):
-        return send(ostage.at[lax.rem(k, 2)], oex.at[k], oss.at[k], ors.at[k], d + flips[1], z)
+    def ostage(k):
+        return wo.at[:, pl.ds(pl.multiple_of(3 * width + lax.rem(k, 2) * rows, rows), rows)]
+
+    def oacross(k):
+        return send(ostage(k), oex.at[k], oss.at[k], ors.at[k], d + flips[1], z)
 
     @pl.loop(0, blocks)
     def _(k):
-        pl.when(k >= 2)(lambda: across(k - 2).wait_send())
-        ostage[lax.rem(k, 2)] = oblock(2 * k + 1 - core).astype(BF)
-        across(k).start()
-
-    planes = PlaneChain(osum, orecv, omid, d, z, flips, pss, prs)
+        pl.when(k >= 2)(lambda: oacross(k - 2).wait_send())
+        ostage(k)[...] = oblock(2 * k + 1 - core).astype(BF)
+        oacross(k).start()
+
+    oplanes = PlaneChain(osum, orecv, omid, d, z, flips, pss, prs)
 
     @pl.loop(0, blocks)
     def _(k):
-        across(k).wait_recv()
-        fetch = pltpu.make_async_copy(oex.at[k], ofetch, local.at[8])
+        oacross(k).wait_recv()
+        fetch = pltpu.make_async_copy(oex.at[k], ofull, local.at[8])
         fetch.start()
         fetch.wait()
-        osum[k] = (oblock(2 * k + core) + ofetch[...].astype(F32)).astype(BF)
-
-    planes.start()
-    across(blocks - 2).wait_send()
-    across(blocks - 1).wait_send()
-    sum_blocks(ghalf.at[chip], grecv, ggrad, sbuf, sobuf, ssem, rows // sbuf.shape[1])
-    for k in range(1, line):
-        frm = lax.rem(z + k, line)
-        send(dsend.at[frm], datt.at[pl.ds(pl.multiple_of(frm * rows, rows), rows)], ass.at[k], ars.at[frm], d, frm).wait_recv()
-
-    relay(0)
+        osum[k] = (oblock(2 * k + core) + ofull[...].astype(F32)).astype(BF)
+
+    oplanes.start()
+    oacross(blocks - 2).wait_send()
+    oacross(blocks - 1).wait_send()
     lanes = lax.broadcasted_iota(jnp.int32, (1, 128), 1)
     mine = (lanes < 64, lanes >= 64)
     which = lax.broadcasted_iota(jnp.int32, (16, 128), 0)
@@ -1376,10 +1457,10 @@
         )
 
     def plane_total():
-        planes.arrive()
+        oplanes.arrive()
 
         def add(at):
-            ofull[at, :] = planes.total((at, slice(None))).astype(BF)
+            ofull[at, :] = oplanes.total((at, slice(None))).astype(BF)
 
         each_piece(model, 256, add)
         for k in range(1, line):
@@ -1412,200 +1493,161 @@
                 ds = (probs * (dprobs - inner[a : a + 1, lo:])).astype(BF)
                 dk += nn(ds, qm)
                 dq[pl.ds(lo, count), :] += tn(ds, km)
-            dk = turn(dk, cos[at, :], sin_up[at, :], sin_down[at, :], -1.0)
+            dk = turn(dk, cos[at, :], sin[at, :], -1.0)
             dpre[at, pl.ds(pl.multiple_of(width + p * 128, 128), 128)] = dk.astype(BF)
             dpre[at, pl.ds(pl.multiple_of(2 * width + p * 128, 128), 128)] = dv.astype(BF)
-        dpre[:, cols] = turn(dq[...] * scale, cos[...], sin_up[...], sin_down[...], -1.0).astype(BF)
+        dpre[:, cols] = turn(dq[...] * scale, cos[...], sin[...], -1.0).astype(BF)
 
     @pl.loop(0, pairs)
     def _(p):
+        for k in range(1, line):
+            taken(k, p).wait_recv()
         back_pair(p)
-        pl.when(p == 0)(lambda: planes.relay())
-        pl.when(p == 1)(lambda: relay(1))
-        pl.when(p == 2)(lambda: plane_total())
-
+
+        @pl.when(p == 1)
+        def _():
+            oplanes.relay()
+            ups.start(6)
+            downs.start(2, 4, 6)
+
+        pl.when(p == pairs - 1)(lambda: plane_total())
+
+    weights_in.wait()
+    chains = chain(part, slots, ss, rs)
+
+    @pl.loop(0, line)
+    def _(i):
+        s = far_first(z, i)
+        at = pl.ds(pl.multiple_of(s * rows, rows), rows)
+        for lo, size in spans(model, 512):
+            part[s, :, pl.ds(lo, size)] = nt(dpre[at, :], wo[pl.ds(lo, size), pl.ds(0, 3 * width)]).astype(BF)
+        chains.head(s)
+
+    hidden = uhalf.shape[2]
+    chip = lax.div(d, 2)
+
+    def wide(i):
+        return [wo.at[pl.ds((i + k) * rows, rows), pl.ds(0, hidden)] for k in range(blocks)]
+
+    gate_sum = BlockSum(ghalf.at[chip], grecv, wide(0), wide_sum, ggrad, fsem.at[0], gsem)
+    up_sum = BlockSum(uhalf.at[chip], urecv, wide(blocks), wide_sum, ugrad, fsem.at[1], gsem)
+    tall = [osum.at[k, pl.ds(0, hidden)] for k in range(blocks)]
+    down_sum = BlockSum(dhalf.at[chip], drecv, tall, tall_sum, dgrad, fsem.at[2], gsem)
+    gate_sum.fetch()
+    mixed_in = [
+        pltpu.make_async_copy(mixed.at[pl.ds(pl.multiple_of(z * rows, rows), rows)], wo.at[pl.ds(4 * rows, rows)], local.at[0]),
+        pltpu.make_async_copy(mland.at[3], wo.at[pl.ds(5 * rows, rows)], local.at[1]),
+    ]
+    for copy in mixed_in:
+        copy.start()
+
+    def tile_in(i):
+        t = 2 * lax.rem(i, blocks) + jnp.where(i < blocks, 1 - core, core)
+        cols = pl.ds(pl.multiple_of(t * rows, rows), rows)
+        return pltpu.make_async_copy(n1.at[:, cols], nbuf.at[lax.rem(i, 2)], tsem.at[lax.rem(i, 2)])
+
+    def qblock(i):
+        tile_in(i).wait()
+        pl.when(i < 2 * blocks - 1)(lambda: tile_in(i + 1).start())
+        return lambda lo, size: tn(nbuf[lax.rem(i, 2)], dpre[:, pl.ds(lo, size)])
+
+    tile_in(jnp.int32(0)).start()
+
+    def qacross(k):
+        return send(qstage.at[lax.rem(k, 2)], qex.at[k], xss.at[k], xrs.at[k], d + flips[1], z)
+
+    @pl.loop(0, blocks)
+    def _(k):
+        pl.when(k >= 2)(lambda: qacross(k - 2).wait_send())
+        make = qblock(k)
+        for lo, size in spans(3 * width, 512):
+            qstage[lax.rem(k, 2), :, pl.ds(lo, size)] = make(lo, size).astype(BF)
+        qacross(k).start()
+
+    qplanes = PlaneChain(qsum, qrecv, qmid, d, z, flips, qss, qrs)
+
+    @pl.loop(0, blocks)
+    def _(k):
+        qacross(k).wait_recv()
+        fetch = pltpu.make_async_copy(qex.at[k], qfetch, local.at[8])
+        fetch.start()
+        fetch.wait()
+        make = qblock(k + blocks)
+        for lo, size in spans(3 * width, 512):
+            qsum[k, :, pl.ds(lo, size)] = (make(lo, size) + qfetch[:, pl.ds(lo, size)].astype(F32)).astype(BF)
+
+    qplanes.start()
+    chains.relay(1)
+    for h in range(2):
+        pl.when(~at_end)(lambda: mixed_last(h).wait_recv())
+
+    for copy in mixed_in:
+        copy.wait()
+
+    @pl.loop(0, rows // 32)
+    def _(i):
+        at = pl.ds(pl.multiple_of(i * 32, 32), 32)
+        total = marr[at, :].astype(F32)
+        for k in (4, 5):
+            total = total + wo[pl.ds(pl.multiple_of(k * rows + i * 32, 32), 32), :].astype(F32)
+        da[at, :] = (hid[at, :] + total).astype(BF)
+
+    lay_out = pltpu.make_async_copy(da, lay, local.at[0])
+    lay_out.start()
+    bsums[0] = jnp.zeros(bsums.shape[1:], F32)
+
+    def bias(at):
+        bsums[0, 0:1, :] += jnp.sum(dpre[at, :].astype(F32), 0, keepdims=True)
+
+    each_piece(length, 64, bias)
+
+    def bcopy(r):
+        return send(bsums.at[0], bsums.at[r], bss.at[r], brs.at[r], d + flips[r], z)
+
+    for r in range(1, 8):
+        bcopy(r).start()
+    qplanes.relay()
     ups.wait()
-    sum_blocks(uhalf.at[chip], urecv, ugrad, sbuf, sobuf, ssem, rows // sbuf.shape[1])
-    for h in range(2):
-        scatter.arrive(h)
-
-        @pl.loop(0, half // 32)
-        def _(i):
-            at = pl.ds(pl.multiple_of(h * half + i * 32, 32), 32)
-            total = scatter.total(h, pl.ds(pl.multiple_of(i * 32, 32), 32))
-            lay[at, :] = (hid[at, :] + total).astype(BF)
-
+    up_sum.fetch()
+    gate_sum.add()
+    chains.relay(2)
+    oplanes.finish()
     total = ofull[pl.ds(pl.multiple_of(z * width, width), width), :].astype(F32)
     for k in range(1, line):
         zaway(k).wait()
         total = total + ozr[k - 1].astype(F32)
     ograd[...] = total
-    for k in range(1, line):
-        away(k).wait_send()
-    planes.finish()
-    for s in range(line):
-        for h in range(2):
-            sent = (z != s) & ((z > 0) | (s == 1)) & ((z < line - 1) | (s == line - 2))
-            pl.when(sent)(lambda: scatter.copy(s, h, 0, z, s).wait_send())
-
-
-def attention_backward(dn2, hid, cot, small, wout, attall, qkv, lse, mixed, mland, ghalf, grecv, uhalf, tabs):
-    rows, model = hid.shape
-    line = 4
-    length = rows * line
-    width = model // line
-    pairs = width // 128
-    blocks = model // rows // 2
-    hidden = ghalf.shape[2]
-    sds = jax.ShapeDtypeStruct
-    dma = pltpu.SemaphoreType.DMA
-    return pl.pallas_call(
-        attention_back_kernel,
-        out_shape=(
-            sds((rows, model), BF), sds((rows, model), F32), sds((length, 3 * width), BF),
-            sds((width, rows), F32), sds((rows, hidden), F32), sds((rows, hidden), F32), sds((8, model), F32),
-            sds((blocks - 1, rows, hidden), BF), sds((blocks, model, rows), BF),
-        ),
-        in_specs=[INV] * 4 + [ANY] * 3 + [INV] + [ANY] * 5 + [INV] * 3,
-        out_specs=(INV, INV, INV, INV, ANY, ANY, INV, ANY, ANY),
-        scratch_shapes=[
-            pltpu.VMEM((model, model), BF),
-            pltpu.VMEM((rows, model), BF),
-            pltpu.VMEM((rows, model), BF),
-            pltpu.VMEM((model, rows), BF),
-            pltpu.VMEM((length, width), BF),
-            pltpu.VMEM((3, pairs, length, 128), BF),
-            pltpu.VMEM((line, rows, width), BF),
-            pltpu.VMEM((length, width), BF),
-            pltpu.VMEM((128, length), F32),
-            pltpu.VMEM((line, rows, model), BF),
-            pltpu.VMEM((line + 1, rows, model), BF),
-            pltpu.VMEM((2, model, rows), BF),
-            pltpu.VMEM((model, rows), BF),
-            pltpu.VMEM((blocks, model, rows), BF),
-            pltpu.VMEM((2, model, rows), BF),
-            pltpu.VMEM((2, model // 2, rows), BF),
-            pltpu.VMEM((model, rows), BF),
-            pltpu.VMEM((line - 1, width, rows), BF),
-            pltpu.VMEM((blocks, 64, hidden), BF),
-            pltpu.VMEM((64, hidden), F32),
-            pltpu.VMEM((length, 128), F32),
-            dma((line, 2)), dma((line + 1, 2)), dma((line,)), dma((line,)), dma((blocks,)), dma((blocks,)),
-            dma((6,)), dma((6,)), dma((blocks,)), dma((blocks,)), dma((line,)), dma((line,)),
-            dma((12,)), dma((blocks + 1,)),
-        ],
-        compiler_params=pltpu.CompilerParams(
-            collective_id=3, has_side_effects=True, vmem_limit_bytes=62 * 1024 * 1024
-        ),
-        cost_estimate=pl.CostEstimate(flops=10**11, bytes_accessed=10**8, transcendentals=0),
-        name="attention_backward",
-    )(dn2, hid, cot, small, wout, attall, qkv, lse, mixed, mland, ghalf, grecv, uhalf, *tabs)
-
-
-def input_back_kernel(
-    dpre, wqkv, n1, dhalf, tok, dhid, small, sums_in,
-    tgrad, qgrad, dgrad, gains, bout, drecv, qex,
-    pbuf, wbuf, nbuf, part, slots, qstage, qfetch, qsum, qrecv, qmid, sums, zsums, dsums, bsums, sbuf, sobuf,
-    ss, rs, xss, xrs, pss, prs, dss, drs, zss, zrs, gss, grs, bss, brs, local, ssem,
-):
-    line = 4
-    rows, model = tok.shape
-    width = dpre.shape[1] // 3
-    blocks = model // rows // 2
-    d, z, flips = place()
-    greet(d, z, flips, line, range(1, 8))
-    core, chip = lax.rem(d, 2), lax.div(d, 2)
-    loads = [
-        pltpu.make_async_copy(a, b, local.at[i]) for i, (a, b) in enumerate(((dpre, pbuf), (wqkv, wbuf), (n1, nbuf)))
-    ]
-    for copy in loads:
-        copy.start()
-    downs = PlaneSum(dhalf, drecv, d, z, blocks, dss, drs)
-    for j in range(blocks - 1):
-        downs.copy(j).start()
-    half = rows // 2
-    scatter = LineScatter(
-        lambda s, h: part.at[s, pl.ds(h * half, half)],
-        lambda i, h: slots.at[i, pl.ds(h * half, half)],
-        2, d, z, line, ss, rs,
-    )
-    pl.when(z == 0)(lambda: slots.__setitem__((0,), jnp.zeros((rows, model), BF)))
-    pl.when(z == line - 1)(lambda: slots.__setitem__((line,), jnp.zeros((rows, model), BF)))
-    for copy in loads[:2]:
-        copy.wait()
-
-    @pl.loop(0, line)
+    downs.wait()
+    down_sum.fetch()
+    up_sum.add()
+    down_sum.add()
+    qplanes.arrive()
+    piece = qtotal.shape[1]
+
+    @pl.loop(0, rows // piece)
     def _(i):
-        s = far_first(z, i)
-        at = pl.ds(pl.multiple_of(s * rows, rows), rows)
-        for lo, size in spans(model, 512):
-            part[s, :, pl.ds(lo, size)] = nt(pbuf[at, :], wbuf[pl.ds(lo, size), :]).astype(BF)
-        scatter.head(s)
-
-    loads[2].wait()
-
-    def qblock(t):
-        return lambda lo, size: tn(nbuf[:, pl.ds(pl.multiple_of(t * rows, rows), rows)], pbuf[:, pl.ds(lo, size)])
-
-    def across(k):
-        return send(qstage.at[k], qex.at[k], xss.at[k], xrs.at[k], d + flips[1], z)
-
-    @pl.loop(0, blocks)
-    def _(k):
-        make = qblock(2 * k + 1 - core)
-        for lo, size in spans(3 * width, 512):
-            qstage[k, :, pl.ds(lo, size)] = make(lo, size).astype(BF)
-        across(k).start()
-
-    planes = PlaneChain(qsum, qrecv, qmid, d, z, flips, pss, prs)
-
-    @pl.loop(0, blocks)
-    def _(k):
-        across(k).wait_recv()
-        fetch = pltpu.make_async_copy(qex.at[k], qfetch, local.at[3])
-        fetch.start()
-        fetch.wait()
-        make = qblock(2 * k + core)
-        for lo, size in spans(3 * width, 512):
-            qsum[k, :, pl.ds(lo, size)] = (make(lo, size) + qfetch[:, pl.ds(lo, size)].astype(F32)).astype(BF)
-
-    planes.start()
-    scatter.relay(1)
-    bsums[0] = jnp.zeros(bsums.shape[1:], F32)
-
-    def bias(at):
-        bsums[0, 0:1, :] += jnp.sum(pbuf[at, :].astype(F32), 0, keepdims=True)
-
-    each_piece(rows * line, 64, bias)
-
-    def bcopy(r):
-        return send(bsums.at[0], bsums.at[r], bss.at[r], brs.at[r], d + flips[r], z)
-
-    for r in range(1, 8):
-        bcopy(r).start()
-    planes.relay()
-    scatter.relay(2)
-    planes.arrive()
-    for j in range(3):
-        cols = pl.ds(j * width, width)
-        qgrad[j] = planes.total((slice(None), cols))
-    downs.wait()
-    sum_blocks(dhalf.at[chip], drecv, dgrad, sbuf, sobuf, ssem, dhalf.shape[1] // sbuf.shape[1])
+        at = pl.ds(pl.multiple_of(i * piece, piece), piece)
+        for j in range(3):
+            qtotal[j] = qplanes.total((at, pl.ds(j * width, width)))
+        back = pltpu.make_async_copy(qtotal, qgrad.at[:, at], local.at[1])
+        back.start()
+        back.wait()
+
     total = jnp.zeros(bout.shape, F32)
     for r in range(8):
         if r:
             bcopy(r).wait()
         total = total + bsums[r]
     bout[...] = total
-    sums[...] = sums_in[...]
+    tok_in.wait()
     for h in range(2):
-        scatter.arrive(h)
+        chains.arrive(h)
 
         @pl.loop(0, half // 32)
         def _(i):
             at = pl.ds(pl.multiple_of(h * half + i * 32, 32), 32)
-            grad = scatter.total(h, pl.ds(pl.multiple_of(i * 32, 32), 32))
-            standard, inverse = norm_parts(tok[at, :].astype(F32))
+            grad = chains.total(h, pl.ds(pl.multiple_of(i * 32, 32), 32))
+            standard, inverse = norm_parts(attr[at, :].astype(F32))
             sums[0:1, :] += jnp.sum(grad * standard, 0, keepdims=True)
             sums[1:2, :] += jnp.sum(grad, 0, keepdims=True)
             tgrad[at, :] = (dhid[at, :] + norm_back(grad, standard, inverse, small[0:1, :])).astype(BF)
@@ -1619,7 +1661,7 @@
         return send(columns(d + flips[r]), dsums.at[r], gss.at[r], grs.at[r], d + flips[r], z)
 
     def zcopy(k):
-        return send(zsums.at[0], zsums.at[k], zss.at[k], zrs.at[k], d, lax.rem(z + k, line))
+        return send(zsums.at[0], zsums.at[k], yss.at[k], yrs.at[k], d, lax.rem(z + k, line))
 
     for r in range(1, 8):
         dcopy(r).start()
@@ -1634,56 +1676,66 @@
         zcopy(k).wait()
         total = total + zsums[k]
     gains[...] = total
-    planes.finish()
-    for k in range(blocks):
-        across(k).wait_send()
-    scatter.finish()
-
-
-def input_backward(dpre, wqkv, n1, dhalf, tok, dhid, small, sums):
-    rows, model = tok.shape
+    for k in range(1, line):
+        for p in range(pairs):
+            away(k, p).wait_send()
+    qplanes.finish()
+    qacross(blocks - 2).wait_send()
+    qacross(blocks - 1).wait_send()
+    lay_out.wait()
+    for h in range(2):
+        pl.when(at_end)(lambda: mixed_last(h).wait_send())
+    chains.finish()
+
+
+def attention_backward(dn2, hid, cot, small, lse, tok, tabs, wout, attall, qkv, mixed, mland, ghalf, grecv, uhalf, dhalf, wqkv, n1):
+    rows, model = hid.shape
     line = 4
     length = rows * line
-    triple = dpre.shape[1]
+    width = model // line
+    pairs = width // 128
     blocks = model // rows // 2
-    hidden = dhalf.shape[1]
+    hidden = uhalf.shape[2]
     sds = jax.ShapeDtypeStruct
     dma = pltpu.SemaphoreType.DMA
+    vmem = pltpu.VMEM
     return pl.pallas_call(
-        input_back_kernel,
+        attention_back_kernel,
         out_shape=(
-            sds((rows, model), BF), sds((3, rows, triple // 3), F32), sds((hidden, rows), F32), sds((8, rows), F32),
-            sds((8, triple), F32), sds((blocks - 1, hidden, rows), BF), sds((blocks, rows, triple), BF),
+            sds((rows, model), BF), sds((width, rows), F32),
+            sds((8, rows), F32), sds((8, 3 * width), F32), sds((rows, model), BF),
+            sds((rows, hidden), F32), sds((rows, hidden), F32), sds((hidden, rows), F32), sds((3, rows, width), F32),
+            sds((blocks - 1, rows, hidden), BF), sds((blocks - 1, hidden, rows), BF),
+            sds((blocks, model, rows), BF), sds((blocks, rows, 3 * width), BF),
         ),
-        in_specs=[ANY, ANY, ANY, ANY, INV, INV, INV, INV],
-        out_specs=(INV, INV, ANY, INV, INV, ANY, ANY),
+        in_specs=[INV] * 5 + [ANY] * 14,
+        out_specs=(INV,) * 4 + (ANY,) * 9,
         scratch_shapes=[
-            pltpu.VMEM((length, triple), BF),
-            pltpu.VMEM((model, triple), BF),
-            pltpu.VMEM((length, model), BF),
-            pltpu.VMEM((line, rows, model), BF),
-            pltpu.VMEM((line + 1, rows, model), BF),
-            pltpu.VMEM((blocks, rows, triple), BF),
-            pltpu.VMEM((rows, triple), BF),
-            pltpu.VMEM((blocks, rows, triple), BF),
-            pltpu.VMEM((2, rows, triple), BF),
-            pltpu.VMEM((2, rows // 2, triple), BF),
-            pltpu.VMEM((8, model), F32),
-            pltpu.VMEM((line, 8, rows), F32),
-            pltpu.VMEM((8, 8, rows), F32),
-            pltpu.VMEM((8, 8, triple), F32),
-            pltpu.VMEM((blocks, 352, rows), BF),
-            pltpu.VMEM((352, rows), F32),
+            vmem((model, model), BF), vmem((rows, model), BF), vmem((rows, model), F32), vmem((rows, model), BF),
+            vmem((model, rows), BF), vmem((length, width), BF), vmem((3, pairs, length, 128), BF),
+            vmem((line, rows, width), BF), vmem((length, width), BF),
+            vmem((line, rows, model), BF), vmem((line + 1, rows, model), BF),
+            vmem((rows, model), BF),
+            vmem((model, rows), BF), vmem((blocks, model, rows), BF),
+            vmem((2, model, rows), BF), vmem((2, model // 2, rows), BF),
+            vmem((line - 1, width, rows), BF),
+            vmem((length, 128), F32), vmem((length, 3 * width), BF), vmem((2, length, rows), BF),
+            vmem((2, rows, 3 * width), BF), vmem((rows, 3 * width), BF), vmem((blocks, rows, 3 * width), BF),
+            vmem((2, rows, 3 * width), BF), vmem((2, rows // 2, 3 * width), BF),
+            vmem((2, 64, hidden), F32), vmem((2, hidden // 4, rows), F32), vmem((3, 64, width), F32),
+            vmem((8, model), F32), vmem((line, 8, rows), F32), vmem((8, 8, rows), F32), vmem((8, 8, 3 * width), F32),
+            dma((2,)), dma((2,)), dma((line, pairs)), dma((line, pairs)), dma((blocks,)), dma((blocks,)),
+            dma((6,)), dma((6,)), dma((3,)), dma((3,)), dma((line,)), dma((line,)),
             dma((line, 2)), dma((line + 1, 2)), dma((blocks,)), dma((blocks,)), dma((6,)), dma((6,)),
-            dma((blocks,)), dma((blocks,)), dma((line,)), dma((line,)), dma((8,)), dma((8,)),
-            dma((8,)), dma((8,)), dma((4,)), dma((blocks + 1,)),
+            dma((3,)), dma((3,)), dma((line,)), dma((line,)), dma((8,)), dma((8,)), dma((8,)), dma((8,)), dma((13,)), dma((2,)),
+            dma((3, blocks)), dma((2,)),
         ],
         compiler_params=pltpu.CompilerParams(
-            collective_id=4, has_side_effects=True, vmem_limit_bytes=62 * 1024 * 1024
+            collective_id=3, has_side_effects=True, vmem_limit_bytes=63 * 1024 * 1024
         ),
         cost_estimate=pl.CostEstimate(flops=10**11, bytes_accessed=10**8, transcendentals=0),
-        name="input_backward",
-    )(dpre, wqkv, n1, dhalf, tok, dhid, small, sums)
+        name="attention_backward",
+    )(hid, small, lse, *tabs, dn2, cot, tok, wout, attall, qkv, mixed, mland, ghalf, grecv, uhalf, dhalf, wqkv, n1)
 
 
 def turn_tables(length):
@@ -1691,12 +1743,11 @@
     freqs = np.float32(10000.0) ** (-np.arange(0, ROT, 2, dtype=np.float32) / np.float32(ROT))
     angles = np.arange(length, dtype=np.float32)[:, None] * freqs[None, :]
     cos = np.ones((length, HEAD_DIM), np.float32)
-    up = np.zeros((length, HEAD_DIM), np.float32)
-    down = np.zeros((length, HEAD_DIM), np.float32)
+    sin = np.zeros((length, HEAD_DIM), np.float32)
     cos[:, :half] = cos[:, half:ROT] = np.cos(angles)
-    up[:, half:ROT] = np.sin(angles)
-    down[:, :half] = -np.sin(angles)
-    return tuple(jnp.asarray(np.tile(t, (1, 2))) for t in (cos, up, down))
+    sin[:, half:ROT] = np.sin(angles)
+    sin[:, :half] = -np.sin(angles)
+    return tuple(jnp.asarray(np.tile(t, (1, 2))) for t in (cos, sin))
 
 
 def pack_smalls(d, model, width, qkv_bias, *vectors):
@@ -1721,16 +1772,15 @@
     tabs = turn_tables(length)
     depth, width = qkv_weight.shape[1:]
     smalls = pack_smalls(d, model, width, qkv_bias, norm1_gain, norm1_shift, norm2_gain, norm2_shift)
-    wq = qkv_weight.transpose(1, 0, 2).reshape(depth, 3 * width)
     cotnear, n1, qkv, lse, attall, wqkv, small, wout, n2, hidden, wgate, wup, wdown = attention_forward(
-        tokens, cotangent, wq, out_weight, gate_weight, up_weight, down_weight, smalls, tabs
+        tokens, cotangent, qkv_weight, out_weight, gate_weight, up_weight, down_weight, smalls, tabs
     )
     dn2, mixed, mland, _, _, _, ghalf, uhalf, dhalf, grecv = mlp(n2, cotangent, cotnear, wgate, wup, wdown)
-    layer_output, dhid, dpre, outw_grad, gatew_grad, upw_grad, sums, _, _ = attention_backward(
-        dn2, hidden, cotangent, small, wout, attall, qkv, lse, mixed, mland, ghalf, grecv, uhalf, tabs
-    )
-    token_gradient, qkvw_grad, downw_grad, gains, bias, _, _ = input_backward(
-        dpre, wqkv, n1, dhalf, tokens, dhid, small, sums
+    (
+        token_gradient, outw_grad, gains, bias, layer_output, gatew_grad, upw_grad, downw_grad, qkvw_grad, _, _, _, _
+    ) = attention_backward(
+        dn2, hidden, cotangent, small, lse, tokens, tabs, wout, attall, qkv, mixed, mland, ghalf, grecv, uhalf, dhalf,
+        wqkv, n1,
     )
     part = qkv_bias.shape[1]
     bias = bias[0].reshape(3, width)

time: 569 us -> 521 us (0.916)
  Pallas kernels: 541 us -> 495 us
    pallas_call x1 -> x0, Pallas kernels: 92.8 us -> none  [input_backward(): pl.pallas_call(input_back_kernel, out_shape=(sds((rows, model), BF), sds(...]
    pallas_call x1, Pallas kernels: 114 us -> 158 us  [attention_backward(): pl.pallas_call(attention_back_kernel, out_shape=(sds((rows, model), BF),...]
    unnamed x32 -> x29, local copies, waits for them, and re-layouts: 12.7 us -> 12.6 us
where the time goes in v4:
time: 521 us; the launch traced here: 513 us
  Pallas kernels  495 us (95%)
  local copies, waits for them, and re-layouts  16.4 us (3%)
    pallas_call x1, Pallas kernels, attention_forward(): pl.pallas_call(attention_kernel, out_shape=(sds((line, rows, model), BF),...  200 us
    pallas_call x1, Pallas kernels, attention_backward(): pl.pallas_call(attention_back_kernel, out_shape=(sds((rows, model), BF),...  158 us
    pallas_call x1, Pallas kernels, mlp(): pl.pallas_call(mlp_kernel, out_shape=(sds((rows, model), F32), sds((lengt...  137 us
    unnamed x29, local copies, waits for them, and re-layouts  12.6 us

profile of v4, /device:TPU:0, one launch (start us, length us, event | category | flops | bytes accessed | tf_op | source)
XLA Modules:
  0.0 513.3 jit_solution(1457639888492056690)
XLA Ops:
  0.6 0.0 copy-start
  0.7 0.1 pad.7.clone
  0.8 0.5 copy-done
  1.3 0.7 broadcast_bitcast_fusion.2
  2.0 0.7 broadcast_bitcast_fusion.1
  2.7 0.7 broadcast_bitcast_fusion
  3.3 0.1 maximum_select_fusion
  3.4 0.7 tile.16
  4.1 0.1 tile.17
  4.2 0.7 maximum_maximum_fusion.smalls
  4.9 199.8 %attention_forward.1 = (bf16[4,256,2048]{2,1,0:T(8,128)(2,1)}, bf16[1024,2048]{1,0:T(8,128)(2,1)}, bf16[3,4,1024,128]{3,2,1,0:T(8,128)(2,1)}, f32[128,1024]{1,0:...) custom-call(bf16[256,2048]{1,0:T(8,128)(2,1)} %tok.3, ...), custom_call_target="tpu_custom_call" | custom-call | flops 199999995904 | bytes 100000000 | tf_op jit(solution)/shard_map/attention_forward/pallas_call | solution.py:462
  204.7 136.7 %mlp.1 = (f32[256,2048]{1,0:T(8,128)}, bf16[1024,2048]{1,0:T(8,128)(2,1)}, bf16[4,256,2048]{2,1,0:T(8,128)(2,1)}, bf16[4,256,1408]{2,1,0:T(8,128)(2,1)}, bf16[4,...) custom-call(bf16[1024,2048]{1,0:T(8,128)(2,1)} %get-tuple-element.44, ...), custom_call_target="tpu_custom_call" | custom-call | flops 99999997952 | bytes 100000000 | tf_op jit(solution)/shard_map/mlp/pallas_call | solution.py:1137
  341.4 158.5 %attention_backward.1 = (bf16[256,2048]{1,0:T(8,128)(2,1)}, f32[512,256]{1,0:T(8,128)}, f32[8,256]{1,0:T(8,128)}, f32[8,1536]{1,0:T(8,128)}, bf16[256,2048]{1,0:...) custom-call(f32[256,2048]{1,0:T(8,128)} %get-tuple-element.41.hid, ...), custom_call_target="tpu_custom_call" | custom-call | flops 99999997952 | bytes 100000000 | tf_op jit(solution)/shard_map/attention_backward/pallas_call | solution.py:1702
  499.9 0.0 copy-start.2
  499.9 1.4 fusion.4
  501.3 0.8 slice_reduce_fusion
  502.1 0.7 constant_dynamic-slice_fusion
  502.8 2.3 copy.37
  505.1 0.0 copy-start.6
  505.1 0.0 copy-start.5
  505.1 2.4 copy.38
  507.6 0.0 copy-done.2
  507.6 0.0 copy-start.4
  507.6 1.1 copy.39
  508.7 0.0 copy-done.6
  508.7 0.8 copy.40
  509.5 0.0 copy-done.5
  509.5 0.0 copy-start.3
  509.5 0.0 copy-start.1
  509.5 1.1 copy.41
  510.6 0.0 copy-done.4
  510.6 1.1 copy.42
  511.7 0.0 copy-done.3
  511.7 1.1 copy.43
  512.8 0.0 copy-done.1
  (9 shorter events, 0.1 us)
Async XLA Ops:
  0.6 0.7 copy-start
  499.9 7.7 %copy-start.2 = (f32[3,256,512]{2,1,0:T(8,128)S(1)}, f32[3,256,512]{2,1,0:T(8,128)}, u32[]{:S(2)}) copy-start(f32[3,256,512]{2,1,0:T(8,128)} %get-tuple-element.88) | copy-start | bytes 4718596
  505.1 3.6 copy-start.6
  505.1 4.4 copy-start.5
  507.6 3.1 copy-start.4
  509.5 2.2 copy-start.3
  509.5 3.3 copy-start.1

commit v5 on v4

--- a/solution.py
+++ b/solution.py
@@ -868,11 +868,29 @@
     return lax.rem(lax.div(code, power), 4)
 
 
+class PlaneSum:
+    def __init__(self, half, recv, d, z, flips, send_sems, recv_sems):
+        self.half, self.recv, self.d, self.z, self.flips = half, recv, d, z, flips
+        self.ss, self.rs = send_sems, recv_sems
+
+    def copy(self, r):
+        to, slot = self.d + self.flips[r], (r // 2 - 1) % self.recv.shape[0]
+        return send(self.half.at[lax.div(to, 2)], self.recv.at[slot], self.ss.at[slot], self.rs.at[slot], to, self.z)
+
+    def start(self, *which):
+        for r in which:
+            self.copy(r).start()
+
+    def wait(self, *which):
+        for r in which:
+            self.copy(r).wait()
+
+
 def mlp_kernel(
     n2, cot, cotnear, wgate, wup, wdown,
-    dn2, mixed, mland, gex, uex, dex, ghalf, uhalf, dhalf, grecv,
+    dn2, mixed, mland, gex, uex, dex, ghalf, uhalf, dhalf, grecv, unear,
     nbuf, cbuf, gw, uw, dw, act, act_t, dga, dup, part, slots, mixbuf, wide, tall, wide_in, tall_in,
-    ss, rs, css, crs, lss, lrs, local, mixsem, outsem, exs, exr, gss, grs,
+    ss, rs, css, crs, lss, lrs, local, lsem, mixsem, outsem, exs, exr, gss, grs, uss, urs,
 ):
     line = 4
     rows = n2.shape[0] // line
@@ -882,11 +900,22 @@
     greet(d, z, flips, line, (1, 2, 4, 6))
     core = lax.rem(d, 2)
     chip = lax.div(d, 2)
-    loads = [
-        pltpu.make_async_copy(a, b, local.at[i])
-        for i, (a, b) in enumerate(((n2, nbuf), (wgate, gw), (wup, uw), (wdown, dw)))
-    ]
-    for copy in loads:
+    parts = spans(hidden, 512)
+
+    def rows_in(i):
+        at = pl.ds(pl.multiple_of(far_first(z, i) * rows, rows), rows)
+        return pltpu.make_async_copy(n2.at[at], nbuf.at[at], lsem.at[i])
+
+    def columns_in(c):
+        cols = pl.ds(*parts[c])
+        return [
+            pltpu.make_async_copy(wgate.at[:, cols], gw.at[:, cols], lsem.at[line + c]),
+            pltpu.make_async_copy(wup.at[:, cols], uw.at[:, cols], lsem.at[line + len(parts) + c]),
+        ]
+
+    down_in = pltpu.make_async_copy(wdown, dw, lsem.at[line + 2 * len(parts)])
+    first = [rows_in(jnp.int32(0))] + columns_in(0)
+    for copy in first:
         copy.start()
     half = rows // 2
     scatter = LineScatter(
@@ -921,11 +950,17 @@
 
     pl.when(z >= 2)(lambda: first_half(z - 2, 0).start())
     pl.when(z + 2 < line)(lambda: first_half(z + 2, 1).start())
+    for copy in first:
+        copy.wait()
+    for c in range(1, len(parts)):
+        for copy in columns_in(c):
+            copy.start()
+    down_in.start()
+    for i in range(1, line):
+        rows_in(jnp.int32(i)).start()
     near(z, 0).start()
     pl.when(z > 0)(lambda: near(z - 1, 1).start())
     pl.when(z < line - 1)(lambda: near(z + 1, 2).start())
-    for copy in loads:
-        copy.wait()
 
     def mixed_out(i):
         s = far_first(z, i)
@@ -943,8 +978,15 @@
     def _(i):
         s = far_first(z, i)
         at = pl.ds(pl.multiple_of(s * rows, rows), rows)
-        for lo, size in spans(hidden, 512):
+        pl.when(i > 0)(lambda: rows_in(i).wait())
+        for c, (lo, size) in enumerate(parts):
             cols = pl.ds(lo, size)
+            if c > 0:
+                @pl.when(i == 0)
+                def _():
+                    for copy in columns_in(c):
+                        copy.wait()
+
             gate = nn(nbuf[at, :], gw[:, cols])
             up = nn(nbuf[at, :], uw[:, cols])
             sigma = lax.logistic(gate)
@@ -954,6 +996,7 @@
             act_t[cols, at] = value.T
             dga[at, cols] = (up * (sigma * (1.0 + gate * (1.0 - sigma)))).astype(BF)
             dup[at, cols] = silu.astype(BF)
+        pl.when(i == 0)(lambda: down_in.wait())
         for lo, size in spans(model, 512):
             mixbuf[lax.rem(i, 2), :, pl.ds(lo, size)] = nn(act[...], dw[:, pl.ds(lo, size)]).astype(BF)
         mixed_out(i).start()
@@ -1102,6 +1145,8 @@
     mixed_relay()
 
     exchanged(1)
+    ups = PlaneSum(uhalf, unear, d, z, flips, uss, urs)
+    ups.start(2, 4)
     scatter.relay(2)
     exchanged(2)
     for h in range(2):
@@ -1123,6 +1168,7 @@
         pl.when((z + k < line) & (z > 0))(lambda: cots.copy(z + k, h, 1).wait_send())
     for j in range(blocks - 1):
         onward(j).wait()
+    ups.wait(2, 4)
 
 
 def mlp(n2, cot, cotnear, wgate, wup, wdown):
@@ -1138,10 +1184,10 @@
         mlp_kernel,
         out_shape=(
             sds((rows, model), F32), sds((length, model), BF), sds((4, rows, model), BF),
-            wide, wide, tall, wide, wide, tall, sds((blocks - 1, rows, hidden), BF),
+            wide, wide, tall, wide, wide, tall, sds((blocks - 1, rows, hidden), BF), sds((2, rows, hidden), BF),
         ),
         in_specs=[ANY] * 6,
-        out_specs=(INV,) + (ANY,) * 9,
+        out_specs=(INV,) + (ANY,) * 10,
         scratch_shapes=[
             pltpu.VMEM((length, model), BF),
             pltpu.VMEM((length, model), BF),
@@ -1166,12 +1212,15 @@
             pltpu.SemaphoreType.DMA((4,)),
             pltpu.SemaphoreType.DMA((4,)),
             pltpu.SemaphoreType.DMA((10,)),
+            pltpu.SemaphoreType.DMA((line + 1 + 2 * len(spans(hidden, 512)),)),
             pltpu.SemaphoreType.DMA((2,)),
             pltpu.SemaphoreType.DMA((2,)),
             pltpu.SemaphoreType.DMA((3, blocks)),
             pltpu.SemaphoreType.DMA((3, blocks)),
             pltpu.SemaphoreType.DMA((blocks,)),
             pltpu.SemaphoreType.DMA((blocks,)),
+            pltpu.SemaphoreType.DMA((2,)),
+            pltpu.SemaphoreType.DMA((2,)),
         ],
         compiler_params=pltpu.CompilerParams(
             collective_id=2, has_side_effects=True, vmem_limit_bytes=62 * 1024 * 1024
@@ -1202,24 +1251,6 @@
         body(pl.ds(pl.multiple_of(i * piece, piece), piece))
 
 
-class PlaneSum:
-    def __init__(self, half, recv, d, z, flips, send_sems, recv_sems):
-        self.half, self.recv, self.d, self.z, self.flips = half, recv, d, z, flips
-        self.ss, self.rs = send_sems, recv_sems
-
-    def copy(self, r):
-        to, slot = self.d + self.flips[r], r // 2 - 1
-        return send(self.half.at[lax.div(to, 2)], self.recv.at[slot], self.ss.at[slot], self.rs.at[slot], to, self.z)
-
-    def start(self, *which):
-        for r in which:
-            self.copy(r).start()
-
-    def wait(self):
-        for r in (2, 4, 6):
-            self.copy(r).wait()
-
-
 class PlaneChain:
     def __init__(self, half, recv, mid, d, z, flips, send_sems, recv_sems):
         self.half, self.recv, self.mid, self.d, self.z, self.flips = half, recv, mid, d, z, flips
@@ -1273,7 +1304,7 @@
 
 class BlockSum:
     def __init__(self, own, recv, bufs, stage, out, in_sems, out_sems):
-        self.ins = [own] + [recv.at[j] for j in range(recv.shape[0])]
+        self.ins = [own] + recv
         self.bufs, self.stage, self.out, self.in_sems, self.out_sems = bufs, stage, out, in_sems, out_sems
 
     def copies(self):
@@ -1314,7 +1345,7 @@
 
 
 def attention_back_kernel(
-    hid, small, lse_t, cos, sin, dn2, cot, tok, wout, attall, qkv, mixed, mland, ghalf, grecv, uhalf, dhalf, wqkv, n1,
+    hid, small, lse_t, cos, sin, dn2, cot, tok, wout, attall, qkv, mixed, mland, ghalf, grecv, uhalf, unear, dhalf, wqkv, n1,
     tgrad, ograd, gains, bout, lay, ggrad, ugrad, dgrad, qgrad, urecv, drecv, oex, qex,
     wo, da, dhid, attr, att_t, attc, qbuf, dsend, datt, part, slots, marr, ofull, osum, orecv, omid, ozr,
     dq, dpre, nbuf, qstage, qfetch, qsum, qrecv, qmid, wide_sum, tall_sum, qtotal, sums, zsums, dsums, bsums,
@@ -1354,7 +1385,8 @@
     pl.when(at_end)(lambda: marr.__setitem__(Ellipsis, jnp.zeros((rows, model), BF)))
     for copy in loads:
         copy.start()
-    ups.start(2, 4)
+    ups.start(6)
+    downs.start(2, 4, 6)
 
     def chain(part, slots, send_sems, recv_sems):
         pl.when(z == 0)(lambda: slots.__setitem__((0,), jnp.zeros((rows, model), BF)))
@@ -1430,19 +1462,6 @@
         ostage(k)[...] = oblock(2 * k + 1 - core).astype(BF)
         oacross(k).start()
 
-    oplanes = PlaneChain(osum, orecv, omid, d, z, flips, pss, prs)
-
-    @pl.loop(0, blocks)
-    def _(k):
-        oacross(k).wait_recv()
-        fetch = pltpu.make_async_copy(oex.at[k], ofull, local.at[8])
-        fetch.start()
-        fetch.wait()
-        osum[k] = (oblock(2 * k + core) + ofull[...].astype(F32)).astype(BF)
-
-    oplanes.start()
-    oacross(blocks - 2).wait_send()
-    oacross(blocks - 1).wait_send()
     lanes = lax.broadcasted_iota(jnp.int32, (1, 128), 1)
     mine = (lanes < 64, lanes >= 64)
     which = lax.broadcasted_iota(jnp.int32, (16, 128), 0)
@@ -1504,14 +1523,9 @@
             taken(k, p).wait_recv()
         back_pair(p)
 
-        @pl.when(p == 1)
-        def _():
-            oplanes.relay()
-            ups.start(6)
-            downs.start(2, 4, 6)
-
-        pl.when(p == pairs - 1)(lambda: plane_total())
-
+
+    oacross(blocks - 2).wait_send()
+    oacross(blocks - 1).wait_send()
     weights_in.wait()
     chains = chain(part, slots, ss, rs)
 
@@ -1529,10 +1543,10 @@
     def wide(i):
         return [wo.at[pl.ds((i + k) * rows, rows), pl.ds(0, hidden)] for k in range(blocks)]
 
-    gate_sum = BlockSum(ghalf.at[chip], grecv, wide(0), wide_sum, ggrad, fsem.at[0], gsem)
-    up_sum = BlockSum(uhalf.at[chip], urecv, wide(blocks), wide_sum, ugrad, fsem.at[1], gsem)
+    gate_sum = BlockSum(ghalf.at[chip], [grecv.at[k] for k in range(blocks - 1)], wide(0), wide_sum, ggrad, fsem.at[0], gsem)
+    up_sum = BlockSum(uhalf.at[chip], [unear.at[0], unear.at[1], urecv.at[0]], wide(blocks), wide_sum, ugrad, fsem.at[1], gsem)
     tall = [osum.at[k, pl.ds(0, hidden)] for k in range(blocks)]
-    down_sum = BlockSum(dhalf.at[chip], drecv, tall, tall_sum, dgrad, fsem.at[2], gsem)
+    down_sum = BlockSum(dhalf.at[chip], [drecv.at[k] for k in range(blocks - 1)], tall, tall_sum, dgrad, fsem.at[2], gsem)
     gate_sum.fetch()
     mixed_in = [
         pltpu.make_async_copy(mixed.at[pl.ds(pl.multiple_of(z * rows, rows), rows)], wo.at[pl.ds(4 * rows, rows)], local.at[0]),
@@ -1541,6 +1555,17 @@
     for copy in mixed_in:
         copy.start()
 
+    oplanes = PlaneChain(osum, orecv, omid, d, z, flips, pss, prs)
+
+    @pl.loop(0, blocks)
+    def _(k):
+        oacross(k).wait_recv()
+        fetch = pltpu.make_async_copy(oex.at[k], ofull, local.at[8])
+        fetch.start()
+        fetch.wait()
+        osum[k] = (oblock(2 * k + core) + ofull[...].astype(F32)).astype(BF)
+
+    oplanes.start()
     def tile_in(i):
         t = 2 * lax.rem(i, blocks) + jnp.where(i < blocks, 1 - core, core)
         cols = pl.ds(pl.multiple_of(t * rows, rows), rows)
@@ -1564,6 +1589,7 @@
             qstage[lax.rem(k, 2), :, pl.ds(lo, size)] = make(lo, size).astype(BF)
         qacross(k).start()
 
+    chains.relay(1)
     qplanes = PlaneChain(qsum, qrecv, qmid, d, z, flips, qss, qrs)
 
     @pl.loop(0, blocks)
@@ -1577,7 +1603,7 @@
             qsum[k, :, pl.ds(lo, size)] = (make(lo, size) + qfetch[:, pl.ds(lo, size)].astype(F32)).astype(BF)
 
     qplanes.start()
-    chains.relay(1)
+    oplanes.relay()
     for h in range(2):
         pl.when(~at_end)(lambda: mixed_last(h).wait_recv())
 
@@ -1606,33 +1632,13 @@
 
     for r in range(1, 8):
         bcopy(r).start()
-    qplanes.relay()
-    ups.wait()
+    ups.wait(6)
     up_sum.fetch()
     gate_sum.add()
     chains.relay(2)
-    oplanes.finish()
-    total = ofull[pl.ds(pl.multiple_of(z * width, width), width), :].astype(F32)
-    for k in range(1, line):
-        zaway(k).wait()
-        total = total + ozr[k - 1].astype(F32)
-    ograd[...] = total
-    downs.wait()
-    down_sum.fetch()
+    qplanes.relay()
     up_sum.add()
-    down_sum.add()
-    qplanes.arrive()
-    piece = qtotal.shape[1]
-
-    @pl.loop(0, rows // piece)
-    def _(i):
-        at = pl.ds(pl.multiple_of(i * piece, piece), piece)
-        for j in range(3):
-            qtotal[j] = qplanes.total((at, pl.ds(j * width, width)))
-        back = pltpu.make_async_copy(qtotal, qgrad.at[:, at], local.at[1])
-        back.start()
-        back.wait()
-
+    plane_total()
     total = jnp.zeros(bout.shape, F32)
     for r in range(8):
         if r:
@@ -1642,7 +1648,6 @@
     tok_in.wait()
     for h in range(2):
         chains.arrive(h)
-
         @pl.loop(0, half // 32)
         def _(i):
             at = pl.ds(pl.multiple_of(h * half + i * 32, 32), 32)
@@ -1665,6 +1670,21 @@
 
     for r in range(1, 8):
         dcopy(r).start()
+    qplanes.arrive()
+    piece = qtotal.shape[1]
+
+    @pl.loop(0, rows // piece)
+    def _(i):
+        at = pl.ds(pl.multiple_of(i * piece, piece), piece)
+        for j in range(3):
+            qtotal[j] = qplanes.total((at, pl.ds(j * width, width)))
+        back = pltpu.make_async_copy(qtotal, qgrad.at[:, at], local.at[1])
+        back.start()
+        back.wait()
+
+    oplanes.finish()
+    downs.wait(2, 4, 6)
+    down_sum.fetch()
     total = columns(d)[...]
     for r in range(1, 8):
         dcopy(r).wait()
@@ -1672,10 +1692,16 @@
     zsums[0] = total
     for k in range(1, line):
         zcopy(k).start()
+    down_sum.add()
     for k in range(1, line):
         zcopy(k).wait()
         total = total + zsums[k]
     gains[...] = total
+    total = ofull[pl.ds(pl.multiple_of(z * width, width), width), :].astype(F32)
+    for k in range(1, line):
+        zaway(k).wait()
+        total = total + ozr[k - 1].astype(F32)
+    ograd[...] = total
     for k in range(1, line):
         for p in range(pairs):
             away(k, p).wait_send()
@@ -1688,7 +1714,7 @@
     chains.finish()
 
 
-def attention_backward(dn2, hid, cot, small, lse, tok, tabs, wout, attall, qkv, mixed, mland, ghalf, grecv, uhalf, dhalf, wqkv, n1):
+def attention_backward(dn2, hid, cot, small, lse, tok, tabs, wout, attall, qkv, mixed, mland, ghalf, grecv, uhalf, unear, dhalf, wqkv, n1):
     rows, model = hid.shape
     line = 4
     length = rows * line
@@ -1705,10 +1731,10 @@
             sds((rows, model), BF), sds((width, rows), F32),
             sds((8, rows), F32), sds((8, 3 * width), F32), sds((rows, model), BF),
             sds((rows, hidden), F32), sds((rows, hidden), F32), sds((hidden, rows), F32), sds((3, rows, width), F32),
-            sds((blocks - 1, rows, hidden), BF), sds((blocks - 1, hidden, rows), BF),
+            sds((1, rows, hidden), BF), sds((blocks - 1, hidden, rows), BF),
             sds((blocks, model, rows), BF), sds((blocks, rows, 3 * width), BF),
         ),
-        in_specs=[INV] * 5 + [ANY] * 14,
+        in_specs=[INV] * 5 + [ANY] * 15,
         out_specs=(INV,) * 4 + (ANY,) * 9,
         scratch_shapes=[
             vmem((model, model), BF), vmem((rows, model), BF), vmem((rows, model), F32), vmem((rows, model), BF),
@@ -1735,7 +1761,7 @@
         ),
         cost_estimate=pl.CostEstimate(flops=10**11, bytes_accessed=10**8, transcendentals=0),
         name="attention_backward",
-    )(hid, small, lse, *tabs, dn2, cot, tok, wout, attall, qkv, mixed, mland, ghalf, grecv, uhalf, dhalf, wqkv, n1)
+    )(hid, small, lse, *tabs, dn2, cot, tok, wout, attall, qkv, mixed, mland, ghalf, grecv, uhalf, unear, dhalf, wqkv, n1)
 
 
 def turn_tables(length):
@@ -1775,12 +1801,12 @@
     cotnear, n1, qkv, lse, attall, wqkv, small, wout, n2, hidden, wgate, wup, wdown = attention_forward(
         tokens, cotangent, qkv_weight, out_weight, gate_weight, up_weight, down_weight, smalls, tabs
     )
-    dn2, mixed, mland, _, _, _, ghalf, uhalf, dhalf, grecv = mlp(n2, cotangent, cotnear, wgate, wup, wdown)
+    dn2, mixed, mland, _, _, _, ghalf, uhalf, dhalf, grecv, unear = mlp(n2, cotangent, cotnear, wgate, wup, wdown)
     (
         token_gradient, outw_grad, gains, bias, layer_output, gatew_grad, upw_grad, downw_grad, qkvw_grad, _, _, _, _
     ) = attention_backward(
-        dn2, hidden, cotangent, small, lse, tokens, tabs, wout, attall, qkv, mixed, mland, ghalf, grecv, uhalf, dhalf,
-        wqkv, n1,
+        dn2, hidden, cotangent, small, lse, tokens, tabs, wout, attall, qkv, mixed, mland, ghalf, grecv, uhalf, unear,
+        dhalf, wqkv, n1,
     )
     part = qkv_bias.shape[1]
     bias = bias[0].reshape(3, width)

time: 521 us -> 497 us (0.954)
  Pallas kernels: 495 us -> 470 us
    pallas_call x1, Pallas kernels: 158 us -> 137 us  [attention_backward(): pl.pallas_call(attention_back_kernel, out_shape=(sds((rows, model), BF),...]
where the time goes in v5:
time: 497 us; the launch traced here: 489 us
  Pallas kernels  470 us (95%)
  local copies, waits for them, and re-layouts  16.4 us (3%)
    pallas_call x1, Pallas kernels, attention_forward(): pl.pallas_call(attention_kernel, out_shape=(sds((line, rows, model), BF),...  200 us
    pallas_call x1, Pallas kernels, attention_backward(): pl.pallas_call(attention_back_kernel, out_shape=(sds((rows, model), BF),...  137 us
    pallas_call x1, Pallas kernels, mlp(): pl.pallas_call(mlp_kernel, out_shape=(sds((rows, model), F32), sds((lengt...  134 us
    unnamed x29, local copies, waits for them, and re-layouts  12.6 us

profile of v5, /device:TPU:0, one launch (start us, length us, event | category | flops | bytes accessed | tf_op | source)
XLA Modules:
  0.0 488.7 jit_solution(12972879817433170928)
XLA Ops:
  0.6 0.0 copy-start
  0.7 0.1 pad.7.clone
  0.8 0.5 copy-done
  1.3 0.7 broadcast_bitcast_fusion.2
  2.0 0.7 broadcast_bitcast_fusion.1
  2.7 0.7 broadcast_bitcast_fusion
  3.3 0.1 maximum_select_fusion
  3.4 0.7 tile.16
  4.1 0.1 tile.17
  4.2 0.7 maximum_maximum_fusion.smalls
  4.9 199.8 %attention_forward.1 = (bf16[4,256,2048]{2,1,0:T(8,128)(2,1)}, bf16[1024,2048]{1,0:T(8,128)(2,1)}, bf16[3,4,1024,128]{3,2,1,0:T(8,128)(2,1)}, f32[128,1024]{1,0:...) custom-call(bf16[256,2048]{1,0:T(8,128)(2,1)} %tok.3, ...), custom_call_target="tpu_custom_call" | custom-call | flops 199999995904 | bytes 100000000 | tf_op jit(solution)/shard_map/attention_forward/pallas_call | solution.py:462
  204.7 133.7 %mlp.1 = (f32[256,2048]{1,0:T(8,128)}, bf16[1024,2048]{1,0:T(8,128)(2,1)}, bf16[4,256,2048]{2,1,0:T(8,128)(2,1)}, bf16[4,256,1408]{2,1,0:T(8,128)(2,1)}, bf16[4,...) custom-call(bf16[1024,2048]{1,0:T(8,128)(2,1)} %get-tuple-element.45, ...), custom_call_target="tpu_custom_call" | custom-call | flops 99999997952 | bytes 100000000 | tf_op jit(solution)/shard_map/mlp/pallas_call | solution.py:1183
  338.4 136.9 %attention_backward.1 = (bf16[256,2048]{1,0:T(8,128)(2,1)}, f32[512,256]{1,0:T(8,128)}, f32[8,256]{1,0:T(8,128)}, f32[8,1536]{1,0:T(8,128)}, bf16[256,2048]{1,0:...) custom-call(f32[256,2048]{1,0:T(8,128)} %get-tuple-element.42.hid, ...), custom_call_target="tpu_custom_call" | custom-call | flops 99999997952 | bytes 100000000 | tf_op jit(solution)/shard_map/attention_backward/pallas_call | solution.py:1728
  475.3 0.0 copy-start.2
  475.3 1.4 fusion.4
  476.7 0.8 slice_reduce_fusion
  477.6 0.7 constant_dynamic-slice_fusion
  478.2 2.3 copy.37
  480.5 0.0 copy-start.6
  480.5 0.0 copy-start.5
  480.5 2.4 copy.38
  483.0 0.0 copy-done.2
  483.0 0.0 copy-start.4
  483.0 1.1 copy.39
  484.1 0.0 copy-done.6
  484.1 0.8 copy.40
  484.9 0.0 copy-done.5
  484.9 0.0 copy-start.3
  484.9 0.0 copy-start.1
  484.9 1.1 copy.41
  486.0 0.0 copy-done.4
  486.0 1.1 copy.42
  487.1 0.0 copy-done.3
  487.1 1.1 copy.43
  488.2 0.0 copy-done.1
  (9 shorter events, 0.1 us)
Async XLA Ops:
  0.6 0.7 copy-start
  475.3 7.7 %copy-start.2 = (f32[3,256,512]{2,1,0:T(8,128)S(1)}, f32[3,256,512]{2,1,0:T(8,128)}, u32[]{:S(2)}) copy-start(f32[3,256,512]{2,1,0:T(8,128)} %get-tuple-element.90) | copy-start | bytes 4718596
  480.5 3.6 copy-start.6
  480.5 4.4 copy-start.5
  483.0 3.1 copy-start.4
  484.9 2.2 copy-start.3
  484.9 3.3 copy-start.1

commit v6 on v5

--- a/solution.py
+++ b/solution.py
@@ -246,8 +246,6 @@
     for copy in w_in:
         copy.wait()
     qkv_plane.start()
-    o_in.wait()
-    outs_z.start(0)
     for copy in small_copies:
         copy.wait()
     total = smalls[...].astype(F32)
@@ -281,14 +279,12 @@
     normalise(z)
     for h in range(2):
         toks.step(1, h)
-    outs_z.step(1, 0)
     qkv_plane.relay()
     gate_plane.start()
     normalise(arrival(z, 1))
     qkv_plane.pass_on()
     for h in range(2):
         toks.step(2, h)
-    outs_z.step(2, 0)
     normalise(arrival(z, 2))
     gate_plane.relay()
     qkv_plane.arrive()
@@ -300,19 +296,16 @@
         @pl.when(i == line - 1)
         def _():
             gate_plane.pass_on()
+            up_plane.start()
+            o_in.wait()
+            outs_z.start(0)
             for h in range(2):
                 toks.step(3, h)
-            for h in range(2):
-                cots.start(h, cot.at[pl.ds(h * half, half)])
-            outs_z.step(3, 0)
-            out_plane.start()
             normalise(s)
 
         project(s)
 
     o_own = pltpu.make_async_copy(wz, oblock(d), local.at[15])
-    o_own.start()
-
     outs = [
         pltpu.make_async_copy(n1buf, n1, local.at[3]),
         pltpu.make_async_copy(wbuf, wqkv, local.at[4]),
@@ -356,18 +349,24 @@
     def _(p):
         attend(p)
         atts.start(p)
+        for k in range(1, line):
+            pl.when(p == k - 1)(lambda: outs_z.step(k, 0))
+
+        @pl.when(p == line - 2)
+        def _():
+            up_plane.relay()
+            out_plane.start()
+            o_own.start()
 
     lse_t[...] = lse[...].T
-    up_plane.start()
     for p in range(pairs):
         atts.step(1, p)
-    for h in range(2):
-        cots.step(1, h, forward=False)
+    up_plane.pass_on()
     out_plane.relay()
     down_plane.start()
-    out_plane.pass_on()
     for p in range(pairs):
         atts.step(2, p)
+    out_plane.pass_on()
     o_own.wait()
     out_plane.arrive()
     keep_wo = pltpu.make_async_copy(wo, wout, local.at[6])
@@ -388,20 +387,12 @@
                 acc[at, pl.ds(lo, size)] = base + project_out(s, at, lo, size)
 
         if i == 1:
-            up_plane.relay()
+            down_plane.relay()
     for copy in outs:
         copy.wait()
-    down_plane.relay()
-    up_plane.pass_on()
     for p in range(pairs):
         atts.step(3, p)
-    inner = (z > 0) & (z < line - 1)
-
-    @pl.when(inner)
-    def _():
-        cots.copy(z - 1, 0, 0).start()
-        cots.copy(z + 1, 0, 1).start()
-
+    cots.start(0, cot.at[pl.ds(0, half)])
     keep_att = pltpu.make_async_copy(attv, attall, local.at[7])
     keep_att.start()
     last = arrival(z, line - 1)
@@ -431,15 +422,9 @@
     down_plane.pass_on()
     for gather in (toks, atts, outs_z):
         gather.finish()
-    cots.finish(0, 1)
-
-    @pl.when(inner)
-    def _():
-        cots.copy(z - 1, 0, 0).wait_send()
-        cots.copy(z + 1, 0, 1).wait_send()
-
-    pl.when(z >= 2)(lambda: cots.copy(z - 2, 0, 0).wait_recv())
-    pl.when(z + 2 < line)(lambda: cots.copy(z + 2, 0, 1).wait_recv())
+    cots.step(1, 0, forward=False)
+    pl.when(z < line - 1)(lambda: cots.copy(z, 0, 0).wait_send())
+    pl.when(z > 0)(lambda: cots.copy(z, 0, 1).wait_send())
     for plane in (gate_plane, up_plane, down_plane):
         plane.arrive()
     for plane in planes:
@@ -929,27 +914,19 @@
         lambda s, h: cbuf.at[pl.ds(pl.multiple_of(s * rows + h * half, half), half)], 2, d, z, line, css, crs
     )
 
-    def near(s, k):
-        return pltpu.make_async_copy(
-            cot if k == 0 else cotnear.at[s], cbuf.at[pl.ds(pl.multiple_of(s * rows, rows), rows)], local.at[5 + k]
-        )
-
-    for h in (1, 0):
-        @pl.when((z > 0) & (z < line - 1))
-        def _():
-            if h == 1:
-                cots.copy(z - 1, h, 0, cotnear.at[z - 1, pl.ds(h * half, half)]).start()
-                cots.copy(z + 1, h, 1, cotnear.at[z + 1, pl.ds(h * half, half)]).start()
-            else:
-                pl.when(z == 2)(lambda: cots.copy(z - 2, h, 0, cotnear.at[z - 2, pl.ds(0, half)]).start())
-                pl.when(z == 1)(lambda: cots.copy(z + 2, h, 1, cotnear.at[z + 2, pl.ds(0, half)]).start())
+    own_cot = pltpu.make_async_copy(cot, cbuf.at[pl.ds(pl.multiple_of(z * rows, rows), rows)], local.at[5])
+    @pl.when((z > 0) & (z < line - 1))
+    def _():
+        cots.copy(z - 1, 0, 0, cotnear.at[z - 1, pl.ds(0, half)]).start()
+        cots.copy(z + 1, 0, 1, cotnear.at[z + 1, pl.ds(0, half)]).start()
+
+    cots.start(1, cot.at[pl.ds(half, half)])
+
     def first_half(s, k):
         return pltpu.make_async_copy(
             cotnear.at[s, pl.ds(0, half)], cbuf.at[pl.ds(pl.multiple_of(s * rows, rows), half)], local.at[8 + k]
         )
 
-    pl.when(z >= 2)(lambda: first_half(z - 2, 0).start())
-    pl.when(z + 2 < line)(lambda: first_half(z + 2, 1).start())
     for copy in first:
         copy.wait()
     for c in range(1, len(parts)):
@@ -958,9 +935,9 @@
     down_in.start()
     for i in range(1, line):
         rows_in(jnp.int32(i)).start()
-    near(z, 0).start()
-    pl.when(z > 0)(lambda: near(z - 1, 1).start())
-    pl.when(z < line - 1)(lambda: near(z + 1, 2).start())
+    own_cot.start()
+    pl.when(z > 0)(lambda: first_half(z - 1, 0).start())
+    pl.when(z < line - 1)(lambda: first_half(z + 1, 1).start())
 
     def mixed_out(i):
         s = far_first(z, i)
@@ -1002,7 +979,9 @@
         mixed_out(i).start()
         mixed_out(i).wait()
         pl.when(at_end & (i < 2))(lambda: mixed_ahead(i).start())
-        pl.when(i == 1)(lambda: cots.step(2, 1))
+        pl.when(i == 0)(lambda: cots.step(2, 0))
+        pl.when(i == 1)(lambda: cots.step(1, 1))
+        pl.when(i == 2)(lambda: cots.step(2, 1))
 
     def add_mixed(s, slot, send_slot, to, lands):
         at = pl.ds(pl.multiple_of(s * rows, rows), rows)
@@ -1044,17 +1023,18 @@
             add_mixed(edge, 2, 0, edge, 3)
 
     mixed_on(0)
-    near(z, 0).wait()
-    pl.when(z >= 2)(lambda: first_half(z - 2, 0).wait())
-    pl.when(z + 2 < line)(lambda: first_half(z + 2, 1).wait())
-    pl.when(z > 0)(lambda: near(z - 1, 1).wait())
-    pl.when(z < line - 1)(lambda: near(z + 1, 2).wait())
-    for h in range(2):
-        cots.step(3, h)
+    own_cot.wait()
 
     @pl.loop(0, line)
     def _(i):
-        s = far_first(z, i)
+        @pl.when(i == 1)
+        def _():
+            pl.when(z > 0)(lambda: first_half(z - 1, 0).wait())
+            pl.when(z < line - 1)(lambda: first_half(z + 1, 1).wait())
+            for h in range(2):
+                cots.step(3, h)
+
+        s = far_first(z, lax.rem(i + line - 1, line))
         at = pl.ds(pl.multiple_of(s * rows, rows), rows)
         for lo, size in spans(hidden, 512):
             cols = pl.ds(lo, size)
@@ -1163,7 +1143,7 @@
     for i in (0, 2, 3):
         pl.when(~at_end)(lambda: landing(3, i).wait_send())
     landing(3, 3).wait_recv()
-    for k, h in ((1, 1), (2, 0), (2, 1)):
+    for k, h in ((0, 1), (1, 0), (1, 1), (2, 0), (2, 1)):
         pl.when((z - k >= 0) & (z < line - 1))(lambda: cots.copy(z - k, h, 0).wait_send())
         pl.when((z + k < line) & (z > 0))(lambda: cots.copy(z + k, h, 1).wait_send())
     for j in range(blocks - 1):

time: 497 us -> 489 us (0.984)
  Pallas kernels: 470 us -> 462 us
    pallas_call x1, Pallas kernels: 200 us -> 182 us  [attention_forward(): pl.pallas_call(attention_kernel, out_shape=(sds((line, rows, model), BF),...]
    pallas_call x1, Pallas kernels: 134 us -> 141 us  [mlp(): pl.pallas_call(mlp_kernel, out_shape=(sds((rows, model), F32), sds((lengt...]
where the time goes in v6:
time: 489 us; the launch traced here: 481 us
  Pallas kernels  462 us (94%)
  local copies, waits for them, and re-layouts  16.4 us (3%)
    pallas_call x1, Pallas kernels, attention_forward(): pl.pallas_call(attention_kernel, out_shape=(sds((line, rows, model), BF),...  182 us
    pallas_call x1, Pallas kernels, mlp(): pl.pallas_call(mlp_kernel, out_shape=(sds((rows, model), F32), sds((lengt...  141 us
    pallas_call x1, Pallas kernels, attention_backward(): pl.pallas_call(attention_back_kernel, out_shape=(sds((rows, model), BF),...  140 us
    unnamed x29, local copies, waits for them, and re-layouts  12.6 us

profile of v6, /device:TPU:0, one launch (start us, length us, event | category | flops | bytes accessed | tf_op | source)
XLA Modules:
  0.0 480.6 jit_solution(12412230569134914660)
XLA Ops:
  0.6 0.0 copy-start
  0.7 0.1 pad.7.clone
  0.8 0.5 copy-done
  1.3 0.7 broadcast_bitcast_fusion.2
  2.0 0.7 broadcast_bitcast_fusion.1
  2.7 0.7 broadcast_bitcast_fusion
  3.3 0.1 maximum_select_fusion
  3.4 0.7 tile.16
  4.1 0.1 tile.17
  4.2 0.7 maximum_maximum_fusion.smalls
  4.9 182.1 %attention_forward.1 = (bf16[4,256,2048]{2,1,0:T(8,128)(2,1)}, bf16[1024,2048]{1,0:T(8,128)(2,1)}, bf16[3,4,1024,128]{3,2,1,0:T(8,128)(2,1)}, f32[128,1024]{1,0:...) custom-call(bf16[256,2048]{1,0:T(8,128)(2,1)} %tok.3, ...), custom_call_target="tpu_custom_call" | custom-call | flops 199999995904 | bytes 100000000 | tf_op jit(solution)/shard_map/attention_forward/pallas_call | solution.py:447
  187.0 140.7 %mlp.1 = (f32[256,2048]{1,0:T(8,128)}, bf16[1024,2048]{1,0:T(8,128)(2,1)}, bf16[4,256,2048]{2,1,0:T(8,128)(2,1)}, bf16[4,256,1408]{2,1,0:T(8,128)(2,1)}, bf16[4,...) custom-call(bf16[1024,2048]{1,0:T(8,128)(2,1)} %get-tuple-element.45, ...), custom_call_target="tpu_custom_call" | custom-call | flops 99999997952 | bytes 100000000 | tf_op jit(solution)/shard_map/mlp/pallas_call | solution.py:1163
  327.7 139.5 %attention_backward.1 = (bf16[256,2048]{1,0:T(8,128)(2,1)}, f32[512,256]{1,0:T(8,128)}, f32[8,256]{1,0:T(8,128)}, f32[8,1536]{1,0:T(8,128)}, bf16[256,2048]{1,0:...) custom-call(f32[256,2048]{1,0:T(8,128)} %get-tuple-element.42.hid, ...), custom_call_target="tpu_custom_call" | custom-call | flops 99999997952 | bytes 100000000 | tf_op jit(solution)/shard_map/attention_backward/pallas_call | solution.py:1708
  467.2 0.0 copy-start.2
  467.3 1.4 fusion.4
  468.7 0.8 slice_reduce_fusion
  469.5 0.7 constant_dynamic-slice_fusion
  470.2 2.3 copy.37
  472.5 0.0 copy-start.6
  472.5 0.0 copy-start.5
  472.5 2.4 copy.38
  474.9 0.0 copy-done.2
  474.9 0.0 copy-start.4
  475.0 1.1 copy.39
  476.1 0.0 copy-done.6
  476.1 0.8 copy.40
  476.9 0.0 copy-done.5
  476.9 0.0 copy-start.3
  476.9 0.0 copy-start.1
  476.9 1.1 copy.41
  478.0 0.0 copy-done.4
  478.0 1.1 copy.42
  479.1 0.0 copy-done.3
  479.1 1.1 copy.43
  480.2 0.0 copy-done.1
  (9 shorter events, 0.1 us)
Async XLA Ops:
  0.6 0.7 copy-start
  467.2 7.7 %copy-start.2 = (f32[3,256,512]{2,1,0:T(8,128)S(1)}, f32[3,256,512]{2,1,0:T(8,128)}, u32[]{:S(2)}) copy-start(f32[3,256,512]{2,1,0:T(8,128)} %get-tuple-element.90) | copy-start | bytes 4718596
  472.5 3.6 copy-start.6
  472.5 4.4 copy-start.5
  474.9 3.1 copy-start.4
  476.9 2.2 copy-start.3
  476.9 3.3 copy-start.1

commit v7 on v6

--- a/solution.py
+++ b/solution.py
@@ -1034,6 +1034,7 @@
             for h in range(2):
                 cots.step(3, h)
 
+        pl.when(i == line - 1)(lambda: mixed_on(1))
         s = far_first(z, lax.rem(i + line - 1, line))
         at = pl.ds(pl.multiple_of(s * rows, rows), rows)
         for lo, size in spans(hidden, 512):
@@ -1119,7 +1120,6 @@
                 onward(j).start()
         return onward
 
-    mixed_on(1)
     onward = exchanged(0)
     scatter.relay(1)
     mixed_relay()

time: 489 us -> 488 us (level)
  no operation moved by 1% of the time
where the time goes in v7:
time: 488 us; the launch traced here: 479 us
  Pallas kernels  461 us (94%)
  local copies, waits for them, and re-layouts  16.4 us (3%)
    pallas_call x1, Pallas kernels, attention_forward(): pl.pallas_call(attention_kernel, out_shape=(sds((line, rows, model), BF),...  182 us
    pallas_call x1, Pallas kernels, mlp(): pl.pallas_call(mlp_kernel, out_shape=(sds((rows, model), F32), sds((lengt...  141 us
    pallas_call x1, Pallas kernels, attention_backward(): pl.pallas_call(attention_back_kernel, out_shape=(sds((rows, model), BF),...  138 us
    unnamed x29, local copies, waits for them, and re-layouts  12.6 us

profile of v7, /device:TPU:0, one launch (start us, length us, event | category | flops | bytes accessed | tf_op | source)
XLA Modules:
  0.0 479.2 jit_solution(10760812085073963745)
XLA Ops:
  0.6 0.0 copy-start
  0.7 0.1 pad.7.clone
  0.8 0.5 copy-done
  1.3 0.7 broadcast_bitcast_fusion.2
  2.0 0.7 broadcast_bitcast_fusion.1
  2.7 0.7 broadcast_bitcast_fusion
  3.3 0.1 maximum_select_fusion
  3.4 0.7 tile.16
  4.1 0.1 tile.17
  4.2 0.7 maximum_maximum_fusion.smalls
  4.9 182.1 %attention_forward.1 = (bf16[4,256,2048]{2,1,0:T(8,128)(2,1)}, bf16[1024,2048]{1,0:T(8,128)(2,1)}, bf16[3,4,1024,128]{3,2,1,0:T(8,128)(2,1)}, f32[128,1024]{1,0:...) custom-call(bf16[256,2048]{1,0:T(8,128)(2,1)} %tok.3, ...), custom_call_target="tpu_custom_call" | custom-call | flops 199999995904 | bytes 100000000 | tf_op jit(solution)/shard_map/attention_forward/pallas_call | solution.py:447
  187.0 140.7 %mlp.1 = (f32[256,2048]{1,0:T(8,128)}, bf16[1024,2048]{1,0:T(8,128)(2,1)}, bf16[4,256,2048]{2,1,0:T(8,128)(2,1)}, bf16[4,256,1408]{2,1,0:T(8,128)(2,1)}, bf16[4,...) custom-call(bf16[1024,2048]{1,0:T(8,128)(2,1)} %get-tuple-element.45, ...), custom_call_target="tpu_custom_call" | custom-call | flops 99999997952 | bytes 100000000 | tf_op jit(solution)/shard_map/mlp/pallas_call | solution.py:1163
  327.7 138.1 %attention_backward.1 = (bf16[256,2048]{1,0:T(8,128)(2,1)}, f32[512,256]{1,0:T(8,128)}, f32[8,256]{1,0:T(8,128)}, f32[8,1536]{1,0:T(8,128)}, bf16[256,2048]{1,0:...) custom-call(f32[256,2048]{1,0:T(8,128)} %get-tuple-element.42.hid, ...), custom_call_target="tpu_custom_call" | custom-call | flops 99999997952 | bytes 100000000 | tf_op jit(solution)/shard_map/attention_backward/pallas_call | solution.py:1708
  465.8 0.0 copy-start.2
  465.8 1.4 fusion.4
  467.3 0.8 slice_reduce_fusion
  468.1 0.7 constant_dynamic-slice_fusion
  468.8 2.3 copy.37
  471.1 0.0 copy-start.6
  471.1 0.0 copy-start.5
  471.1 2.4 copy.38
  473.5 0.0 copy-done.2
  473.5 0.0 copy-start.4
  473.5 1.1 copy.39
  474.7 0.0 copy-done.6
  474.7 0.8 copy.40
  475.5 0.0 copy-done.5
  475.5 0.0 copy-start.3
  475.5 0.0 copy-start.1
  475.5 1.1 copy.41
  476.6 0.0 copy-done.4
  476.6 1.1 copy.42
  477.7 0.0 copy-done.3
  477.7 1.1 copy.43
  478.8 0.0 copy-done.1
  (9 shorter events, 0.1 us)
Async XLA Ops:
  0.6 0.7 copy-start
  465.8 7.7 %copy-start.2 = (f32[3,256,512]{2,1,0:T(8,128)S(1)}, f32[3,256,512]{2,1,0:T(8,128)}, u32[]{:S(2)}) copy-start(f32[3,256,512]{2,1,0:T(8,128)} %get-tuple-element.90) | copy-start | bytes 4718596
  471.1 3.6 copy-start.6
  471.1 4.4 copy-start.5
  473.5 3.1 copy-start.4
  475.5 2.2 copy-start.3
  475.5 3.3 copy-start.1
